TPU v7x, 256 devices: a whole 4x4x8 slice. The times are simulated.
256 devices in a mesh: dp: 8 (over y, core), expert: 32 (over z, x).
Axes of the slice: x: 4, y: 4, z: 8, core: 2. Of those that a mesh axis runs over, the one named last changes fastest.
Arguments:
- tokens: bfloat16 [8192, 8192], P('expert', 'dp'), may hold values from -6 to 6
- cotangent: bfloat16 [8192, 8192], P('expert', 'dp'), may hold values from -1.5 to 1.5
- route: int32 [8192, 2], P('expert'), may hold values from 0 to 31, all different within a row; in each aligned block of 256 rows (0 to 255, 256 to 511, ...) at most 32 rows name the same one
- score: int32 [8192, 2], P('expert'), may hold values from 1 to 16
- clusters: int32 [14336, 1], P('expert'), may hold values from 0 to 31; in each aligned block of 448 rows (0 to 447, 448 to 895, ...) at most 20 rows name the same one
- w_gate: bfloat16 [14336, 8192], P('expert', 'dp'), may hold values from -0.0625 to 0.0625
- w_up: bfloat16 [14336, 8192], P('expert', 'dp'), may hold values from -0.0625 to 0.0625
- w_down: bfloat16 [14336, 8192], P('expert', 'dp'), may hold values from -0.25 to 0.25
Outputs:
- mixed: bfloat16 [8192, 8192], P('expert', 'dp')
- input_grad: bfloat16 [8192, 8192], P('expert', 'dp')
- grad_gate: bfloat16 [32, 640, 8192], P('expert', None, 'dp')
- grad_up: bfloat16 [32, 640, 8192], P('expert', None, 'dp')
- grad_down: bfloat16 [32, 640, 8192], P('expert', None, 'dp')
Inputs may be any that keep to these rules, and one draw needn't show every extreme that they name: `route`: in each aligned block of 256 tokens no expert is named more than 32 times. `clusters`: in each initial shard of 448 consecutive hidden units no expert holds more than 20 of them.
All inputs are finite; a program needn't handle non-finite values.
Results may differ from a plain program's by a relative error of at most 0.029.
Values may be sent and summed in bfloat16 or wider, within the bound.
No kernel may reach another device: no remote copies, remote signals or barrier semaphores. Data moves between devices by JAX's collectives and lax.ppermute only.
A program may use at most 128 MiB of HBM per device.

v0:
```python
import jax
import jax.numpy as jnp
from jax import lax
from jax.sharding import PartitionSpec as P

SLOTS = 640


def block_rank(ids, count):
    onehot = (ids[:, None] == jnp.arange(count, dtype=jnp.int32)[None, :]).astype(jnp.int32)
    before = jnp.cumsum(onehot, axis=0) - onehot
    return jnp.sum(before * onehot, axis=1)


def source_of(target, total):
    match = target[None, :] == jnp.arange(total, dtype=jnp.int32)[:, None]
    numbers = jnp.arange(target.shape[0], dtype=jnp.int32)[None, :]
    source = jnp.sum(jnp.where(match, numbers, 0), axis=1)
    return (source, jnp.any(match, axis=1))


def activate(gate, upper):
    sig = jax.nn.sigmoid(gate)
    return (gate * sig * upper).astype(jnp.bfloat16)


def backprop(back, gate, upper):
    sig = jax.nn.sigmoid(gate)
    d_gate = (back * upper * sig * (1.0 + gate * (1.0 - sig))).astype(jnp.bfloat16)
    d_up = (back * gate * sig).astype(jnp.bfloat16)
    return (d_gate, d_up)


def body(tokens, cotangent, route, score, clusters, w_gate, w_up, w_down):
    experts = lax.axis_size("expert")
    pair_cap = SLOTS // experts
    width = tokens.shape[1]
    neuron_ids = clusters[:, 0]
    target = neuron_ids * pair_cap + block_rank(neuron_ids, experts)
    slot_src, slot_used = source_of(target, SLOTS)
    used = slot_used[:, None]
    zero = jnp.zeros((), jnp.bfloat16)
    packed = jnp.stack(
        [
            jnp.where(used, w_gate[slot_src], zero),
            jnp.where(used, w_up[slot_src], zero),
            jnp.where(used, w_down[slot_src], zero),
        ]
    )
    arrived = lax.all_to_all(
        packed.reshape(3, experts, pair_cap, width),
        "expert",
        split_axis=1,
        concat_axis=1,
        tiled=True,
    )
    weights = arrived.reshape(3, SLOTS, width)
    gate_rows, up_rows, down_rows = (weights[0], weights[1], weights[2])
    tok_count = tokens.shape[0]
    tok_cap = 4 * tok_count // experts
    rows_total = experts * tok_cap
    chosen = route.reshape(-1)
    places = chosen * tok_cap + block_rank(chosen, experts)
    shares = score.astype(jnp.float32)
    shares = (shares / jnp.sum(shares, axis=1, keepdims=True)).reshape(-1)
    row_src, row_used = source_of(places, rows_total)
    token_of = row_src // 2
    live = row_used[:, None]
    sent_tokens = jnp.where(live, tokens[token_of], zero)
    row_share = jnp.where(row_used, shares[row_src], 0.0)
    sent_grads = (row_share[:, None] * cotangent[token_of].astype(jnp.float32)).astype(jnp.bfloat16)
    recv_tokens, recv_grads = (
        lax.all_to_all(
            sent_tokens.reshape(experts, tok_cap, width),
            "expert",
            split_axis=0,
            concat_axis=0,
            tiled=True,
        ),
        lax.all_to_all(
            sent_grads.reshape(experts, tok_cap, width),
            "expert",
            split_axis=0,
            concat_axis=0,
            tiled=True,
        ),
    )
    rows_x = recv_tokens.reshape(rows_total, width)
    rows_dy = recv_grads.reshape(rows_total, width)
    contract = (((1,), (1,)), ((), ()))
    gate_part = lax.dot_general(rows_x, gate_rows, contract, preferred_element_type=jnp.float32)
    up_part = lax.dot_general(rows_x, up_rows, contract, preferred_element_type=jnp.float32)
    back_part = lax.dot_general(rows_dy, down_rows, contract, preferred_element_type=jnp.float32)
    gate_sum, up_sum = (
        lax.psum(gate_part.astype(jnp.bfloat16), "dp").astype(jnp.float32),
        lax.psum(up_part.astype(jnp.bfloat16), "dp").astype(jnp.float32),
    )
    hidden = activate(gate_sum, up_sum)
    back_sum = lax.psum(back_part.astype(jnp.bfloat16), "dp").astype(jnp.float32)
    d_gate, d_up = backprop(back_sum, gate_sum, up_sum)
    out_part = jnp.dot(hidden, down_rows, preferred_element_type=jnp.float32).astype(jnp.bfloat16)
    input_part = (
        jnp.dot(d_gate, gate_rows, preferred_element_type=jnp.float32)
        + jnp.dot(d_up, up_rows, preferred_element_type=jnp.float32)
    ).astype(jnp.bfloat16)
    over_rows = (((0,), (0,)), ((), ()))
    grad_down = lax.dot_general(
        hidden, rows_dy, over_rows, preferred_element_type=jnp.float32
    ).astype(jnp.bfloat16)
    grad_gate = lax.dot_general(
        d_gate, rows_x, over_rows, preferred_element_type=jnp.float32
    ).astype(jnp.bfloat16)
    grad_up = lax.dot_general(d_up, rows_x, over_rows, preferred_element_type=jnp.float32).astype(
        jnp.bfloat16
    )
    back_out, back_in = (
        lax.all_to_all(
            out_part.reshape(experts, tok_cap, width),
            "expert",
            split_axis=0,
            concat_axis=0,
            tiled=True,
        ),
        lax.all_to_all(
            input_part.reshape(experts, tok_cap, width),
            "expert",
            split_axis=0,
            concat_axis=0,
            tiled=True,
        ),
    )
    picked_out = back_out.reshape(rows_total, width)[places].astype(jnp.float32)
    picked_in = back_in.reshape(rows_total, width)[places].astype(jnp.float32)
    mixed = jnp.sum((shares[:, None] * picked_out).reshape(tok_count, 2, width), axis=1).astype(
        jnp.bfloat16
    )
    input_grad = jnp.sum(picked_in.reshape(tok_count, 2, width), axis=1).astype(jnp.bfloat16)
    return (mixed, input_grad, grad_gate[None], grad_up[None], grad_down[None])


def solution(mesh):
    placed = (
        P("expert", "dp"),
        P("expert", "dp"),
        P("expert", None),
        P("expert", None),
        P("expert", None),
        P("expert", "dp"),
        P("expert", "dp"),
        P("expert", "dp"),
    )
    return jax.shard_map(
        body,
        mesh=mesh,
        in_specs=placed,
        out_specs=(
            P("expert", "dp"),
            P("expert", "dp"),
            P("expert", None, "dp"),
            P("expert", None, "dp"),
            P("expert", None, "dp"),
        ),
        check_vma=False,
    )
```

profile of v0, /device:TPU:24, one launch (start us, length us, event | category | flops | bytes accessed | tf_op | source)
XLA Modules:
  0.0 459.2 jit_solution(13727654490660205995)
XLA Ops:
  10.7 4.1 gather_fusion
  16.4 11.6 %all-to-all-start = ((bf16[32,32,1024]{2,1,0:T(8,128)(2,1)}), bf16[32,32,1024]{2,1,0:T(8,128)(2,1)}, u32[]{:S(2)}, u32[]{:S(2)}) async-start(bf16[32,32,1024]{2,1,0:T(8,128)(2,1)} %broadcast_select_fusion), calls=%async_computation | async-start | bytes 4194304 | tf_op jit(solution)/shard_map/all_to_all | solution.py:73
  30.2 3.5 gather_fusion.3
  35.9 3.5 gather_fusion.2
  39.4 3.3 gather.41
  42.7 3.5 gather_fusion.1
  55.0 23.1 %all-to-all-done = bf16[32,32,1024]{2,1,0:T(8,128)(2,1)} async-done(((bf16[32,32,1024]{2,1,0:T(8,128)(2,1)}), bf16[32,32,1024]{2,1,0:T(8,128)(2,1)}, u32[]{:S(2)}, u32[]{:S(2)}) %all-to-all-start) | async-done | bytes 2097184 | tf_op jit(solution)/shard_map/all_to_all | solution.py:73
  78.1 6.1 %all-to-all-start.1 = ((bf16[3,32,20,1024]{3,2,0,1:T(8,128)(2,1)}), bf16[3,32,20,1024]{3,2,0,1:T(8,128)(2,1)}, u32[]{:S(2)}, u32[]{:S(2)}) async-start(bf16[3,32,20,1024]{3,2,0,1:T(8,128)(2,1)} %copy.37), calls=%async_computation.1 | async-start | bytes 9437184 | tf_op jit(solution)/shard_map/all_to_all | solution.py:50
  84.5 6.9 %gather_fusion.5 = f32[1024]{0:T(1024)S(1)} fusion(f32[512]{0:T(512)S(1)} %reshape.298, s32[1024]{0:T(1024)S(1)} %broadcast_clamp_fusion), kind=kCustom, calls=%fused_computation.5 | custom fusion | bytes 12288 | tf_op jit(solution)/shard_map/gather | solution.py:70
  91.4 4.1 gather_fusion.6
  97.4 91.2 %all-to-all-done.1 = bf16[3,32,20,1024]{3,2,0,1:T(8,128)(2,1)} async-done(((bf16[3,32,20,1024]{3,2,0,1:T(8,128)(2,1)}), bf16[3,32,20,1024]{3,2,0,1:T(8,128)(2,1)}, u32[]{:S(2)}, u32[]{:S(2)}) %all-to-all-start.1) | async-done | bytes 3932192 | tf_op jit(solution)/shard_map/all_to_all | solution.py:50
  188.6 6.9 %all-to-all-start.3 = ((bf16[32,32,1024]{2,1,0:T(8,128)(2,1)}), bf16[32,32,1024]{2,1,0:T(8,128)(2,1)}, u32[]{:S(2)}, u32[]{:S(2)}) async-start(bf16[32,32,1024]{2,1,0:T(8,128)(2,1)} %fusion), calls=%async_computation.3 | async-start | bytes 4194304 | tf_op jit(solution)/shard_map/all_to_all | solution.py:80
  195.8 4.7 %fusion.27 = (bf16[1,32,20,1024]{3,2,0,1:T(8,128)(2,1)}, bf16[1,32,20,1024]{3,2,0,1:T(8,128)(2,1)}, bf16[1,32,20,1024]{3,2,0,1:T(8,128)(2,1)S(1)}) fusion(bf16[3,32,20,1024]{3,2,0,1:T(8,128)(2,1)} %all-to-all-done.1), kind=kLoop, calls=%fused_computation.87 | loop fusion | bytes 7864320 | tf_op jit(solution)/shard_map/slice | solution.py:58
  200.4 3.3 squeeze.13
  208.2 4.9 %convolution_convert_fusion.5 = bf16[1024,640]{1,0:T(8,128)(2,1)} fusion(bf16[1024,1024]{1,0:T(8,128)(2,1)} %bitcast.4, bf16[640,1024]{1,0:T(8,128)(2,1)} %squeeze.14), kind=kOutput, calls=%fused_computation.38 | convolution fusion | flops 1342832640 | bytes 4718592 | tf_op jit(solution)/shard_map/dot_general | solution.py:92
  213.1 4.6 convolution_convert_fusion.6
  217.7 27.4 %all-to-all-done.3 = bf16[32,32,1024]{2,1,0:T(8,128)(2,1)} async-done(((bf16[32,32,1024]{2,1,0:T(8,128)(2,1)}), bf16[32,32,1024]{2,1,0:T(8,128)(2,1)}, u32[]{:S(2)}, u32[]{:S(2)}) %all-to-all-start.3) | async-done | bytes 2097184 | tf_op jit(solution)/shard_map/all_to_all | solution.py:80
  245.1 4.5 convolution_convert_fusion.4
  249.6 71.2 %all-reduce.4.cloned.1.call-done = (bf16[1024,640]{1,0:T(8,128)(2,1)}, bf16[1024,640]{1,0:T(8,128)(2,1)}, bf16[1024,640]{1,0:T(8,128)(2,1)}) async-done(((bf16[1024,640]{1,0:T(8,128)(2,1)}, bf16[1024,640]{1,0:T(8,128)(2,1)}, bf16[1024,640]{1,0:T(8,128)(2,1)}), (bf16[1024,640]{1,0:T(8,128)(2,1)}, bf16[1024,640]{1,0:T(8,128)(2,1)}, bf16[1024,640]{1,0:T(8,128)(2,1)})) %all-reduce.4.cloned.1.call-update) | async-done | bytes 3932176 | tf_op jit(solution)/shard_map/psum | solution.py:96
  320.8 5.0 %convolution_convert_fusion = bf16[1024,1024]{1,0:T(8,128)(2,1)} fusion(bf16[640,1024]{1,0:T(8,128)(2,1)S(1)} %copy-done.15, bf16[1024,640]{1,0:T(8,128)(2,1)} %get-tuple-element.5, bf16[1024,640]{1,0:T(8,128)(2,1)} %get-tuple-element.6), kind=kOutput, calls=%fused_computation.33 | convolution fusion | flops 1348468736 | bytes 6029312 | tf_op jit(solution)/shard_map/dot_general | solution.py:101
  325.8 9.8 %all-to-all-start.2 = ((bf16[32,32,1024]{2,1,0:T(8,128)(2,1)}), bf16[32,32,1024]{2,1,0:T(8,128)(2,1)S(1)}, u32[]{:S(2)}, u32[]{:S(2)}) async-start(bf16[32,32,1024]{2,1,0:T(8,128)(2,1)} %bitcast.76), calls=%async_computation.2 | async-start | bytes 4194304 | tf_op jit(solution)/shard_map/all_to_all | solution.py:117
  335.6 3.4 fusion.4
  342.2 3.3 add_convert_fusion
  345.5 40.7 %all-to-all-done.2 = bf16[32,32,1024]{2,1,0:T(8,128)(2,1)S(1)} async-done(((bf16[32,32,1024]{2,1,0:T(8,128)(2,1)}), bf16[32,32,1024]{2,1,0:T(8,128)(2,1)S(1)}, u32[]{:S(2)}, u32[]{:S(2)}) %all-to-all-start.2) | async-done | bytes 2097184 | tf_op jit(solution)/shard_map/all_to_all | solution.py:117
  386.2 6.8 %all-to-all-start.4 = ((bf16[32,32,1024]{2,1,0:T(8,128)(2,1)}), bf16[32,32,1024]{2,1,0:T(8,128)(2,1)}, u32[]{:S(2)}, u32[]{:S(2)}) async-start(bf16[32,32,1024]{2,1,0:T(8,128)(2,1)} %bitcast.75), calls=%async_computation.4 | async-start | bytes 4194304 | tf_op jit(solution)/shard_map/all_to_all | solution.py:124
  393.3 4.7 %fusion.12 = bf16[1,640,1024]{2,1,0:T(8,128)(2,1)} fusion(bf16[1024,640]{1,0:T(8,128)(2,1)} %copy-done.11, bf16[1024,1024]{1,0:T(8,128)(2,1)} %bitcast.4), kind=kOutput, calls=%fused_computation.43 | convolution fusion | flops 1342832640 | bytes 4718592 | tf_op jit(solution)/shard_map/dot_general | solution.py:110
  398.1 4.5 fusion.14
  402.6 4.4 fusion.13
  412.1 3.5 multiply_reduce_fusion
  415.6 27.8 %all-to-all-done.4 = bf16[32,32,1024]{2,1,0:T(8,128)(2,1)} async-done(((bf16[32,32,1024]{2,1,0:T(8,128)(2,1)}), bf16[32,32,1024]{2,1,0:T(8,128)(2,1)}, u32[]{:S(2)}, u32[]{:S(2)}) %all-to-all-start.4) | async-done | bytes 2097184 | tf_op jit(solution)/shard_map/all_to_all | solution.py:124
  443.4 4.7 %gather_fusion.7 = bf16[512,1024]{1,0:T(8,128)(2,1)S(1)} fusion(bf16[1024,1024]{1,0:T(8,128)(2,1)} %bitcast.15, s32[1024]{0:T(1024)S(1)} %pad_clamp_fusion), kind=kCustom, calls=%fused_computation.7 | custom fusion | bytes 2099200 | tf_op jit(solution)/shard_map/gather | solution.py:133
  448.8 3.6 reduce_sum.81
  (94 shorter events, 34.5 us)
Async XLA Ops:
  7.2 23.0 %copy-start = (bf16[448,1024]{1,0:T(8,128)(2,1)S(1)}, bf16[448,1024]{1,0:T(8,128)(2,1)}, u32[]{:S(2)}) copy-start(bf16[448,1024]{1,0:T(8,128)(2,1)} %param.15) | copy-start | bytes 2752516
  7.2 3.5 copy-start.2
  16.4 11.6 %copy-start.16 = (s32[448,1]{0,1:T(1,128)S(1)}, s32[448,1]{0,1:T(1,128)}, u32[]{:S(2)}) copy-start(s32[448,1]{0,1:T(1,128)} %param.12) | copy-start | bytes 5380
  16.4 61.7 %all-to-all-start = ((bf16[32,32,1024]{2,1,0:T(8,128)(2,1)}), bf16[32,32,1024]{2,1,0:T(8,128)(2,1)}, u32[]{:S(2)}, u32[]{:S(2)}) async-start(bf16[32,32,1024]{2,1,0:T(8,128)(2,1)} %broadcast_select_fusion), calls=%async_computation | async-start | bytes 4194304 | tf_op jit(solution)/shard_map/all_to_all | solution.py:73
  33.6 2.3 copy-start.4
  39.4 3.3 copy-start.5
  55.0 29.2 %copy-start.18 = (s32[256,2]{0,1:T(2,128)S(1)}, s32[256,2]{0,1:T(2,128)}, u32[]{:S(2)}) copy-start(s32[256,2]{0,1:T(2,128)} %param.11) | copy-start | bytes 6148
  78.1 110.5 %all-to-all-start.1 = ((bf16[3,32,20,1024]{3,2,0,1:T(8,128)(2,1)}), bf16[3,32,20,1024]{3,2,0,1:T(8,128)(2,1)}, u32[]{:S(2)}, u32[]{:S(2)}) async-start(bf16[3,32,20,1024]{3,2,0,1:T(8,128)(2,1)} %copy.37), calls=%async_computation.1 | async-start | bytes 9437184 | tf_op jit(solution)/shard_map/all_to_all | solution.py:50
  84.5 7.0 %copy-start.3 = (bf16[256,1024]{1,0:T(8,128)(2,1)S(1)}, bf16[256,1024]{1,0:T(8,128)(2,1)}, u32[]{:S(2)}) copy-start(bf16[256,1024]{1,0:T(8,128)(2,1)} %param.9) | copy-start | bytes 1572868
  188.6 56.5 %all-to-all-start.3 = ((bf16[32,32,1024]{2,1,0:T(8,128)(2,1)}), bf16[32,32,1024]{2,1,0:T(8,128)(2,1)}, u32[]{:S(2)}, u32[]{:S(2)}) async-start(bf16[32,32,1024]{2,1,0:T(8,128)(2,1)} %fusion), calls=%async_computation.3 | async-start | bytes 4194304 | tf_op jit(solution)/shard_map/all_to_all | solution.py:80
  195.5 125.2 %all-reduce.4.cloned.1.call-start = ((), (), s32[]{:S(2)}) async-start(), calls=%async_computation.5 | async-start | bytes 7864320 | tf_op jit(solution)/shard_map/psum | solution.py:96
  208.2 4.9 %copy-start.12 = (bf16[640,1024]{1,0:T(8,128)(2,1)S(1)}, bf16[640,1024]{1,0:T(8,128)(2,1)}, u32[]{:S(2)}) copy-start(bf16[640,1024]{1,0:T(8,128)(2,1)} %squeeze.13) | copy-start | bytes 3932164
  213.1 31.9 %copy-start.15 = (bf16[640,1024]{1,0:T(8,128)(2,1)S(1)}, bf16[640,1024]{1,0:T(8,128)(2,1)}, u32[]{:S(2)}) copy-start(bf16[640,1024]{1,0:T(8,128)(2,1)} %squeeze.15) | copy-start | bytes 3932164
  325.8 60.4 %all-to-all-start.2 = ((bf16[32,32,1024]{2,1,0:T(8,128)(2,1)}), bf16[32,32,1024]{2,1,0:T(8,128)(2,1)S(1)}, u32[]{:S(2)}, u32[]{:S(2)}) async-start(bf16[32,32,1024]{2,1,0:T(8,128)(2,1)} %bitcast.76), calls=%async_computation.2 | async-start | bytes 4194304 | tf_op jit(solution)/shard_map/all_to_all | solution.py:117
  335.6 4.5 copy-start.13
  339.0 1.1 copy-start.11
  340.1 1.8 copy-start.6
  340.1 1.8 copy-start.8
  340.1 2.1 copy-start.14
  386.2 6.8 %copy-start.17 = (s32[256,2]{0,1:T(2,128)S(1)}, s32[256,2]{0,1:T(2,128)}, u32[]{:S(2)}) copy-start(s32[256,2]{0,1:T(2,128)} %param.10) | copy-start | bytes 6148
  386.2 57.3 %all-to-all-start.4 = ((bf16[32,32,1024]{2,1,0:T(8,128)(2,1)}), bf16[32,32,1024]{2,1,0:T(8,128)(2,1)}, u32[]{:S(2)}, u32[]{:S(2)}) async-start(bf16[32,32,1024]{2,1,0:T(8,128)(2,1)} %bitcast.75), calls=%async_computation.4 | async-start | bytes 4194304 | tf_op jit(solution)/shard_map/all_to_all | solution.py:124
  393.3 4.8 %copy-start.7 = (bf16[1024,640]{1,0:T(8,128)(2,1)S(1)}, bf16[1024,640]{1,0:T(8,128)(2,1)}, u32[]{:S(2)}) copy-start(bf16[1024,640]{1,0:T(8,128)(2,1)} %get-tuple-element.6) | copy-start | bytes 3932164
  393.3 4.8 %copy-start.10 = (bf16[1024,640]{1,0:T(8,128)(2,1)S(1)}, bf16[1024,640]{1,0:T(8,128)(2,1)}, u32[]{:S(2)}) copy-start(bf16[1024,640]{1,0:T(8,128)(2,1)} %get-tuple-element.5) | copy-start | bytes 3932164
  398.1 4.5 copy-start.9
  443.4 9.0 %copy-start.1 = (bf16[448,1024]{1,0:T(8,128)(2,1)S(1)}, bf16[448,1024]{1,0:T(8,128)(2,1)}, u32[]{:S(2)}) copy-start(bf16[448,1024]{1,0:T(8,128)(2,1)} %param.15) | copy-start | bytes 2752516
Sparse Core Ops, SparseCore 0:
  249.7 71.0 all-reduce.3
where the time goes:
time: 460 us; the launch traced here: 459 us
  waiting for transfers between devices  281 us (61%)
  local copies, waits for them, and re-layouts  63.7 us (14%)
  starting transfers between devices  41.4 us (9%)
  matrix products  37.7 us (8%)
  other arithmetic  20.6 us (4%)
  between operations  14.5 us (3%)
    all_to_all x1, waiting for transfers between devices, body(): lax.all_to_all(packed.reshape(3, experts, pair_cap, width), 'expert', spl...  91.2 us
    psum x1, waiting for transfers between devices, body(): lax.psum(up_part.astype(jnp.bfloat16), 'dp').astype(jnp.float32)  71.2 us
    all_to_all x1, waiting for transfers between devices, body(): lax.all_to_all(out_part.reshape(experts, tok_cap, width), 'expert', split...  40.7 us
    all_to_all x1, waiting for transfers between devices, body(): lax.all_to_all(input_part.reshape(experts, tok_cap, width), 'expert', spl...  27.8 us
    all_to_all x1, waiting for transfers between devices, body(): lax.all_to_all(sent_grads.reshape(experts, tok_cap, width), 'expert', spl...  27.4 us
    all_to_all x1, waiting for transfers between devices, body(): lax.all_to_all(sent_tokens.reshape(experts, tok_cap, width), 'expert', sp...  23.1 us
    all_to_all x1, starting transfers between devices, body(): lax.all_to_all(sent_tokens.reshape(experts, tok_cap, width), 'expert', sp...  11.6 us
    all_to_all x1, starting transfers between devices, body(): lax.all_to_all(out_part.reshape(experts, tok_cap, width), 'expert', split...  9.84 us
  transfers between devices with their start and end apart: 6, of which 6 were waited for; matrix products, arithmetic and copies ran while one was open for 20% of the time, Pallas kernels for 0%

commit v1 on v0

v1 whole, which is shorter than its diff:
```python
import functools

import jax
import jax.numpy as jnp
from jax import lax
from jax.experimental import pallas as pl
from jax.experimental.pallas import tpu as pltpu
from jax.sharding import Mesh
from jax.sharding import PartitionSpec as P

SLOTS = 640
EXPERT = ("z", "x")
DP = ("y", "core")
BF16 = jnp.bfloat16
F32 = jnp.float32
LIMIT = 48 * 1024 * 1024


def iota(shape, axis):
    return lax.broadcasted_iota(jnp.int32, shape, axis)


def kernel_call(body, name, **kwargs):
    return pl.pallas_call(
        body,
        name=name,
        compiler_params=pltpu.CompilerParams(vmem_limit_bytes=LIMIT),
        **kwargs,
    )


def ranks(rows, count):
    n = rows[0].shape[1]
    hits = [iota((count, n), 0) == ids for ids in rows]
    seen = sum(hit.astype(F32) for hit in hits).astype(BF16)
    earlier = (iota((n, n), 0) < iota((n, n), 1)).astype(F32).astype(BF16)
    before = jnp.dot(seen, earlier, preferred_element_type=F32)
    return [
        jnp.sum(jnp.where(hit, before, 0.0), axis=0, keepdims=True).astype(jnp.int32)
        for hit in hits
    ]


def token_places(route_ref, experts, cap):
    rows = [route_ref[0:1, :], route_ref[1:2, :]]
    return [ids * cap + rank for ids, rank in zip(rows, ranks(rows, experts))]


def token_shares(score_ref):
    score = score_ref[...].astype(F32)
    first, second = score[0:1, :], score[1:2, :]
    total = first + second
    return first / total, second / total


def dispatch_body(scaled, experts, cap, route_ref, score_ref, x_ref, out_ref):
    block, count = out_ref.shape[0], x_ref.shape[0]
    places = token_places(route_ref, experts, cap)
    slot = iota((block, count), 0) + pl.program_id(0) * block
    hits = [slot == place for place in places]
    pick = jnp.where(hits[0] | hits[1], 1.0, 0.0).astype(BF16)
    rows = jnp.dot(pick, x_ref[...], preferred_element_type=F32)
    if scaled:
        shares = token_shares(score_ref)
        weight = jnp.where(hits[0], shares[0], 0.0) + jnp.where(hits[1], shares[1], 0.0)
        rows = rows * jnp.sum(weight, axis=1, keepdims=True)
    out_ref[...] = rows.astype(BF16)


def dispatch(route, score, x, experts, cap, scaled):
    count, width = x.shape
    block = 256
    total = experts * cap
    whole = lambda i: (0, 0)
    return kernel_call(
        functools.partial(dispatch_body, scaled, experts, cap),
        "dispatch",
        grid=(total // block,),
        in_specs=[
            pl.BlockSpec((2, count), whole),
            pl.BlockSpec((2, count), whole),
            pl.BlockSpec((count, width), whole),
        ],
        out_specs=pl.BlockSpec((block, width), lambda i: (i, 0)),
        out_shape=jax.ShapeDtypeStruct((total, width), BF16),
    )(route, score, x)


def pack_body(experts, cap, ids_ref, a_ref, b_ref, out_ref):
    block, count = out_ref.shape[0], a_ref.shape[0]
    ids = ids_ref[...]
    place = ids * (2 * cap) + ranks([ids], experts)[0]
    slot = iota((block, count), 0) + pl.program_id(0) * block
    pick_a = jnp.where(slot == place, 1.0, 0.0).astype(BF16)
    pick_b = jnp.where(slot == place + cap, 1.0, 0.0).astype(BF16)
    out_ref[...] = (
        jnp.dot(pick_a, a_ref[...], preferred_element_type=F32)
        + jnp.dot(pick_b, b_ref[...], preferred_element_type=F32)
    ).astype(BF16)


def pack(ids, a, b, experts, cap, width, columns):
    count = a.shape[0]
    block = 256
    total = 2 * experts * cap
    whole = lambda i: (0, 0)
    return kernel_call(
        functools.partial(pack_body, experts, cap),
        "pack",
        grid=(total // block,),
        in_specs=[
            pl.BlockSpec((1, count), whole),
            pl.BlockSpec((count, width), lambda i: (0, columns[0])),
            pl.BlockSpec((count, width), lambda i: (0, columns[1])),
        ],
        out_specs=pl.BlockSpec((block, width), lambda i: (i, 0)),
        out_shape=jax.ShapeDtypeStruct((total, width), BF16),
    )(ids, a, b)


def unpack_picks(block, cap):
    row, column = iota((block, 2 * block), 0), iota((block, 2 * block), 1)
    group = sum((row >= g * cap).astype(jnp.int32) for g in range(1, block // cap))
    first = row + cap * group
    return [jnp.where(column == first + k * cap, 1.0, 0.0).astype(BF16) for k in (0, 1)]


def unpack_two_body(cap, raw_ref, out_ref):
    picks = unpack_picks(out_ref.shape[1], cap)
    raw = raw_ref[...]
    for k in (0, 1):
        out_ref[k] = jnp.dot(picks[k], raw, preferred_element_type=F32).astype(BF16)


def unpack_one_body(cap, raw_ref, out_ref):
    width = raw_ref.shape[1]
    picks = unpack_picks(out_ref.shape[0], cap)
    raw = raw_ref[...]
    for k in (0, 1):
        out_ref[:, k * width : (k + 1) * width] = jnp.dot(
            picks[k], raw, preferred_element_type=F32
        ).astype(BF16)


def unpack_two(raw, cap):
    rows, width = raw.shape[0] // 2, raw.shape[1]
    block = 160
    return kernel_call(
        functools.partial(unpack_two_body, cap),
        "unpack_two",
        grid=(rows // block,),
        in_specs=[pl.BlockSpec((2 * block, width), lambda i: (i, 0))],
        out_specs=pl.BlockSpec((2, block, width), lambda i: (0, i, 0)),
        out_shape=jax.ShapeDtypeStruct((2, rows, width), BF16),
    )(raw).reshape(2 * rows, width)


def unpack_one(raw, cap):
    rows, width = raw.shape[0] // 2, raw.shape[1]
    block = 160
    return kernel_call(
        functools.partial(unpack_one_body, cap),
        "unpack_one",
        grid=(rows // block,),
        in_specs=[pl.BlockSpec((2 * block, width), lambda i: (i, 0))],
        out_specs=pl.BlockSpec((block, 2 * width), lambda i: (i, 0)),
        out_shape=jax.ShapeDtypeStruct((rows, 2 * width), BF16),
    )(raw)


def column_of(row):
    n = row.shape[1]
    same = iota((n, n), 0) == iota((n, n), 1)
    return jnp.sum(jnp.where(same, row, jnp.zeros_like(row)), axis=1, keepdims=True)


def combine_body(scaled, experts, cap, route_ref, score_ref, rows_ref, out_ref):
    count, total = out_ref.shape[0], rows_ref.shape[0]
    places = [column_of(place) for place in token_places(route_ref, experts, cap)]
    slot = iota((count, total), 1)
    hits = [slot == place for place in places]
    rows = rows_ref[...]
    if scaled:
        shares = [column_of(share) for share in token_shares(score_ref)]
        weight = jnp.where(hits[0], shares[0], 0.0) + jnp.where(hits[1], shares[1], 0.0)
        high = weight.astype(BF16)
        low = (weight - high.astype(F32)).astype(BF16)
        total_rows = jnp.dot(high, rows, preferred_element_type=F32) + jnp.dot(
            low, rows, preferred_element_type=F32
        )
    else:
        pick = jnp.where(hits[0] | hits[1], 1.0, 0.0).astype(BF16)
        total_rows = jnp.dot(pick, rows, preferred_element_type=F32)
    out_ref[...] = total_rows.astype(BF16)


def combine(route, score, rows, experts, cap, scaled):
    count = route.shape[1]
    total, width = rows.shape
    block = 512
    whole = lambda i: (0, 0)
    return kernel_call(
        functools.partial(combine_body, scaled, experts, cap),
        "combine",
        grid=(width // block,),
        in_specs=[
            pl.BlockSpec((2, count), whole),
            pl.BlockSpec((2, count), whole),
            pl.BlockSpec((total, block), lambda i: (0, i)),
        ],
        out_specs=pl.BlockSpec((count, block), lambda i: (0, i)),
        out_shape=jax.ShapeDtypeStruct((count, width), BF16),
    )(route, score, rows)


def exchange(rows, parts):
    total, width = rows.shape
    return lax.all_to_all(
        rows.reshape(parts, total // parts, width),
        EXPERT,
        split_axis=0,
        concat_axis=0,
        tiled=True,
    ).reshape(total, width)


def after(value, other):
    return lax.optimization_barrier((value, other))[0]


def shift(value, axis, step):
    size = lax.axis_size(axis)
    return lax.ppermute(value, axis, [(i, (i + step) % size) for i in range(size)])


def pick(value, index, axis):
    return lax.dynamic_index_in_dim(value, index, axis, keepdims=False)


def put(value, part, y, core):
    return lax.dynamic_update_slice(value, part[None, None], (y, core, 0, 0))


def scatter_sum(value):
    rows, n = value.shape
    ys, cores = lax.axis_size("y"), lax.axis_size("core")
    y, core = lax.axis_index("y"), lax.axis_index("core")
    value = value.reshape(ys, cores, rows // (ys * cores), n)
    other = shift(pick(value, 1 - core, 1), "core", 1)
    pair = (pick(value, core, 1).astype(F32) + other.astype(F32)).astype(BF16)
    half = n // 2
    far = pick(pair, (y + 2) % ys, 0)
    low = shift(far[:, :half], "y", 1).astype(F32)
    high = shift(far[:, half:], "y", -1).astype(F32)
    above = pick(pair, (y + 1) % ys, 0).astype(F32)
    below = pick(pair, (y + ys - 1) % ys, 0).astype(F32)
    to_above = jnp.concatenate([above[:, :half] + low, above[:, half:]], axis=1)
    to_below = jnp.concatenate([below[:, :half], below[:, half:] + high], axis=1)
    from_below = shift(to_above.astype(BF16), "y", 1).astype(F32)
    from_above = shift(to_below.astype(BF16), "y", -1).astype(F32)
    return pick(pair, y, 0).astype(F32) + from_below + from_above


def gather_blocks(part):
    rows, n = part.shape
    ys, cores = lax.axis_size("y"), lax.axis_size("core")
    y, core = lax.axis_index("y"), lax.axis_index("core")
    half = n // 2
    from_below = shift(part, "y", 1)
    from_above = shift(part, "y", -1)
    low = shift(from_below[:, :half], "y", 1)
    high = shift(from_above[:, half:], "y", -1)
    far = jnp.concatenate([low, high], axis=1)
    column = jnp.zeros((ys, rows, n), part.dtype)
    for k, piece in enumerate((part, from_below, far, from_above)):
        column = lax.dynamic_update_slice(column, piece[None], ((y + ys - k) % ys, 0, 0))
    other = shift(column, "core", 1)
    both = jnp.where(
        core == 0, jnp.stack([column, other], axis=1), jnp.stack([other, column], axis=1)
    )
    return both.reshape(ys * cores * rows, n)


def activate(gate, upper):
    sig = jax.nn.sigmoid(gate)
    return (gate * sig * upper).astype(BF16)


def backprop(back, gate, upper):
    sig = jax.nn.sigmoid(gate)
    d_gate = (back * upper * sig * (1.0 + gate * (1.0 - sig))).astype(BF16)
    d_up = (back * gate * sig).astype(BF16)
    return jnp.concatenate([d_gate, d_up], axis=1)


def body(tokens, cotangent, route, score, clusters, w_gate, w_up, w_down):
    experts = lax.axis_size(EXPERT)
    pair_cap = SLOTS // experts
    tok_count, width = tokens.shape
    tok_cap = 4 * tok_count // experts
    route, score, ids = route.T, score.T, clusters.T
    contract = (((1,), (1,)), ((), ()))
    over_rows = (((0,), (0,)), ((), ()))

    sent_tokens = dispatch(route, score, tokens, experts, tok_cap, False)
    rows_x = exchange(sent_tokens, experts)
    packed = pack(ids, w_gate, w_up, experts, pair_cap, width, (0, 0))
    raw = exchange(after(packed, rows_x), experts)
    packed_down = pack(ids, w_down, w_down, experts, pair_cap, width // 2, (0, 1))
    raw_down = exchange(after(packed_down, raw), experts)

    gate_up_rows = unpack_two(raw, pair_cap)
    part = lax.dot_general(rows_x, gate_up_rows, contract, preferred_element_type=F32)
    part = part.astype(BF16)
    sent_grads = dispatch(route, score, cotangent, experts, tok_cap, True)
    rows_dy = exchange(after(sent_grads, (raw_down, part)), experts)
    gate_up = scatter_sum(part)
    gate, upper = gate_up[:, :SLOTS], gate_up[:, SLOTS:]
    hidden = gather_blocks(activate(gate, upper))
    down_rows = unpack_one(raw_down, pair_cap)
    out_part = jnp.dot(hidden, down_rows, preferred_element_type=F32).astype(BF16)
    out_part, rows_dy = lax.optimization_barrier((out_part, rows_dy))
    back_out = exchange(out_part, experts)

    back_part = lax.dot_general(rows_dy, down_rows, contract, preferred_element_type=F32)
    back = scatter_sum(back_part.astype(BF16))
    d_both = gather_blocks(backprop(back, gate, upper))
    input_part = jnp.dot(d_both, gate_up_rows, preferred_element_type=F32).astype(BF16)
    back_in = exchange(after(input_part, back_out), experts)

    d_both, hidden, rows_dy = after((d_both, hidden, rows_dy), input_part)
    grad_down = lax.dot_general(hidden, rows_dy, over_rows, preferred_element_type=F32)
    grad_gate = lax.dot_general(
        d_both[:, :SLOTS], rows_x, over_rows, preferred_element_type=F32
    )
    grad_up = lax.dot_general(d_both[:, SLOTS:], rows_x, over_rows, preferred_element_type=F32)
    mixed = combine(route, score, back_out, experts, tok_cap, True)
    input_grad = combine(route, score, back_in, experts, tok_cap, False)
    return (
        mixed,
        input_grad,
        grad_gate.astype(BF16)[None],
        grad_up.astype(BF16)[None],
        grad_down.astype(BF16)[None],
    )


def solution(mesh):
    fine = Mesh(mesh.devices.reshape(4, 2, 8, 4), DP + EXPERT)
    full, rows_only = P(EXPERT, DP), P(EXPERT, None)
    grads = P(EXPERT, None, DP)
    return jax.shard_map(
        body,
        mesh=fine,
        in_specs=(full, full, rows_only, rows_only, rows_only, full, full, full),
        out_specs=(full, full, grads, grads, grads),
        check_vma=False,
    )
```

time: 460 us -> 361 us (0.78)
  waiting for transfers between devices: 281 us -> 216 us
  local copies, waits for them, and re-layouts: 63.7 us -> 12.2 us
  Pallas kernels: 0 us -> 24.5 us
  starting transfers between devices: 41.4 us -> 62.9 us
  between operations: 14.5 us -> 1.17 us
  other arithmetic: 20.6 us -> 11.2 us
  matrix products: 37.7 us -> 31.2 us
    psum x1 -> x0, waiting for transfers between devices: 71.2 us -> none  [body(): lax.psum(up_part.astype(jnp.bfloat16), 'dp').astype(jnp.float32)]
    gather x13 -> x0, local copies, waits for them, and re-layouts: 42.4 us -> none  [the longest x2 6.94 us: body(): row_share = jnp.where(row_used, shares[row_src], 0.0)]
    ppermute x0 -> x20, waiting for transfers between devices: none -> 41.8 us  [shift(): lax.ppermute(value, axis, [(i, (i + step) % size) for i in range(size)])]
    all_to_all x5 -> x6, waiting for transfers between devices: 210 us -> 174 us  [exchange(): lax.all_to_all(rows.reshape(parts, total // parts, width), EXPERT, split_...]
    pallas_call x0 -> x8, Pallas kernels: none -> 24.5 us  [the longest x2 8.51 us: pack(): kernel_call(functools.partial(pack_body, experts, cap), 'pack', grid=(tot...]
    ppermute x0 -> x20, starting transfers between devices: none -> 21.3 us  [shift(): lax.ppermute(value, axis, [(i, (i + step) % size) for i in range(size)])]
    reduce_sum x7 -> x0, other arithmetic: 7.71 us -> none  [the longest x1 3.59 us: body(): jnp.sum(picked_in.reshape(tok_count, 2, width), axis=1).astype(jnp.bfloat16)]
    squeeze x3 -> x2, local copies, waits for them, and re-layouts: 7.73 us -> 0.15 us  [pick(): return lax.dynamic_index_in_dim(value, index, axis, keepdims=False)]
  transfers between devices with their start and end apart: 6 -> 26, of which waited for: 6 -> 20; matrix products, arithmetic and copies ran while one was open for 20% -> 12% of each run, Pallas kernels for 0% -> 4%
where the time goes in v1:
time: 361 us; the launch traced here: 359 us
  waiting for transfers between devices  216 us (60%)
  starting transfers between devices  62.9 us (17%)
  matrix products  31.2 us (9%)
  Pallas kernels  24.5 us (7%)
  local copies, waits for them, and re-layouts  12.2 us (3%)
  other arithmetic  11.2 us (3%)
    all_to_all x6, waiting for transfers between devices, exchange(): lax.all_to_all(rows.reshape(parts, total // parts, width), EXPERT, split_...  174 us
    ppermute x20, waiting for transfers between devices, shift(): lax.ppermute(value, axis, [(i, (i + step) % size) for i in range(size)])  41.8 us
    all_to_all x6, starting transfers between devices, exchange(): lax.all_to_all(rows.reshape(parts, total // parts, width), EXPERT, split_...  41.5 us
    ppermute x20, starting transfers between devices, shift(): lax.ppermute(value, axis, [(i, (i + step) % size) for i in range(size)])  21.3 us
    pallas_call x2, Pallas kernels, pack(): kernel_call(functools.partial(pack_body, experts, cap), 'pack', grid=(tot...  8.51 us
    unnamed x34, local copies, waits for them, and re-layouts  8.5 us
  transfers between devices with their start and end apart: 26, of which 20 were waited for; matrix products, arithmetic and copies ran while one was open for 12% of the time, Pallas kernels for 4%

profile of v1, /device:TPU:24, one launch (start us, length us, event | category | flops | bytes accessed | tf_op | source)
XLA Modules:
  0.0 358.8 jit_solution(10158256182310785115)
XLA Ops:
  6.0 11.6 %all-to-all-start = ((bf16[32,32,1024]{2,1,0:T(8,128)(2,1)}), bf16[32,32,1024]{2,1,0:T(8,128)(2,1)}, u32[]{:S(2)}, u32[]{:S(2)}) async-start(bf16[32,32,1024]{2,1,0:T(8,128)(2,1)} %bitcast.2), calls=%async_computation | async-start | bytes 4194304 | tf_op jit(solution)/shard_map/all_to_all | solution.py:218
  17.6 5.3 %pack.2 = bf16[1280,1024]{1,0:T(8,128)(2,1)} custom-call(s32[1,448]{1,0:T(1,128)S(1)} %bitcast.109, bf16[448,1024]{1,0:T(8,128)(2,1)S(1)} %copy-done.4, bf16[448,1024]{1,0:T(8,128)(2,1)S(1)} %copy-done.5), custom_call_target="tpu_custom_call" | custom-call | tf_op jit(solution)/shard_map/pack/pallas_call | solution.py:107
  22.9 44.8 %all-to-all-done = bf16[32,32,1024]{2,1,0:T(8,128)(2,1)} async-done(((bf16[32,32,1024]{2,1,0:T(8,128)(2,1)}), bf16[32,32,1024]{2,1,0:T(8,128)(2,1)}, u32[]{:S(2)}, u32[]{:S(2)}) %all-to-all-start) | async-done | bytes 2097184 | tf_op jit(solution)/shard_map/all_to_all | solution.py:218
  67.8 6.1 %all-to-all-start.1 = ((bf16[32,40,1024]{2,1,0:T(8,128)(2,1)}), bf16[32,40,1024]{2,1,0:T(8,128)(2,1)S(1)}, u32[]{:S(2)}, u32[]{:S(2)}) async-start(bf16[32,40,1024]{2,1,0:T(8,128)(2,1)} %bitcast.5), calls=%async_computation.1 | async-start | bytes 5242880 | tf_op jit(solution)/shard_map/all_to_all | solution.py:218
  73.8 3.2 pack.3
  78.1 55.9 %all-to-all-done.1 = bf16[32,40,1024]{2,1,0:T(8,128)(2,1)S(1)} async-done(((bf16[32,40,1024]{2,1,0:T(8,128)(2,1)}), bf16[32,40,1024]{2,1,0:T(8,128)(2,1)S(1)}, u32[]{:S(2)}, u32[]{:S(2)}) %all-to-all-start.1) | async-done | bytes 2621472 | tf_op jit(solution)/shard_map/all_to_all | solution.py:218
  137.7 6.1 %all-to-all-start.2 = ((bf16[32,40,512]{2,1,0:T(8,128)(2,1)}), bf16[32,40,512]{2,1,0:T(8,128)(2,1)S(1)}, u32[]{:S(2)}, u32[]{:S(2)}) async-start(bf16[32,40,512]{2,1,0:T(8,128)(2,1)} %bitcast.98), calls=%async_computation.2 | async-start | bytes 2621440 | tf_op jit(solution)/shard_map/all_to_all | solution.py:218
  143.8 5.3 %convolution_convert_fusion = bf16[1024,1280]{1,0:T(8,128)(2,1)S(1)} fusion(bf16[1024,1024]{1,0:T(8,128)(2,1)} %bitcast.3, bf16[1280,1024]{1,0:T(8,128)(2,1)} %bitcast.99), kind=kOutput, calls=%fused_computation | convolution fusion | flops 2685665280 | bytes 7340032 | tf_op jit(solution)/shard_map/dot_general | solution.py:313
  150.9 3.1 collective-permute-done
  157.6 3.0 dispatch.3
  160.6 15.1 %all-to-all-done.2 = bf16[32,40,512]{2,1,0:T(8,128)(2,1)S(1)} async-done(((bf16[32,40,512]{2,1,0:T(8,128)(2,1)}), bf16[32,40,512]{2,1,0:T(8,128)(2,1)S(1)}, u32[]{:S(2)}, u32[]{:S(2)}) %all-to-all-start.2) | async-done | bytes 1310752 | tf_op jit(solution)/shard_map/all_to_all | solution.py:218
  175.8 5.8 %all-to-all-start.3 = ((bf16[32,32,1024]{2,1,0:T(8,128)(2,1)}), bf16[32,32,1024]{2,1,0:T(8,128)(2,1)}, u32[]{:S(2)}, u32[]{:S(2)}) async-start(bf16[32,32,1024]{2,1,0:T(8,128)(2,1)} %bitcast.24), calls=%async_computation.3 | async-start | bytes 4194304 | tf_op jit(solution)/shard_map/all_to_all | solution.py:218
  191.6 3.2 collective-permute-done.2
  199.8 3.9 %collective-permute-done.5 = bf16[128,640]{1,0:T(8,128)(2,1)S(1)} collective-permute-done((bf16[128,640]{1,0:T(8,128)(2,1)S(1)}, bf16[128,640]{1,0:T(8,128)(2,1)S(1)}, u32[]{:S(2)}, u32[]{:S(2)}) %collective-permute-start.5) | collective-permute-done | bytes 163872 | tf_op jit(solution)/shard_map/ppermute | solution.py:233
  203.8 3.7 %collective-permute-start.6 = (bf16[128,320]{1,0:T(8,128)(2,1)S(1)}, bf16[128,320]{1,0:T(8,128)(2,1)S(1)}, u32[]{:S(2)}, u32[]{:S(2)}) collective-permute-start(bf16[128,320]{1,0:T(8,128)(2,1)S(1)} %slice.108), channel_id=1, source_target_pairs={{0,64},{64,128},{128,192},{192,0},{1,65},{65,129},{129,193},{193,1... | collective-permute-start | bytes 245768 | tf_op jit(solution)/shard_map/ppermute | solution.py:233
  209.7 3.8 %collective-permute-done.8 = bf16[128,320]{1,0:T(8,128)(2,1)S(1)} collective-permute-done((bf16[128,320]{1,0:T(8,128)(2,1)S(1)}, bf16[128,320]{1,0:T(8,128)(2,1)S(1)}, u32[]{:S(2)}, u32[]{:S(2)}) %collective-permute-start.8) | collective-permute-done | bytes 81952 | tf_op jit(solution)/shard_map/ppermute | solution.py:233
  220.5 3.1 convolution_convert_fusion.2
  223.6 6.5 %all-to-all-done.3 = bf16[32,32,1024]{2,1,0:T(8,128)(2,1)} async-done(((bf16[32,32,1024]{2,1,0:T(8,128)(2,1)}), bf16[32,32,1024]{2,1,0:T(8,128)(2,1)}, u32[]{:S(2)}, u32[]{:S(2)}) %all-to-all-start.3) | async-done | bytes 2097184 | tf_op jit(solution)/shard_map/all_to_all | solution.py:218
  230.0 3.4 convolution_convert_fusion.6
  242.6 3.3 collective-permute-start.12
  245.9 5.9 %all-to-all-start.4 = ((bf16[32,32,1024]{2,1,0:T(8,128)(2,1)}), bf16[32,32,1024]{2,1,0:T(8,128)(2,1)S(1)}, u32[]{:S(2)}, u32[]{:S(2)}) async-start(bf16[32,32,1024]{2,1,0:T(8,128)(2,1)} %bitcast.114), calls=%async_computation.4 | async-start | bytes 4194304 | tf_op jit(solution)/shard_map/all_to_all | solution.py:218
  255.3 5.9 %collective-permute-done.15 = bf16[128,1280]{1,0:T(8,128)(2,1)S(1)} collective-permute-done((bf16[128,1280]{1,0:T(8,128)(2,1)S(1)}, bf16[128,1280]{1,0:T(8,128)(2,1)S(1)}, u32[]{:S(2)}, u32[]{:S(2)}) %collective-permute-start.15) | collective-permute-done | bytes 327712 | tf_op jit(solution)/shard_map/ppermute | solution.py:233
  263.5 3.2 collective-permute-done.16
  275.3 5.9 %convolution_convert_fusion.1 = bf16[1024,1024]{1,0:T(8,128)(2,1)} fusion(bf16[1024,1280]{1,0:T(8,128)(2,1)} %bitcast.41, bf16[1280,1024]{1,0:T(8,128)(2,1)S(1)} %bitcast.100), kind=kOutput, calls=%fused_computation.4 | convolution fusion | flops 2685403136 | bytes 7340032 | tf_op jit(solution)/shard_map/dot_general | solution.py:328
  281.2 19.7 %all-to-all-done.4 = bf16[32,32,1024]{2,1,0:T(8,128)(2,1)S(1)} async-done(((bf16[32,32,1024]{2,1,0:T(8,128)(2,1)}), bf16[32,32,1024]{2,1,0:T(8,128)(2,1)S(1)}, u32[]{:S(2)}, u32[]{:S(2)}) %all-to-all-start.4) | async-done | bytes 2097184 | tf_op jit(solution)/shard_map/all_to_all | solution.py:218
  301.0 6.1 %all-to-all-start.5 = ((bf16[32,32,1024]{2,1,0:T(8,128)(2,1)}), bf16[32,32,1024]{2,1,0:T(8,128)(2,1)}, u32[]{:S(2)}, u32[]{:S(2)}) async-start(bf16[32,32,1024]{2,1,0:T(8,128)(2,1)} %bitcast.115), calls=%async_computation.5 | async-start | bytes 4194304 | tf_op jit(solution)/shard_map/all_to_all | solution.py:218
  307.0 4.6 %fusion.2 = bf16[1,640,1024]{2,1,0:T(8,128)(2,1)} fusion(bf16[1024,1024]{1,0:T(8,128)(2,1)} %bitcast.3, bf16[1024,1280]{1,0:T(8,128)(2,1)} %bitcast.41), kind=kOutput, calls=%fused_computation.11 | convolution fusion | flops 1342832640 | bytes 4718592 | tf_op jit(solution)/shard_map/dot_general | solution.py:336
  311.6 4.7 %fusion.1 = bf16[1,640,1024]{2,1,0:T(8,128)(2,1)} fusion(bf16[1024,1024]{1,0:T(8,128)(2,1)} %bitcast.3, bf16[1024,1280]{1,0:T(8,128)(2,1)} %bitcast.41), kind=kOutput, calls=%fused_computation.10 | convolution fusion | flops 1342832640 | bytes 4718592 | tf_op jit(solution)/shard_map/dot_general | solution.py:333
  316.3 4.2 %fusion.3 = bf16[1,640,1024]{2,1,0:T(8,128)(2,1)} fusion(bf16[1024,640]{1,0:T(8,128)(2,1)S(1)} %bitcast.119, bf16[1024,1024]{1,0:T(8,128)(2,1)} %bitcast.25), kind=kOutput, calls=%fused_computation.12 | convolution fusion | flops 1342832640 | bytes 4718592 | tf_op jit(solution)/shard_map/dot_general | solution.py:332
  320.6 3.0 combine.2
  323.6 31.8 %all-to-all-done.5 = bf16[32,32,1024]{2,1,0:T(8,128)(2,1)} async-done(((bf16[32,32,1024]{2,1,0:T(8,128)(2,1)}), bf16[32,32,1024]{2,1,0:T(8,128)(2,1)}, u32[]{:S(2)}, u32[]{:S(2)}) %all-to-all-start.5) | async-done | bytes 2097184 | tf_op jit(solution)/shard_map/all_to_all | solution.py:218
  355.4 3.4 combine.3
  (108 shorter events, 62.9 us)
Async XLA Ops:
  6.0 11.6 %copy-start.4 = (bf16[448,1024]{1,0:T(8,128)(2,1)S(1)}, bf16[448,1024]{1,0:T(8,128)(2,1)}, u32[]{:S(2)}) copy-start(bf16[448,1024]{1,0:T(8,128)(2,1)} %a_ref.2) | copy-start | bytes 2752516
  6.0 11.6 %copy-start.5 = (bf16[448,1024]{1,0:T(8,128)(2,1)S(1)}, bf16[448,1024]{1,0:T(8,128)(2,1)}, u32[]{:S(2)}) copy-start(bf16[448,1024]{1,0:T(8,128)(2,1)} %b_ref.2) | copy-start | bytes 2752516
  6.0 11.6 %copy-start.12 = (s32[448,1]{0,1:T(1,128)S(1)}, s32[448,1]{0,1:T(1,128)}, u32[]{:S(2)}) copy-start(s32[448,1]{0,1:T(1,128)} %param.12) | copy-start | bytes 5380
  6.0 61.7 %all-to-all-start = ((bf16[32,32,1024]{2,1,0:T(8,128)(2,1)}), bf16[32,32,1024]{2,1,0:T(8,128)(2,1)}, u32[]{:S(2)}, u32[]{:S(2)}) async-start(bf16[32,32,1024]{2,1,0:T(8,128)(2,1)} %bitcast.2), calls=%async_computation | async-start | bytes 4194304 | tf_op jit(solution)/shard_map/all_to_all | solution.py:218
  67.8 6.1 %copy-start.1 = (bf16[448,1024]{1,0:T(8,128)(2,1)S(1)}, bf16[448,1024]{1,0:T(8,128)(2,1)}, u32[]{:S(2)}) copy-start(bf16[448,1024]{1,0:T(8,128)(2,1)} %b_ref.3) | copy-start | bytes 2752516
  67.8 66.3 %all-to-all-start.1 = ((bf16[32,40,1024]{2,1,0:T(8,128)(2,1)}), bf16[32,40,1024]{2,1,0:T(8,128)(2,1)S(1)}, u32[]{:S(2)}, u32[]{:S(2)}) async-start(bf16[32,40,1024]{2,1,0:T(8,128)(2,1)} %bitcast.5), calls=%async_computation.1 | async-start | bytes 5242880 | tf_op jit(solution)/shard_map/all_to_all | solution.py:218
  137.7 38.0 %all-to-all-start.2 = ((bf16[32,40,512]{2,1,0:T(8,128)(2,1)}), bf16[32,40,512]{2,1,0:T(8,128)(2,1)S(1)}, u32[]{:S(2)}, u32[]{:S(2)}) async-start(bf16[32,40,512]{2,1,0:T(8,128)(2,1)} %bitcast.98), calls=%async_computation.2 | async-start | bytes 2621440 | tf_op jit(solution)/shard_map/all_to_all | solution.py:218
  150.7 3.3 collective-permute-start
  156.8 25.1 %collective-permute-start.3 = (bf16[128,640]{1,0:T(8,128)(2,1)}, bf16[128,640]{1,0:T(8,128)(2,1)}, u32[]{:S(2)}, u32[]{:S(2)}) collective-permute-start(bf16[128,640]{1,0:T(8,128)(2,1)} %get-tuple-element.34), channel_id=1, source_target_pairs={{0,192},{64,0},{128,64},{192,128},{1,193},{65,1},{129,65},{193,129... | collective-permute-start | bytes 491528 | tf_op jit(solution)/shard_map/ppermute | solution.py:233
  175.8 54.3 %all-to-all-start.3 = ((bf16[32,32,1024]{2,1,0:T(8,128)(2,1)}), bf16[32,32,1024]{2,1,0:T(8,128)(2,1)}, u32[]{:S(2)}, u32[]{:S(2)}) async-start(bf16[32,32,1024]{2,1,0:T(8,128)(2,1)} %bitcast.24), calls=%async_computation.3 | async-start | bytes 4194304 | tf_op jit(solution)/shard_map/all_to_all | solution.py:218
  181.6 5.9 %collective-permute-start.1 = (bf16[128,640]{1,0:T(8,128)(2,1)S(1)}, bf16[128,640]{1,0:T(8,128)(2,1)S(1)}, u32[]{:S(2)}, u32[]{:S(2)}) collective-permute-start(bf16[128,640]{1,0:T(8,128)(2,1)S(1)} %get-tuple-element.33), channel_id=1, source_target_pairs={{0,64},{64,128},{128,192},{192,0},{1,65},{65,129},{129,193},{193,1... | collective-permute-start | bytes 491528 | tf_op jit(solution)/shard_map/ppermute | solution.py:233
  182.9 8.7 %collective-permute-start.4 = (bf16[128,1280]{1,0:T(8,128)(2,1)S(1)}, bf16[128,1280]{1,0:T(8,128)(2,1)}, u32[]{:S(2)}, u32[]{:S(2)}) collective-permute-start(bf16[128,1280]{1,0:T(8,128)(2,1)S(1)} %pad_maximum_fusion.1), channel_id=1, source_target_pairs={{0,192},{64,0},{128,64},{192,128},{1,193},{65,1},{129,65},{193,129... | collective-permute-start | bytes 983048 | tf_op jit(solution)/shard_map/ppermute | solution.py:233
  187.6 7.3 %collective-permute-start.2 = (bf16[128,1280]{1,0:T(8,128)(2,1)S(1)}, bf16[128,1280]{1,0:T(8,128)(2,1)}, u32[]{:S(2)}, u32[]{:S(2)}) collective-permute-start(bf16[128,1280]{1,0:T(8,128)(2,1)S(1)} %pad_maximum_fusion), channel_id=1, source_target_pairs={{0,64},{64,128},{128,192},{192,0},{1,65},{65,129},{129,193},{193,1... | collective-permute-start | bytes 983048 | tf_op jit(solution)/shard_map/ppermute | solution.py:233
  197.7 6.1 %collective-permute-start.5 = (bf16[128,640]{1,0:T(8,128)(2,1)S(1)}, bf16[128,640]{1,0:T(8,128)(2,1)S(1)}, u32[]{:S(2)}, u32[]{:S(2)}) collective-permute-start(bf16[128,640]{1,0:T(8,128)(2,1)S(1)} %get-tuple-element.24), channel_id=1, source_target_pairs={{0,64},{64,128},{128,192},{192,0},{1,65},{65,129},{129,193},{193,1... | collective-permute-start | bytes 491528 | tf_op jit(solution)/shard_map/ppermute | solution.py:233
  199.8 7.7 %collective-permute-start.7 = (bf16[128,640]{1,0:T(8,128)(2,1)S(1)}, bf16[128,640]{1,0:T(8,128)(2,1)S(1)}, u32[]{:S(2)}, u32[]{:S(2)}) collective-permute-start(bf16[128,640]{1,0:T(8,128)(2,1)S(1)} %get-tuple-element.24), channel_id=1, source_target_pairs={{0,192},{64,0},{128,64},{192,128},{1,193},{65,1},{129,65},{193,129... | collective-permute-start | bytes 491528 | tf_op jit(solution)/shard_map/ppermute | solution.py:233
  203.8 6.0 %collective-permute-start.6 = (bf16[128,320]{1,0:T(8,128)(2,1)S(1)}, bf16[128,320]{1,0:T(8,128)(2,1)S(1)}, u32[]{:S(2)}, u32[]{:S(2)}) collective-permute-start(bf16[128,320]{1,0:T(8,128)(2,1)S(1)} %slice.108), channel_id=1, source_target_pairs={{0,64},{64,128},{128,192},{192,0},{1,65},{65,129},{129,193},{193,1... | collective-permute-start | bytes 245768 | tf_op jit(solution)/shard_map/ppermute | solution.py:233
  207.6 5.9 %collective-permute-start.8 = (bf16[128,320]{1,0:T(8,128)(2,1)S(1)}, bf16[128,320]{1,0:T(8,128)(2,1)S(1)}, u32[]{:S(2)}, u32[]{:S(2)}) collective-permute-start(bf16[128,320]{1,0:T(8,128)(2,1)S(1)} %slice.109), channel_id=1, source_target_pairs={{0,192},{64,0},{128,64},{192,128},{1,193},{65,1},{129,65},{193,129... | collective-permute-start | bytes 245768 | tf_op jit(solution)/shard_map/ppermute | solution.py:233
  215.0 2.4 collective-permute-start.9
  233.5 2.2 collective-permute-start.10
  235.9 6.6 %copy-start.14 = (bf16[4,128,640]{2,1,0:T(8,128)(2,1)}, bf16[4,128,640]{2,1,0:T(8,128)(2,1)S(1)}, u32[]{:S(2)}) copy-start(bf16[4,128,640]{2,1,0:T(8,128)(2,1)S(1)} %fusion.4) | copy-start | bytes 1966084
  236.1 6.1 %collective-permute-start.13 = (bf16[128,320]{1,0:T(8,128)(2,1)S(1)}, bf16[128,320]{1,0:T(8,128)(2,1)S(1)}, u32[]{:S(2)}, u32[]{:S(2)}) collective-permute-start(bf16[128,320]{1,0:T(8,128)(2,1)S(1)} %get-tuple-element.36), channel_id=1, source_target_pairs={{0,192},{64,0},{128,64},{192,128},{1,193},{65,1},{129,65},{193,129... | collective-permute-start | bytes 245768 | tf_op jit(solution)/shard_map/ppermute | solution.py:233
  237.0 5.5 %collective-permute-start.11 = (bf16[128,320]{1,0:T(8,128)(2,1)S(1)}, bf16[128,320]{1,0:T(8,128)(2,1)S(1)}, u32[]{:S(2)}, u32[]{:S(2)}) collective-permute-start(bf16[128,320]{1,0:T(8,128)(2,1)S(1)} %get-tuple-element.35), channel_id=1, source_target_pairs={{0,64},{64,128},{128,192},{192,0},{1,65},{65,129},{129,193},{193,1... | collective-permute-start | bytes 245768 | tf_op jit(solution)/shard_map/ppermute | solution.py:233
  242.4 9.5 %collective-permute-start.14 = (bf16[128,640]{1,0:T(8,128)(2,1)S(1)}, bf16[128,640]{1,0:T(8,128)(2,1)S(1)}, u32[]{:S(2)}, u32[]{:S(2)}) collective-permute-start(bf16[128,640]{1,0:T(8,128)(2,1)S(1)} %pad_maximum_fusion.4), channel_id=1, source_target_pairs={{0,192},{64,0},{128,64},{192,128},{1,193},{65,1},{129,65},{193,129... | collective-permute-start | bytes 491528 | tf_op jit(solution)/shard_map/ppermute | solution.py:233
  242.6 9.2 %collective-permute-start.12 = (bf16[128,640]{1,0:T(8,128)(2,1)S(1)}, bf16[128,640]{1,0:T(8,128)(2,1)S(1)}, u32[]{:S(2)}, u32[]{:S(2)}) collective-permute-start(bf16[128,640]{1,0:T(8,128)(2,1)S(1)} %pad_maximum_fusion.3), channel_id=1, source_target_pairs={{0,64},{64,128},{128,192},{192,0},{1,65},{65,129},{129,193},{193,1... | collective-permute-start | bytes 491528 | tf_op jit(solution)/shard_map/ppermute | solution.py:233
  245.9 55.0 %all-to-all-start.4 = ((bf16[32,32,1024]{2,1,0:T(8,128)(2,1)}), bf16[32,32,1024]{2,1,0:T(8,128)(2,1)S(1)}, u32[]{:S(2)}, u32[]{:S(2)}) async-start(bf16[32,32,1024]{2,1,0:T(8,128)(2,1)} %bitcast.114), calls=%async_computation.4 | async-start | bytes 4194304 | tf_op jit(solution)/shard_map/all_to_all | solution.py:218
  253.1 8.2 %collective-permute-start.15 = (bf16[128,1280]{1,0:T(8,128)(2,1)S(1)}, bf16[128,1280]{1,0:T(8,128)(2,1)S(1)}, u32[]{:S(2)}, u32[]{:S(2)}) collective-permute-start(bf16[128,1280]{1,0:T(8,128)(2,1)S(1)} %pad_maximum_fusion.2), channel_id=1, source_target_pairs={{0,64},{64,128},{128,192},{192,0},{1,65},{65,129},{129,193},{193,1... | collective-permute-start | bytes 983048 | tf_op jit(solution)/shard_map/ppermute | solution.py:233
  253.7 9.1 %collective-permute-start.17 = (bf16[128,1280]{1,0:T(8,128)(2,1)S(1)}, bf16[128,1280]{1,0:T(8,128)(2,1)S(1)}, u32[]{:S(2)}, u32[]{:S(2)}) collective-permute-start(bf16[128,1280]{1,0:T(8,128)(2,1)S(1)} %pad_maximum_fusion.2), channel_id=1, source_target_pairs={{0,192},{64,0},{128,64},{192,128},{1,193},{65,1},{129,65},{193,129... | collective-permute-start | bytes 983048 | tf_op jit(solution)/shard_map/ppermute | solution.py:233
  261.2 5.4 %collective-permute-start.16 = (bf16[128,640]{1,0:T(8,128)(2,1)S(1)}, bf16[128,640]{1,0:T(8,128)(2,1)S(1)}, u32[]{:S(2)}, u32[]{:S(2)}) collective-permute-start(bf16[128,640]{1,0:T(8,128)(2,1)S(1)} %slice.116), channel_id=1, source_target_pairs={{0,64},{64,128},{128,192},{192,0},{1,65},{65,129},{129,193},{193,1... | collective-permute-start | bytes 491528 | tf_op jit(solution)/shard_map/ppermute | solution.py:233
  262.9 6.6 %collective-permute-start.18 = (bf16[128,640]{1,0:T(8,128)(2,1)S(1)}, bf16[128,640]{1,0:T(8,128)(2,1)S(1)}, u32[]{:S(2)}, u32[]{:S(2)}) collective-permute-start(bf16[128,640]{1,0:T(8,128)(2,1)S(1)} %slice.117), channel_id=1, source_target_pairs={{0,192},{64,0},{128,64},{192,128},{1,193},{65,1},{129,65},{193,129... | collective-permute-start | bytes 491528 | tf_op jit(solution)/shard_map/ppermute | solution.py:233
  269.5 3.1 collective-permute-start.19
  301.0 54.4 %all-to-all-start.5 = ((bf16[32,32,1024]{2,1,0:T(8,128)(2,1)}), bf16[32,32,1024]{2,1,0:T(8,128)(2,1)}, u32[]{:S(2)}, u32[]{:S(2)}) async-start(bf16[32,32,1024]{2,1,0:T(8,128)(2,1)} %bitcast.115), calls=%async_computation.5 | async-start | bytes 4194304 | tf_op jit(solution)/shard_map/all_to_all | solution.py:218
  311.6 4.7 %copy-start.16 = (bf16[4,2,128,640]{3,2,1,0:T(8,128)(2,1)S(1)}, bf16[4,2,128,640]{3,2,1,0:T(8,128)(2,1)}, u32[]{:S(2)}) copy-start(bf16[4,2,128,640]{3,2,1,0:T(8,128)(2,1)} %copy-done.15) | copy-start | bytes 3932164
  (11 other events, 14.9 us)

commit v2 on v1

--- a/solution.py
+++ b/solution.py
@@ -53,7 +53,8 @@
     return first / total, second / total
 
 
-def dispatch_body(scaled, experts, cap, route_ref, score_ref, x_ref, out_ref):
+def dispatch_body(scaled, experts, cap, *refs):
+    route_ref, x_ref, out_ref = refs[0], refs[-2], refs[-1]
     block, count = out_ref.shape[0], x_ref.shape[0]
     places = token_places(route_ref, experts, cap)
     slot = iota((block, count), 0) + pl.program_id(0) * block
@@ -61,7 +62,7 @@
     pick = jnp.where(hits[0] | hits[1], 1.0, 0.0).astype(BF16)
     rows = jnp.dot(pick, x_ref[...], preferred_element_type=F32)
     if scaled:
-        shares = token_shares(score_ref)
+        shares = token_shares(refs[1])
         weight = jnp.where(hits[0], shares[0], 0.0) + jnp.where(hits[1], shares[1], 0.0)
         rows = rows * jnp.sum(weight, axis=1, keepdims=True)
     out_ref[...] = rows.astype(BF16)
@@ -76,14 +77,11 @@
         functools.partial(dispatch_body, scaled, experts, cap),
         "dispatch",
         grid=(total // block,),
-        in_specs=[
-            pl.BlockSpec((2, count), whole),
-            pl.BlockSpec((2, count), whole),
-            pl.BlockSpec((count, width), whole),
-        ],
+        in_specs=[pl.BlockSpec((2, count), whole)] * (2 if scaled else 1)
+        + [pl.BlockSpec((count, width), whole)],
         out_specs=pl.BlockSpec((block, width), lambda i: (i, 0)),
         out_shape=jax.ShapeDtypeStruct((total, width), BF16),
-    )(route, score, x)
+    )(*((route, score) if scaled else (route,)), x)
 
 
 def pack_body(experts, cap, ids_ref, a_ref, b_ref, out_ref):
@@ -168,20 +166,125 @@
     )(raw)
 
 
+FREE = pl.CostEstimate(flops=0, bytes_accessed=0, transcendentals=0)
+
+
+def add_half_body(start, rows_ref, half_ref, out_ref):
+    width = half_ref.shape[1]
+    out_ref[...] = rows_ref[...]
+    side = (slice(None), slice(start, start + width))
+    out_ref[side] = (rows_ref[side].astype(F32) + half_ref[...].astype(F32)).astype(BF16)
+
+
+def add_half(rows, half, start):
+    return kernel_call(
+        functools.partial(add_half_body, start),
+        "add_half",
+        out_shape=jax.ShapeDtypeStruct(rows.shape, BF16),
+        cost_estimate=FREE,
+    )(rows, half)
+
+
+def sum_three(refs):
+    return sum(ref[...].astype(F32) for ref in refs)
+
+
+def hidden_body(own_ref, below_ref, above_ref, hidden_ref, sums_ref):
+    sums = sum_three((own_ref, below_ref, above_ref))
+    sums_ref[...] = sums
+    hidden_ref[...] = activate(sums[:, :SLOTS], sums[:, SLOTS:])
+
+
+def hidden_of(parts):
+    rows, n = parts[0].shape
+    return kernel_call(
+        hidden_body,
+        "hidden",
+        out_shape=[
+            jax.ShapeDtypeStruct((rows, n // 2), BF16),
+            jax.ShapeDtypeStruct((rows, n), F32),
+        ],
+        cost_estimate=FREE,
+    )(*parts)
+
+
+def backprop_body(own_ref, below_ref, above_ref, sums_ref, out_ref):
+    back = sum_three((own_ref, below_ref, above_ref))
+    d_gate, d_up = backprop(back, sums_ref[:, :SLOTS], sums_ref[:, SLOTS:])
+    out_ref[:, :SLOTS] = d_gate
+    out_ref[:, SLOTS:] = d_up
+
+
+def backprop_of(parts, sums):
+    return kernel_call(
+        backprop_body,
+        "backprop",
+        out_shape=jax.ShapeDtypeStruct(sums.shape, BF16),
+        cost_estimate=FREE,
+    )(*parts, sums)
+
+
+def interleave_body(core_ref, own_ref, other_ref, out_ref):
+    core = core_ref[0]
+    out_ref[:, core] = own_ref[...]
+    out_ref[:, 1 - core] = other_ref[...]
+
+
+def interleave(own, other, core):
+    ys, rows, n = own.shape
+    return kernel_call(
+        interleave_body,
+        "interleave",
+        in_specs=[
+            pl.BlockSpec(memory_space=pltpu.SMEM),
+            pl.BlockSpec(memory_space=pltpu.VMEM),
+            pl.BlockSpec(memory_space=pltpu.VMEM),
+        ],
+        out_shape=jax.ShapeDtypeStruct((ys, 2, rows, n), own.dtype),
+        cost_estimate=FREE,
+    )(core[None], own, other)
+
+
+def product_body(dims, a_ref, b_ref, out_ref):
+    out_ref[...] = lax.dot_general(
+        a_ref[...], b_ref[...], dims, preferred_element_type=F32
+    ).astype(BF16)
+
+
+def product(a, b, transposed):
+    rows, depth = a.shape
+    n = b.shape[0 if transposed else 1]
+    block = 256
+    dims = (((1,), (1 if transposed else 0,)), ((), ()))
+    return kernel_call(
+        functools.partial(product_body, dims),
+        "product",
+        grid=(rows // block,),
+        in_specs=[
+            pl.BlockSpec((block, depth), lambda i: (i, 0)),
+            pl.BlockSpec(b.shape, lambda i: (0, 0)),
+        ],
+        out_specs=pl.BlockSpec((block, n), lambda i: (i, 0)),
+        out_shape=jax.ShapeDtypeStruct((rows, n), BF16),
+        cost_estimate=FREE,
+    )(a, b)
+
+
 def column_of(row):
     n = row.shape[1]
     same = iota((n, n), 0) == iota((n, n), 1)
     return jnp.sum(jnp.where(same, row, jnp.zeros_like(row)), axis=1, keepdims=True)
 
 
-def combine_body(scaled, experts, cap, route_ref, score_ref, rows_ref, out_ref):
+def combine_body(scaled, experts, cap, *refs):
+    route_ref, rows_ref, out_ref = refs[0], refs[-2], refs[-1]
     count, total = out_ref.shape[0], rows_ref.shape[0]
     places = [column_of(place) for place in token_places(route_ref, experts, cap)]
     slot = iota((count, total), 1)
     hits = [slot == place for place in places]
     rows = rows_ref[...]
     if scaled:
-        shares = [column_of(share) for share in token_shares(score_ref)]
+        shares = [column_of(share) for share in token_shares(refs[1])]
         weight = jnp.where(hits[0], shares[0], 0.0) + jnp.where(hits[1], shares[1], 0.0)
         high = weight.astype(BF16)
         low = (weight - high.astype(F32)).astype(BF16)
@@ -203,14 +306,11 @@
         functools.partial(combine_body, scaled, experts, cap),
         "combine",
         grid=(width // block,),
-        in_specs=[
-            pl.BlockSpec((2, count), whole),
-            pl.BlockSpec((2, count), whole),
-            pl.BlockSpec((total, block), lambda i: (0, i)),
-        ],
+        in_specs=[pl.BlockSpec((2, count), whole)] * (2 if scaled else 1)
+        + [pl.BlockSpec((total, block), lambda i: (0, i))],
         out_specs=pl.BlockSpec((count, block), lambda i: (0, i)),
         out_shape=jax.ShapeDtypeStruct((count, width), BF16),
-    )(route, score, rows)
+    )(*((route, score) if scaled else (route,)), rows)
 
 
 def exchange(rows, parts):
@@ -248,24 +348,20 @@
     value = value.reshape(ys, cores, rows // (ys * cores), n)
     other = shift(pick(value, 1 - core, 1), "core", 1)
     pair = (pick(value, core, 1).astype(F32) + other.astype(F32)).astype(BF16)
-    half = n // 2
+    half = n // 256 * 128
     far = pick(pair, (y + 2) % ys, 0)
-    low = shift(far[:, :half], "y", 1).astype(F32)
-    high = shift(far[:, half:], "y", -1).astype(F32)
-    above = pick(pair, (y + 1) % ys, 0).astype(F32)
-    below = pick(pair, (y + ys - 1) % ys, 0).astype(F32)
-    to_above = jnp.concatenate([above[:, :half] + low, above[:, half:]], axis=1)
-    to_below = jnp.concatenate([below[:, :half], below[:, half:] + high], axis=1)
-    from_below = shift(to_above.astype(BF16), "y", 1).astype(F32)
-    from_above = shift(to_below.astype(BF16), "y", -1).astype(F32)
-    return pick(pair, y, 0).astype(F32) + from_below + from_above
+    low = shift(far[:, :half], "y", 1)
+    high = shift(far[:, half:], "y", -1)
+    to_above = add_half(pick(pair, (y + 1) % ys, 0), low, 0)
+    to_below = add_half(pick(pair, (y + ys - 1) % ys, 0), high, half)
+    return pick(pair, y, 0), shift(to_above, "y", 1), shift(to_below, "y", -1)
 
 
 def gather_blocks(part):
     rows, n = part.shape
     ys, cores = lax.axis_size("y"), lax.axis_size("core")
     y, core = lax.axis_index("y"), lax.axis_index("core")
-    half = n // 2
+    half = n // 256 * 128
     from_below = shift(part, "y", 1)
     from_above = shift(part, "y", -1)
     low = shift(from_below[:, :half], "y", 1)
@@ -275,10 +371,7 @@
     for k, piece in enumerate((part, from_below, far, from_above)):
         column = lax.dynamic_update_slice(column, piece[None], ((y + ys - k) % ys, 0, 0))
     other = shift(column, "core", 1)
-    both = jnp.where(
-        core == 0, jnp.stack([column, other], axis=1), jnp.stack([other, column], axis=1)
-    )
-    return both.reshape(ys * cores * rows, n)
+    return interleave(column, other, core).reshape(ys * cores * rows, n)
 
 
 def activate(gate, upper):
@@ -290,7 +383,7 @@
     sig = jax.nn.sigmoid(gate)
     d_gate = (back * upper * sig * (1.0 + gate * (1.0 - sig))).astype(BF16)
     d_up = (back * gate * sig).astype(BF16)
-    return jnp.concatenate([d_gate, d_up], axis=1)
+    return d_gate, d_up
 
 
 def body(tokens, cotangent, route, score, clusters, w_gate, w_up, w_down):
@@ -299,7 +392,6 @@
     tok_count, width = tokens.shape
     tok_cap = 4 * tok_count // experts
     route, score, ids = route.T, score.T, clusters.T
-    contract = (((1,), (1,)), ((), ()))
     over_rows = (((0,), (0,)), ((), ()))
 
     sent_tokens = dispatch(route, score, tokens, experts, tok_cap, False)
@@ -310,22 +402,19 @@
     raw_down = exchange(after(packed_down, raw), experts)
 
     gate_up_rows = unpack_two(raw, pair_cap)
-    part = lax.dot_general(rows_x, gate_up_rows, contract, preferred_element_type=F32)
-    part = part.astype(BF16)
+    part = product(rows_x, gate_up_rows, True)
     sent_grads = dispatch(route, score, cotangent, experts, tok_cap, True)
     rows_dy = exchange(after(sent_grads, (raw_down, part)), experts)
-    gate_up = scatter_sum(part)
-    gate, upper = gate_up[:, :SLOTS], gate_up[:, SLOTS:]
-    hidden = gather_blocks(activate(gate, upper))
+    hidden, sums = hidden_of(scatter_sum(part))
+    hidden = gather_blocks(hidden)
     down_rows = unpack_one(raw_down, pair_cap)
-    out_part = jnp.dot(hidden, down_rows, preferred_element_type=F32).astype(BF16)
+    out_part = product(hidden, down_rows, False)
     out_part, rows_dy = lax.optimization_barrier((out_part, rows_dy))
     back_out = exchange(out_part, experts)
 
-    back_part = lax.dot_general(rows_dy, down_rows, contract, preferred_element_type=F32)
-    back = scatter_sum(back_part.astype(BF16))
-    d_both = gather_blocks(backprop(back, gate, upper))
-    input_part = jnp.dot(d_both, gate_up_rows, preferred_element_type=F32).astype(BF16)
+    back = scatter_sum(product(rows_dy, down_rows, True))
+    d_both = gather_blocks(backprop_of(back, sums))
+    input_part = product(d_both, gate_up_rows, False)
     back_in = exchange(after(input_part, back_out), experts)
 
     d_both, hidden, rows_dy = after((d_both, hidden, rows_dy), input_part)

time: 361 us -> 349 us (0.967)
  matrix products: 31.2 us -> 11.2 us
  Pallas kernels: 24.5 us -> 42.9 us
  other arithmetic: 11.2 us -> 1.84 us
  waiting for transfers between devices: 216 us -> 208 us
  starting transfers between devices: 62.9 us -> 67.1 us
    pallas_call x0 -> x12, Pallas kernels: none -> 18.6 us  [the longest x4 17.8 us: product(): kernel_call(functools.partial(product_body, dims), 'product', grid=(rows...]
    dot_general x4 -> x0, matrix products: 17.7 us -> none  [the longest x1 5.88 us: body(): jnp.dot(d_both, gate_up_rows, preferred_element_type=F32).astype(BF16)]
    unnamed x34 -> x40, local copies, waits for them, and re-layouts: 8.5 us -> 13.4 us
    ppermute x20, waiting for transfers between devices: 41.8 us -> 37.6 us  [shift(): lax.ppermute(value, axis, [(i, (i + step) % size) for i in range(size)])]
    ppermute x20, starting transfers between devices: 21.3 us -> 25.2 us  [shift(): lax.ppermute(value, axis, [(i, (i + step) % size) for i in range(size)])]
    select_n x2 -> x0, other arithmetic: 3.71 us -> none  [gather_blocks(): jnp.where(core == 0, jnp.stack([column, other], axis=1), jnp.stack([other...]
  transfers between devices with their start and end apart: 26 -> 26, of which waited for: 20 -> 18; matrix products, arithmetic and copies ran while one was open for 12% -> 4% of each run, Pallas kernels for 4% -> 10%
where the time goes in v2:
time: 349 us; the launch traced here: 348 us
  waiting for transfers between devices  208 us (60%)
  starting transfers between devices  67.1 us (19%)
  Pallas kernels  42.9 us (12%)
  local copies, waits for them, and re-layouts  15.2 us (4%)
  matrix products  11.2 us (3%)
    all_to_all x6, waiting for transfers between devices, exchange(): lax.all_to_all(rows.reshape(parts, total // parts, width), EXPERT, split_...  171 us
    all_to_all x6, starting transfers between devices, exchange(): lax.all_to_all(rows.reshape(parts, total // parts, width), EXPERT, split_...  42 us
    ppermute x20, waiting for transfers between devices, shift(): lax.ppermute(value, axis, [(i, (i + step) % size) for i in range(size)])  37.6 us
    ppermute x20, starting transfers between devices, shift(): lax.ppermute(value, axis, [(i, (i + step) % size) for i in range(size)])  25.2 us
    pallas_call x4, Pallas kernels, product(): kernel_call(functools.partial(product_body, dims), 'product', grid=(rows...  17.8 us
    unnamed x40, local copies, waits for them, and re-layouts  13.4 us
    pallas_call x2, Pallas kernels, pack(): kernel_call(functools.partial(pack_body, experts, cap), 'pack', grid=(tot...  7.69 us
    pallas_call x2, Pallas kernels, combine(): kernel_call(functools.partial(combine_body, scaled, experts, cap), 'combi...  7.53 us
  transfers between devices with their start and end apart: 26, of which 18 were waited for; matrix products, arithmetic and copies ran while one was open for 4% of the time, Pallas kernels for 10%

profile of v2, /device:TPU:24, one launch (start us, length us, event | category | flops | bytes accessed | tf_op | source)
XLA Modules:
  0.0 347.6 jit_solution(3438846425872030533)
XLA Ops:
  5.6 11.4 %all-to-all-start = ((bf16[32,32,1024]{2,1,0:T(8,128)(2,1)}), bf16[32,32,1024]{2,1,0:T(8,128)(2,1)S(1)}, u32[]{:S(2)}, u32[]{:S(2)}) async-start(bf16[32,32,1024]{2,1,0:T(8,128)(2,1)} %bitcast.95), calls=%async_computation | async-start | bytes 4194304 | tf_op jit(solution)/shard_map/all_to_all | solution.py:318
  18.3 4.5 %pack.2 = bf16[1280,1024]{1,0:T(8,128)(2,1)S(1)} custom-call(s32[1,448]{1,0:T(1,128)S(1)} %bitcast.107, bf16[448,1024]{1,0:T(8,128)(2,1)S(1)} %copy-done.12, bf16[448,1024]{1,0:T(8,128)(2,1)S(1)} %copy-done.13), custom_call_target="tpu_custom_call" | custom-call | tf_op jit(solution)/shard_map/pack/pallas_call | solution.py:105
  24.2 43.0 %all-to-all-done = bf16[32,32,1024]{2,1,0:T(8,128)(2,1)S(1)} async-done(((bf16[32,32,1024]{2,1,0:T(8,128)(2,1)}), bf16[32,32,1024]{2,1,0:T(8,128)(2,1)S(1)}, u32[]{:S(2)}, u32[]{:S(2)}) %all-to-all-start) | async-done | bytes 2097184 | tf_op jit(solution)/shard_map/all_to_all | solution.py:318
  68.6 6.1 %all-to-all-start.1 = ((bf16[32,40,1024]{2,1,0:T(8,128)(2,1)}), bf16[32,40,1024]{2,1,0:T(8,128)(2,1)S(1)}, u32[]{:S(2)}, u32[]{:S(2)}) async-start(bf16[32,40,1024]{2,1,0:T(8,128)(2,1)} %bitcast.89), calls=%async_computation.1 | async-start | bytes 5242880 | tf_op jit(solution)/shard_map/all_to_all | solution.py:318
  74.7 3.2 pack.3
  78.9 55.9 %all-to-all-done.1 = bf16[32,40,1024]{2,1,0:T(8,128)(2,1)S(1)} async-done(((bf16[32,40,1024]{2,1,0:T(8,128)(2,1)}), bf16[32,40,1024]{2,1,0:T(8,128)(2,1)S(1)}, u32[]{:S(2)}, u32[]{:S(2)}) %all-to-all-start.1) | async-done | bytes 2621472 | tf_op jit(solution)/shard_map/all_to_all | solution.py:318
  134.9 6.2 %all-to-all-start.2 = ((bf16[32,40,512]{2,1,0:T(8,128)(2,1)}), bf16[32,40,512]{2,1,0:T(8,128)(2,1)}, u32[]{:S(2)}, u32[]{:S(2)}) async-start(bf16[32,40,512]{2,1,0:T(8,128)(2,1)} %bitcast.100), calls=%async_computation.2 | async-start | bytes 2621440 | tf_op jit(solution)/shard_map/all_to_all | solution.py:318
  144.8 5.3 %product.4 = bf16[1024,1280]{1,0:T(8,128)(2,1)S(1)} custom-call(bf16[1024,1024]{1,0:T(8,128)(2,1)S(1)} %bitcast.91, bf16[1280,1024]{1,0:T(8,128)(2,1)} %bitcast.81), custom_call_target="tpu_custom_call" | custom-call | tf_op jit(solution)/shard_map/product/pallas_call | solution.py:259
  154.7 18.3 %all-to-all-done.2 = bf16[32,40,512]{2,1,0:T(8,128)(2,1)} async-done(((bf16[32,40,512]{2,1,0:T(8,128)(2,1)}), bf16[32,40,512]{2,1,0:T(8,128)(2,1)}, u32[]{:S(2)}, u32[]{:S(2)}) %all-to-all-start.2) | async-done | bytes 1310752 | tf_op jit(solution)/shard_map/all_to_all | solution.py:318
  173.0 5.8 %all-to-all-start.3 = ((bf16[32,32,1024]{2,1,0:T(8,128)(2,1)}), bf16[32,32,1024]{2,1,0:T(8,128)(2,1)}, u32[]{:S(2)}, u32[]{:S(2)}) async-start(bf16[32,32,1024]{2,1,0:T(8,128)(2,1)} %bitcast.94), calls=%async_computation.3 | async-start | bytes 4194304 | tf_op jit(solution)/shard_map/all_to_all | solution.py:318
  182.8 3.8 %collective-permute-done.1.half_ref = bf16[128,640]{1,0:T(8,128)(2,1)S(1)} collective-permute-done((bf16[128,640]{1,0:T(8,128)(2,1)S(1)}, bf16[128,640]{1,0:T(8,128)(2,1)S(1)}, u32[]{:S(2)}, u32[]{:S(2)}) %collective-permute-start.1) | collective-permute-done | bytes 163872 | tf_op jit(solution)/shard_map/ppermute | solution.py:333
  188.9 4.9 %collective-permute-done.2.below_ref = bf16[128,1280]{1,0:T(8,128)(2,1)S(1)} collective-permute-done((bf16[128,1280]{1,0:T(8,128)(2,1)S(1)}, bf16[128,1280]{1,0:T(8,128)(2,1)S(1)}, u32[]{:S(2)}, u32[]{:S(2)}) %collective-permute-start.2) | collective-permute-done | bytes 327712 | tf_op jit(solution)/shard_map/ppermute | solution.py:333
  199.6 4.1 %collective-permute-done.7 = bf16[128,640]{1,0:T(8,128)(2,1)S(1)} collective-permute-done((bf16[128,640]{1,0:T(8,128)(2,1)S(1)}, bf16[128,640]{1,0:T(8,128)(2,1)S(1)}, u32[]{:S(2)}, u32[]{:S(2)}) %collective-permute-start.7) | collective-permute-done | bytes 163872 | tf_op jit(solution)/shard_map/ppermute | solution.py:333
  203.9 3.5 collective-permute-start.6
  213.0 3.4 product.5
  217.4 9.9 %all-to-all-done.3 = bf16[32,32,1024]{2,1,0:T(8,128)(2,1)} async-done(((bf16[32,32,1024]{2,1,0:T(8,128)(2,1)}), bf16[32,32,1024]{2,1,0:T(8,128)(2,1)}, u32[]{:S(2)}, u32[]{:S(2)}) %all-to-all-start.3) | async-done | bytes 2097184 | tf_op jit(solution)/shard_map/all_to_all | solution.py:318
  227.3 4.0 %product.6 = bf16[1024,640]{1,0:T(8,128)(2,1)S(1)} custom-call(bf16[1024,1024]{1,0:T(8,128)(2,1)} %bitcast.24.a_ref, bf16[640,1024]{1,0:T(8,128)(2,1)S(1)} %unpack_one.1.b_ref), custom_call_target="tpu_custom_call" | custom-call | tf_op jit(solution)/shard_map/product/pallas_call | solution.py:259
  231.5 6.1 %all-to-all-start.4 = ((bf16[32,32,1024]{2,1,0:T(8,128)(2,1)}), bf16[32,32,1024]{2,1,0:T(8,128)(2,1)}, u32[]{:S(2)}, u32[]{:S(2)}) async-start(bf16[32,32,1024]{2,1,0:T(8,128)(2,1)} %bitcast.25), calls=%async_computation.4 | async-start | bytes 4194304 | tf_op jit(solution)/shard_map/all_to_all | solution.py:318
  243.1 3.6 %collective-permute-start.12 = (bf16[128,640]{1,0:T(8,128)(2,1)S(1)}, bf16[128,640]{1,0:T(8,128)(2,1)S(1)}, u32[]{:S(2)}, u32[]{:S(2)}) collective-permute-start(bf16[128,640]{1,0:T(8,128)(2,1)S(1)} %add_half.6), channel_id=1, source_target_pairs={{0,64},{64,128},{128,192},{192,0},{1,65},{65,129},{129,193},{193,1... | collective-permute-start | bytes 491528 | tf_op jit(solution)/shard_map/ppermute | solution.py:333
  249.6 3.8 %collective-permute-done.14.above_ref = bf16[128,640]{1,0:T(8,128)(2,1)S(1)} collective-permute-done((bf16[128,640]{1,0:T(8,128)(2,1)S(1)}, bf16[128,640]{1,0:T(8,128)(2,1)S(1)}, u32[]{:S(2)}, u32[]{:S(2)}) %collective-permute-start.14) | collective-permute-done | bytes 163872 | tf_op jit(solution)/shard_map/ppermute | solution.py:333
  253.7 3.2 collective-permute-start.15
  257.0 5.6 %collective-permute-done.17 = bf16[128,1280]{1,0:T(8,128)(2,1)S(1)} collective-permute-done((bf16[128,1280]{1,0:T(8,128)(2,1)S(1)}, bf16[128,1280]{1,0:T(8,128)(2,1)S(1)}, u32[]{:S(2)}, u32[]{:S(2)}) %collective-permute-start.17) | collective-permute-done | bytes 327712 | tf_op jit(solution)/shard_map/ppermute | solution.py:333
  262.8 3.3 collective-permute-start.16
  266.1 3.2 collective-permute-done.18
  272.6 5.2 %product.7 = bf16[1024,1024]{1,0:T(8,128)(2,1)S(1)} custom-call(bf16[1024,1280]{1,0:T(8,128)(2,1)S(1)} %bitcast.86, bf16[1280,1024]{1,0:T(8,128)(2,1)} %bitcast.82), custom_call_target="tpu_custom_call" | custom-call | tf_op jit(solution)/shard_map/product/pallas_call | solution.py:259
  279.1 9.2 %all-to-all-done.4 = bf16[32,32,1024]{2,1,0:T(8,128)(2,1)} async-done(((bf16[32,32,1024]{2,1,0:T(8,128)(2,1)}), bf16[32,32,1024]{2,1,0:T(8,128)(2,1)}, u32[]{:S(2)}, u32[]{:S(2)}) %all-to-all-start.4) | async-done | bytes 2097184 | tf_op jit(solution)/shard_map/all_to_all | solution.py:318
  288.3 6.3 %all-to-all-start.5 = ((bf16[32,32,1024]{2,1,0:T(8,128)(2,1)}), bf16[32,32,1024]{2,1,0:T(8,128)(2,1)}, u32[]{:S(2)}, u32[]{:S(2)}) async-start(bf16[32,32,1024]{2,1,0:T(8,128)(2,1)} %bitcast.93), calls=%async_computation.5 | async-start | bytes 4194304 | tf_op jit(solution)/shard_map/all_to_all | solution.py:318
  294.6 4.3 %fusion.2 = bf16[1,640,1024]{2,1,0:T(8,128)(2,1)} fusion(bf16[1024,1024]{1,0:T(8,128)(2,1)} %bitcast.90, bf16[1024,1280]{1,0:T(8,128)(2,1)S(1)} %bitcast.87), kind=kOutput, calls=%fused_computation.6 | convolution fusion | flops 1342832640 | bytes 4718592 | tf_op jit(solution)/shard_map/dot_general | solution.py:425
  301.6 4.2 %fusion.3 = bf16[1,640,1024]{2,1,0:T(8,128)(2,1)} fusion(bf16[1024,640]{1,0:T(8,128)(2,1)S(1)} %bitcast.99, bf16[1024,1024]{1,0:T(8,128)(2,1)} %bitcast.24.a_ref), kind=kOutput, calls=%fused_computation.7 | convolution fusion | flops 1342832640 | bytes 4718592 | tf_op jit(solution)/shard_map/dot_general | solution.py:421
  305.8 4.1 %combine.2 = bf16[256,1024]{1,0:T(8,128)(2,1)} custom-call(s32[2,256]{1,0:T(2,128)S(1)} %bitcast.103, s32[2,256]{1,0:T(2,128)S(1)} %bitcast.106, bf16[1024,1024]{1,0:T(8,128)(2,1)} %bitcast.26.refs_2_), custom_call_target="tpu_custom_call" | custom-call | tf_op jit(solution)/shard_map/combine/pallas_call | solution.py:305
  309.9 34.2 %all-to-all-done.5 = bf16[32,32,1024]{2,1,0:T(8,128)(2,1)} async-done(((bf16[32,32,1024]{2,1,0:T(8,128)(2,1)}), bf16[32,32,1024]{2,1,0:T(8,128)(2,1)}, u32[]{:S(2)}, u32[]{:S(2)}) %all-to-all-start.5) | async-done | bytes 2097184 | tf_op jit(solution)/shard_map/all_to_all | solution.py:318
  344.2 3.4 combine.3
  (106 shorter events, 53.3 us)
Async XLA Ops:
  5.6 11.5 %copy-start.12 = (bf16[448,1024]{1,0:T(8,128)(2,1)S(1)}, bf16[448,1024]{1,0:T(8,128)(2,1)}, u32[]{:S(2)}) copy-start(bf16[448,1024]{1,0:T(8,128)(2,1)} %a_ref.2) | copy-start | bytes 2752516
  5.6 11.5 %copy-start.19 = (s32[448,1]{0,1:T(1,128)S(1)}, s32[448,1]{0,1:T(1,128)}, u32[]{:S(2)}) copy-start(s32[448,1]{0,1:T(1,128)} %param.12) | copy-start | bytes 5380
  5.6 61.6 %all-to-all-start = ((bf16[32,32,1024]{2,1,0:T(8,128)(2,1)}), bf16[32,32,1024]{2,1,0:T(8,128)(2,1)S(1)}, u32[]{:S(2)}, u32[]{:S(2)}) async-start(bf16[32,32,1024]{2,1,0:T(8,128)(2,1)} %bitcast.95), calls=%async_computation | async-start | bytes 4194304 | tf_op jit(solution)/shard_map/all_to_all | solution.py:318
  68.6 6.1 %copy-start.11 = (bf16[448,1024]{1,0:T(8,128)(2,1)S(1)}, bf16[448,1024]{1,0:T(8,128)(2,1)}, u32[]{:S(2)}) copy-start(bf16[448,1024]{1,0:T(8,128)(2,1)} %b_ref.3) | copy-start | bytes 2752516
  68.6 66.3 %all-to-all-start.1 = ((bf16[32,40,1024]{2,1,0:T(8,128)(2,1)}), bf16[32,40,1024]{2,1,0:T(8,128)(2,1)S(1)}, u32[]{:S(2)}, u32[]{:S(2)}) async-start(bf16[32,40,1024]{2,1,0:T(8,128)(2,1)} %bitcast.89), calls=%async_computation.1 | async-start | bytes 5242880 | tf_op jit(solution)/shard_map/all_to_all | solution.py:318
  134.9 38.1 %all-to-all-start.2 = ((bf16[32,40,512]{2,1,0:T(8,128)(2,1)}), bf16[32,40,512]{2,1,0:T(8,128)(2,1)}, u32[]{:S(2)}, u32[]{:S(2)}) async-start(bf16[32,40,512]{2,1,0:T(8,128)(2,1)} %bitcast.100), calls=%async_computation.2 | async-start | bytes 2621440 | tf_op jit(solution)/shard_map/all_to_all | solution.py:318
  141.1 3.7 %copy-start.3 = (bf16[32,32,1024]{2,1,0:T(8,128)(2,1)S(1)}, bf16[32,32,1024]{2,1,0:T(8,128)(2,1)}, u32[]{:S(2)}) copy-start(bf16[32,32,1024]{2,1,0:T(8,128)(2,1)} %copy-done.2) | copy-start | bytes 6291460
  151.3 27.6 %collective-permute-start = (bf16[4,128,1280]{2,1,0:T(8,128)(2,1)}, bf16[4,128,1280]{2,1,0:T(8,128)(2,1)}, u32[]{:S(2)}, u32[]{:S(2)}) collective-permute-start(bf16[4,128,1280]{2,1,0:T(8,128)(2,1)} %dynamic-slice_bitcast_fusion), channel_id=1, source_target_pairs={{0,32},{32,0},{1,33},{33,1},{2,34},{34,2},{3,35},{35,3},{4,36},{36... | collective-permute-start | bytes 3932168 | tf_op jit(solution)/shard_map/ppermute | solution.py:333
  173.0 54.3 %all-to-all-start.3 = ((bf16[32,32,1024]{2,1,0:T(8,128)(2,1)}), bf16[32,32,1024]{2,1,0:T(8,128)(2,1)}, u32[]{:S(2)}, u32[]{:S(2)}) async-start(bf16[32,32,1024]{2,1,0:T(8,128)(2,1)} %bitcast.94), calls=%async_computation.3 | async-start | bytes 4194304 | tf_op jit(solution)/shard_map/all_to_all | solution.py:318
  180.6 5.9 %collective-permute-start.1 = (bf16[128,640]{1,0:T(8,128)(2,1)S(1)}, bf16[128,640]{1,0:T(8,128)(2,1)S(1)}, u32[]{:S(2)}, u32[]{:S(2)}) collective-permute-start(bf16[128,640]{1,0:T(8,128)(2,1)S(1)} %get-tuple-element.36), channel_id=1, source_target_pairs={{0,64},{64,128},{128,192},{192,0},{1,65},{65,129},{129,193},{193,1... | collective-permute-start | bytes 491528 | tf_op jit(solution)/shard_map/ppermute | solution.py:333
  180.9 6.7 %collective-permute-start.3 = (bf16[128,640]{1,0:T(8,128)(2,1)S(1)}, bf16[128,640]{1,0:T(8,128)(2,1)S(1)}, u32[]{:S(2)}, u32[]{:S(2)}) collective-permute-start(bf16[128,640]{1,0:T(8,128)(2,1)S(1)} %get-tuple-element.35), channel_id=1, source_target_pairs={{0,192},{64,0},{128,64},{192,128},{1,193},{65,1},{129,65},{193,129... | collective-permute-start | bytes 491528 | tf_op jit(solution)/shard_map/ppermute | solution.py:333
  186.6 7.2 %collective-permute-start.2 = (bf16[128,1280]{1,0:T(8,128)(2,1)S(1)}, bf16[128,1280]{1,0:T(8,128)(2,1)S(1)}, u32[]{:S(2)}, u32[]{:S(2)}) collective-permute-start(bf16[128,1280]{1,0:T(8,128)(2,1)S(1)} %add_half.4), channel_id=1, source_target_pairs={{0,64},{64,128},{128,192},{192,0},{1,65},{65,129},{129,193},{193,1... | collective-permute-start | bytes 983048 | tf_op jit(solution)/shard_map/ppermute | solution.py:333
  187.7 8.4 %collective-permute-start.4 = (bf16[128,1280]{1,0:T(8,128)(2,1)S(1)}, bf16[128,1280]{1,0:T(8,128)(2,1)S(1)}, u32[]{:S(2)}, u32[]{:S(2)}) collective-permute-start(bf16[128,1280]{1,0:T(8,128)(2,1)S(1)} %add_half.5), channel_id=1, source_target_pairs={{0,192},{64,0},{128,64},{192,128},{1,193},{65,1},{129,65},{193,129... | collective-permute-start | bytes 983048 | tf_op jit(solution)/shard_map/ppermute | solution.py:333
  196.2 7.5 %collective-permute-start.7 = (bf16[128,640]{1,0:T(8,128)(2,1)S(1)}, bf16[128,640]{1,0:T(8,128)(2,1)S(1)}, u32[]{:S(2)}, u32[]{:S(2)}) collective-permute-start(bf16[128,640]{1,0:T(8,128)(2,1)S(1)} %get-tuple-element.17), channel_id=1, source_target_pairs={{0,192},{64,0},{128,64},{192,128},{1,193},{65,1},{129,65},{193,129... | collective-permute-start | bytes 491528 | tf_op jit(solution)/shard_map/ppermute | solution.py:333
  196.9 6.9 %collective-permute-start.5 = (bf16[128,640]{1,0:T(8,128)(2,1)S(1)}, bf16[128,640]{1,0:T(8,128)(2,1)S(1)}, u32[]{:S(2)}, u32[]{:S(2)}) collective-permute-start(bf16[128,640]{1,0:T(8,128)(2,1)S(1)} %get-tuple-element.17), channel_id=1, source_target_pairs={{0,64},{64,128},{128,192},{192,0},{1,65},{65,129},{129,193},{193,1... | collective-permute-start | bytes 491528 | tf_op jit(solution)/shard_map/ppermute | solution.py:333
  203.7 5.9 %collective-permute-start.8 = (bf16[128,384]{1,0:T(8,128)(2,1)S(1)}, bf16[128,384]{1,0:T(8,128)(2,1)S(1)}, u32[]{:S(2)}, u32[]{:S(2)}) collective-permute-start(bf16[128,384]{1,0:T(8,128)(2,1)S(1)} %slice.43), channel_id=1, source_target_pairs={{0,192},{64,0},{128,64},{192,128},{1,193},{65,1},{129,65},{193,129... | collective-permute-start | bytes 294920 | tf_op jit(solution)/shard_map/ppermute | solution.py:333
  203.9 5.4 %collective-permute-start.6 = (bf16[128,256]{1,0:T(8,128)(2,1)S(1)}, bf16[128,256]{1,0:T(8,128)(2,1)S(1)}, u32[]{:S(2)}, u32[]{:S(2)}) collective-permute-start(bf16[128,256]{1,0:T(8,128)(2,1)S(1)} %slice.42), channel_id=1, source_target_pairs={{0,64},{64,128},{128,192},{192,0},{1,65},{65,129},{129,193},{193,1... | collective-permute-start | bytes 196616 | tf_op jit(solution)/shard_map/ppermute | solution.py:333
  209.7 3.1 collective-permute-start.9
  231.4 6.2 %collective-permute-start.10 = (bf16[4,128,640]{2,1,0:T(8,128)(2,1)S(1)}, bf16[4,128,640]{2,1,0:T(8,128)(2,1)S(1)}, u32[]{:S(2)}, u32[]{:S(2)}) collective-permute-start(bf16[4,128,640]{2,1,0:T(8,128)(2,1)S(1)} %dynamic-slice_bitcast_fusion.1), channel_id=1, source_target_pairs={{0,32},{32,0},{1,33},{33,1},{2,34},{34,2},{3,35},{35,3},{4,36},{36... | collective-permute-start | bytes 1966088 | tf_op jit(solution)/shard_map/ppermute | solution.py:333
  231.5 56.8 %all-to-all-start.4 = ((bf16[32,32,1024]{2,1,0:T(8,128)(2,1)}), bf16[32,32,1024]{2,1,0:T(8,128)(2,1)}, u32[]{:S(2)}, u32[]{:S(2)}) async-start(bf16[32,32,1024]{2,1,0:T(8,128)(2,1)} %bitcast.25), calls=%async_computation.4 | async-start | bytes 4194304 | tf_op jit(solution)/shard_map/all_to_all | solution.py:318
  237.8 8.9 %collective-permute-start.13 = (bf16[128,384]{1,0:T(8,128)(2,1)S(1)}, bf16[128,384]{1,0:T(8,128)(2,1)S(1)}, u32[]{:S(2)}, u32[]{:S(2)}) collective-permute-start(bf16[128,384]{1,0:T(8,128)(2,1)S(1)} %slice.45), channel_id=1, source_target_pairs={{0,192},{64,0},{128,64},{192,128},{1,193},{65,1},{129,65},{193,129... | collective-permute-start | bytes 294920 | tf_op jit(solution)/shard_map/ppermute | solution.py:333
  238.6 4.4 %collective-permute-start.11 = (bf16[128,256]{1,0:T(8,128)(2,1)S(1)}, bf16[128,256]{1,0:T(8,128)(2,1)S(1)}, u32[]{:S(2)}, u32[]{:S(2)}) collective-permute-start(bf16[128,256]{1,0:T(8,128)(2,1)S(1)} %slice.44), channel_id=1, source_target_pairs={{0,64},{64,128},{128,192},{192,0},{1,65},{65,129},{129,193},{193,1... | collective-permute-start | bytes 196616 | tf_op jit(solution)/shard_map/ppermute | solution.py:333
  243.1 6.5 %collective-permute-start.12 = (bf16[128,640]{1,0:T(8,128)(2,1)S(1)}, bf16[128,640]{1,0:T(8,128)(2,1)S(1)}, u32[]{:S(2)}, u32[]{:S(2)}) collective-permute-start(bf16[128,640]{1,0:T(8,128)(2,1)S(1)} %add_half.6), channel_id=1, source_target_pairs={{0,64},{64,128},{128,192},{192,0},{1,65},{65,129},{129,193},{193,1... | collective-permute-start | bytes 491528 | tf_op jit(solution)/shard_map/ppermute | solution.py:333
  246.8 6.6 %collective-permute-start.14 = (bf16[128,640]{1,0:T(8,128)(2,1)S(1)}, bf16[128,640]{1,0:T(8,128)(2,1)S(1)}, u32[]{:S(2)}, u32[]{:S(2)}) collective-permute-start(bf16[128,640]{1,0:T(8,128)(2,1)S(1)} %add_half.7), channel_id=1, source_target_pairs={{0,192},{64,0},{128,64},{192,128},{1,193},{65,1},{129,65},{193,129... | collective-permute-start | bytes 491528 | tf_op jit(solution)/shard_map/ppermute | solution.py:333
  253.6 9.0 %collective-permute-start.17 = (bf16[128,1280]{1,0:T(8,128)(2,1)S(1)}, bf16[128,1280]{1,0:T(8,128)(2,1)S(1)}, u32[]{:S(2)}, u32[]{:S(2)}) collective-permute-start(bf16[128,1280]{1,0:T(8,128)(2,1)S(1)} %backprop.1), channel_id=1, source_target_pairs={{0,192},{64,0},{128,64},{192,128},{1,193},{65,1},{129,65},{193,129... | collective-permute-start | bytes 983048 | tf_op jit(solution)/shard_map/ppermute | solution.py:333
  253.7 9.1 %collective-permute-start.15 = (bf16[128,1280]{1,0:T(8,128)(2,1)S(1)}, bf16[128,1280]{1,0:T(8,128)(2,1)S(1)}, u32[]{:S(2)}, u32[]{:S(2)}) collective-permute-start(bf16[128,1280]{1,0:T(8,128)(2,1)S(1)} %backprop.1), channel_id=1, source_target_pairs={{0,64},{64,128},{128,192},{192,0},{1,65},{65,129},{129,193},{193,1... | collective-permute-start | bytes 983048 | tf_op jit(solution)/shard_map/ppermute | solution.py:333
  262.6 6.6 %collective-permute-start.18 = (bf16[128,640]{1,0:T(8,128)(2,1)S(1)}, bf16[128,640]{1,0:T(8,128)(2,1)S(1)}, u32[]{:S(2)}, u32[]{:S(2)}) collective-permute-start(bf16[128,640]{1,0:T(8,128)(2,1)S(1)} %slice.47), channel_id=1, source_target_pairs={{0,192},{64,0},{128,64},{192,128},{1,193},{65,1},{129,65},{193,129... | collective-permute-start | bytes 491528 | tf_op jit(solution)/shard_map/ppermute | solution.py:333
  262.8 6.5 %collective-permute-start.16 = (bf16[128,640]{1,0:T(8,128)(2,1)S(1)}, bf16[128,640]{1,0:T(8,128)(2,1)S(1)}, u32[]{:S(2)}, u32[]{:S(2)}) collective-permute-start(bf16[128,640]{1,0:T(8,128)(2,1)S(1)} %slice.46), channel_id=1, source_target_pairs={{0,64},{64,128},{128,192},{192,0},{1,65},{65,129},{129,193},{193,1... | collective-permute-start | bytes 491528 | tf_op jit(solution)/shard_map/ppermute | solution.py:333
  269.3 3.1 collective-permute-start.19
  288.3 55.9 %all-to-all-start.5 = ((bf16[32,32,1024]{2,1,0:T(8,128)(2,1)}), bf16[32,32,1024]{2,1,0:T(8,128)(2,1)}, u32[]{:S(2)}, u32[]{:S(2)}) async-start(bf16[32,32,1024]{2,1,0:T(8,128)(2,1)} %bitcast.93), calls=%async_computation.5 | async-start | bytes 4194304 | tf_op jit(solution)/shard_map/all_to_all | solution.py:318
  294.6 4.4 %copy-start.4 = (bf16[32,32,1024]{2,1,0:T(8,128)(2,1)S(1)}, bf16[32,32,1024]{2,1,0:T(8,128)(2,1)}, u32[]{:S(2)}) copy-start(bf16[32,32,1024]{2,1,0:T(8,128)(2,1)} %copy-done.2) | copy-start | bytes 6291460
  299.0 2.6 copy-start.9
  (14 other events, 17.0 us)

commit v3 on v2

--- a/solution.py
+++ b/solution.py
@@ -14,6 +14,7 @@
 BF16 = jnp.bfloat16
 F32 = jnp.float32
 LIMIT = 48 * 1024 * 1024
+FREE = pl.CostEstimate(flops=0, bytes_accessed=0, transcendentals=0)
 
 
 def iota(shape, axis):
@@ -116,18 +117,77 @@
     )(ids, a, b)
 
 
+def load_body(experts, cap, pair_cap, route_ref, ids_ref, x_ref, a_ref, b_ref, out_ref):
+    per = out_ref.shape[0]
+    first = pl.program_id(0) * per
+    places = token_places(route_ref, experts, cap)
+    slot = iota((per * cap, x_ref.shape[0]), 0) + first * cap
+    pick = jnp.where((slot == places[0]) | (slot == places[1]), 1.0, 0.0).astype(BF16)
+    tokens = jnp.dot(pick, x_ref[...], preferred_element_type=F32)
+    ids, pairs = ids_ref[...], 2 * pair_cap
+    place = ids * pairs + ranks([ids], experts)[0]
+    slot = iota((per * pairs, a_ref.shape[0]), 0) + first * pairs
+    pick_a = jnp.where(slot == place, 1.0, 0.0).astype(BF16)
+    pick_b = jnp.where(slot == place + pair_cap, 1.0, 0.0).astype(BF16)
+    weights = jnp.dot(pick_a, a_ref[...], preferred_element_type=F32) + jnp.dot(
+        pick_b, b_ref[...], preferred_element_type=F32
+    )
+    for k in range(per):
+        out_ref[k, :cap, :] = tokens[k * cap : (k + 1) * cap, :].astype(BF16)
+        out_ref[k, cap:, :] = weights[k * pairs : (k + 1) * pairs, :].astype(BF16)
+
+
+def load(route, ids, x, a, b, experts, cap, pair_cap):
+    width = x.shape[1]
+    per = 4
+    whole = lambda i: (0, 0)
+    return kernel_call(
+        functools.partial(load_body, experts, cap, pair_cap),
+        "load",
+        grid=(experts // per,),
+        in_specs=[pl.BlockSpec(v.shape, whole) for v in (route, ids, x, a, b)],
+        out_specs=pl.BlockSpec((per, cap + 2 * pair_cap, width), lambda i: (i, 0, 0)),
+        out_shape=jax.ShapeDtypeStruct((experts, cap + 2 * pair_cap, width), BF16),
+    )(route, ids, x, a, b)
+
+
+def unload_body(cap, pair_cap, raw_ref, rows_ref, weights_ref):
+    per = raw_ref.shape[0]
+    for k in range(per):
+        rows_ref[k * cap : (k + 1) * cap, :] = raw_ref[k, :cap, :]
+    raw = jnp.concatenate(
+        [raw_ref[k, cap:, :].astype(F32) for k in range(per)], axis=0
+    ).astype(BF16)
+    picks = unpack_picks(weights_ref.shape[1], pair_cap)
+    for k in (0, 1):
+        weights_ref[k] = jnp.dot(picks[k], raw, preferred_element_type=F32).astype(BF16)
+
+
+def unload(raw, cap, pair_cap):
+    experts, width = raw.shape[0], raw.shape[2]
+    per = 8
+    rows, weights = kernel_call(
+        functools.partial(unload_body, cap, pair_cap),
+        "unload",
+        grid=(experts // per,),
+        in_specs=[pl.BlockSpec((per,) + raw.shape[1:], lambda i: (i, 0, 0))],
+        out_specs=[
+            pl.BlockSpec((per * cap, width), lambda i: (i, 0)),
+            pl.BlockSpec((2, per * pair_cap, width), lambda i: (0, i, 0)),
+        ],
+        out_shape=[
+            jax.ShapeDtypeStruct((experts * cap, width), BF16),
+            jax.ShapeDtypeStruct((2, experts * pair_cap, width), BF16),
+        ],
+    )(raw)
+    return rows, weights.reshape(2 * experts * pair_cap, width)
+
+
 def unpack_picks(block, cap):
     row, column = iota((block, 2 * block), 0), iota((block, 2 * block), 1)
     group = sum((row >= g * cap).astype(jnp.int32) for g in range(1, block // cap))
     first = row + cap * group
     return [jnp.where(column == first + k * cap, 1.0, 0.0).astype(BF16) for k in (0, 1)]
-
-
-def unpack_two_body(cap, raw_ref, out_ref):
-    picks = unpack_picks(out_ref.shape[1], cap)
-    raw = raw_ref[...]
-    for k in (0, 1):
-        out_ref[k] = jnp.dot(picks[k], raw, preferred_element_type=F32).astype(BF16)
 
 
 def unpack_one_body(cap, raw_ref, out_ref):
@@ -140,19 +200,6 @@
         ).astype(BF16)
 
 
-def unpack_two(raw, cap):
-    rows, width = raw.shape[0] // 2, raw.shape[1]
-    block = 160
-    return kernel_call(
-        functools.partial(unpack_two_body, cap),
-        "unpack_two",
-        grid=(rows // block,),
-        in_specs=[pl.BlockSpec((2 * block, width), lambda i: (i, 0))],
-        out_specs=pl.BlockSpec((2, block, width), lambda i: (0, i, 0)),
-        out_shape=jax.ShapeDtypeStruct((2, rows, width), BF16),
-    )(raw).reshape(2 * rows, width)
-
-
 def unpack_one(raw, cap):
     rows, width = raw.shape[0] // 2, raw.shape[1]
     block = 160
@@ -164,9 +211,6 @@
         out_specs=pl.BlockSpec((block, 2 * width), lambda i: (i, 0)),
         out_shape=jax.ShapeDtypeStruct((rows, 2 * width), BF16),
     )(raw)
-
-
-FREE = pl.CostEstimate(flops=0, bytes_accessed=0, transcendentals=0)
 
 
 def add_half_body(start, rows_ref, half_ref, out_ref):
@@ -243,6 +287,45 @@
         out_shape=jax.ShapeDtypeStruct((ys, 2, rows, n), own.dtype),
         cost_estimate=FREE,
     )(core[None], own, other)
+
+
+def pair_body(core_ref, value_ref, other_ref, out_ref):
+    own = value_ref[:, core_ref[0]]
+    out_ref[...] = (own.astype(F32) + other_ref[...].astype(F32)).astype(BF16)
+
+
+def pair_sum(core, value, other):
+    vmem = pl.BlockSpec(memory_space=pltpu.VMEM)
+    return kernel_call(
+        pair_body,
+        "pair_sum",
+        in_specs=[pl.BlockSpec(memory_space=pltpu.SMEM), vmem, vmem],
+        out_shape=jax.ShapeDtypeStruct(other.shape, BF16),
+        cost_estimate=FREE,
+    )(core[None], value, other)
+
+
+def column_body(y_ref, own_ref, below_ref, above_ref, low_ref, high_ref, out_ref):
+    ys, half = out_ref.shape[0], low_ref.shape[1]
+    y = y_ref[0]
+    out_ref[y] = own_ref[...]
+    out_ref[lax.rem(y + ys - 1, ys)] = below_ref[...]
+    out_ref[lax.rem(y + 1, ys)] = above_ref[...]
+    far = lax.rem(y + 2, ys)
+    out_ref[far, :, :half] = low_ref[...]
+    out_ref[far, :, half:] = high_ref[...]
+
+
+def column(y, own, below, above, low, high):
+    ys = lax.axis_size("y")
+    vmem = pl.BlockSpec(memory_space=pltpu.VMEM)
+    return kernel_call(
+        column_body,
+        "column",
+        in_specs=[pl.BlockSpec(memory_space=pltpu.SMEM)] + [vmem] * 5,
+        out_shape=jax.ShapeDtypeStruct((ys,) + own.shape, own.dtype),
+        cost_estimate=FREE,
+    )(y[None], own, below, above, low, high)
 
 
 def product_body(dims, a_ref, b_ref, out_ref):
@@ -347,7 +430,7 @@
     y, core = lax.axis_index("y"), lax.axis_index("core")
     value = value.reshape(ys, cores, rows // (ys * cores), n)
     other = shift(pick(value, 1 - core, 1), "core", 1)
-    pair = (pick(value, core, 1).astype(F32) + other.astype(F32)).astype(BF16)
+    pair = pair_sum(core, value, other)
     half = n // 256 * 128
     far = pick(pair, (y + 2) % ys, 0)
     low = shift(far[:, :half], "y", 1)
@@ -366,12 +449,9 @@
     from_above = shift(part, "y", -1)
     low = shift(from_below[:, :half], "y", 1)
     high = shift(from_above[:, half:], "y", -1)
-    far = jnp.concatenate([low, high], axis=1)
-    column = jnp.zeros((ys, rows, n), part.dtype)
-    for k, piece in enumerate((part, from_below, far, from_above)):
-        column = lax.dynamic_update_slice(column, piece[None], ((y + ys - k) % ys, 0, 0))
-    other = shift(column, "core", 1)
-    return interleave(column, other, core).reshape(ys * cores * rows, n)
+    held = column(y, part, from_below, from_above, low, high)
+    other = shift(held, "core", 1)
+    return interleave(held, other, core).reshape(ys * cores * rows, n)
 
 
 def activate(gate, upper):
@@ -394,14 +474,11 @@
     route, score, ids = route.T, score.T, clusters.T
     over_rows = (((0,), (0,)), ((), ()))
 
-    sent_tokens = dispatch(route, score, tokens, experts, tok_cap, False)
-    rows_x = exchange(sent_tokens, experts)
-    packed = pack(ids, w_gate, w_up, experts, pair_cap, width, (0, 0))
-    raw = exchange(after(packed, rows_x), experts)
+    sent = load(route, ids, tokens, w_gate, w_up, experts, tok_cap, pair_cap)
+    raw = lax.all_to_all(sent, EXPERT, split_axis=0, concat_axis=0, tiled=True)
     packed_down = pack(ids, w_down, w_down, experts, pair_cap, width // 2, (0, 1))
     raw_down = exchange(after(packed_down, raw), experts)
-
-    gate_up_rows = unpack_two(raw, pair_cap)
+    rows_x, gate_up_rows = unload(raw, tok_cap, pair_cap)
     part = product(rows_x, gate_up_rows, True)
     sent_grads = dispatch(route, score, cotangent, experts, tok_cap, True)
     rows_dy = exchange(after(sent_grads, (raw_down, part)), experts)

time: 349 us -> 349 us (level)
  Pallas kernels: 42.9 us -> 50 us
    all_to_all x6 -> x4, waiting for transfers between devices: 171 us -> 58.6 us  [exchange(): lax.all_to_all(rows.reshape(parts, total // parts, width), EXPERT, split_...]
    all_to_all x0 -> x1, waiting for transfers between devices: none -> 101 us  [body(): raw = lax.all_to_all(sent, EXPERT, split_axis=0, concat_axis=0, tiled=True)]
    all_to_all x6 -> x4, starting transfers between devices: 42 us -> 28.3 us  [exchange(): lax.all_to_all(rows.reshape(parts, total // parts, width), EXPERT, split_...]
    pallas_call x1 -> x6, Pallas kernels: 2.22 us -> 14.7 us  [the longest x1 8.32 us: load(): kernel_call(functools.partial(load_body, experts, cap, pair_cap), 'load',...]
    all_to_all x0 -> x1, starting transfers between devices: none -> 11.6 us  [body(): raw = lax.all_to_all(sent, EXPERT, split_axis=0, concat_axis=0, tiled=True)]
    ppermute x20, waiting for transfers between devices: 37.6 us -> 45.3 us  [shift(): lax.ppermute(value, axis, [(i, (i + step) % size) for i in range(size)])]
    pallas_call x2 -> x1, Pallas kernels: 7.69 us -> 4.04 us  [pack(): kernel_call(functools.partial(pack_body, experts, cap), 'pack', grid=(tot...]
    unnamed x40 -> x34, local copies, waits for them, and re-layouts: 13.4 us -> 11.4 us
  transfers between devices with their start and end apart: 26 -> 25, of which waited for: 18 -> 19; matrix products, arithmetic and copies ran while one was open for 4% -> 4% of each run, Pallas kernels for 10% -> 11%
where the time goes in v3:
time: 349 us; the launch traced here: 345 us
  waiting for transfers between devices  205 us (59%)
  starting transfers between devices  65.2 us (19%)
  Pallas kernels  50 us (14%)
  local copies, waits for them, and re-layouts  12.9 us (4%)
  matrix products  11.2 us (3%)
    all_to_all x1, waiting for transfers between devices, body(): raw = lax.all_to_all(sent, EXPERT, split_axis=0, concat_axis=0, tiled=True)  101 us
    all_to_all x4, waiting for transfers between devices, exchange(): lax.all_to_all(rows.reshape(parts, total // parts, width), EXPERT, split_...  58.6 us
    ppermute x20, waiting for transfers between devices, shift(): lax.ppermute(value, axis, [(i, (i + step) % size) for i in range(size)])  45.3 us
    all_to_all x4, starting transfers between devices, exchange(): lax.all_to_all(rows.reshape(parts, total // parts, width), EXPERT, split_...  28.3 us
    ppermute x20, starting transfers between devices, shift(): lax.ppermute(value, axis, [(i, (i + step) % size) for i in range(size)])  25.3 us
    pallas_call x4, Pallas kernels, product(): kernel_call(functools.partial(product_body, dims), 'product', grid=(rows...  18 us
    all_to_all x1, starting transfers between devices, body(): raw = lax.all_to_all(sent, EXPERT, split_axis=0, concat_axis=0, tiled=True)  11.6 us
    unnamed x34, local copies, waits for them, and re-layouts  11.4 us
  transfers between devices with their start and end apart: 25, of which 19 were waited for; matrix products, arithmetic and copies ran while one was open for 4% of the time, Pallas kernels for 11%

profile of v3, /device:TPU:24, one launch (start us, length us, event | category | flops | bytes accessed | tf_op | source)
XLA Modules:
  0.0 345.3 jit_solution(14402006064763562578)
XLA Ops:
  5.4 8.3 %load.1 = bf16[32,72,1024]{2,1,0:T(8,128)(2,1)} custom-call(s32[2,256]{1,0:T(2,128)S(1)} %bitcast.61, s32[1,448]{1,0:T(1,128)S(1)} %bitcast.67, bf16[256,1024]{1,0:T(8,128)(2,1)S(1)} %copy-done.10, bf16[448,1024]{1,0:T(8,128)(2,1)S(1)} %copy-done.8, bf16[448,1024]{1,0:T(8,128)(2,1)S(1)} %copy-done.9), custom_call_target="tpu_custom_call" | custom-call | tf_op jit(solution)/shard_map/load/pallas_call | solution.py:144
  13.7 11.6 %all-to-all-start = ((bf16[32,72,1024]{2,1,0:T(8,128)(2,1)}), bf16[32,72,1024]{2,1,0:T(8,128)(2,1)}, u32[]{:S(2)}, u32[]{:S(2)}) async-start(bf16[32,72,1024]{2,1,0:T(8,128)(2,1)} %load.1), calls=%async_computation | async-start | bytes 9437184 | tf_op jit(solution)/shard_map/all_to_all | solution.py:478
  25.3 4.0 %pack.1 = bf16[1280,512]{1,0:T(8,128)(2,1)} custom-call(s32[1,448]{1,0:T(1,128)S(1)} %bitcast.68, bf16[448,1024]{1,0:T(8,128)(2,1)S(1)} %copy-done.5, bf16[448,1024]{1,0:T(8,128)(2,1)S(1)} %copy-done.5), custom_call_target="tpu_custom_call" | custom-call | tf_op jit(solution)/shard_map/pack/pallas_call | solution.py:106
  29.4 101.2 %all-to-all-done.raw_ref = bf16[32,72,1024]{2,1,0:T(8,128)(2,1)} async-done(((bf16[32,72,1024]{2,1,0:T(8,128)(2,1)}), bf16[32,72,1024]{2,1,0:T(8,128)(2,1)}, u32[]{:S(2)}, u32[]{:S(2)}) %all-to-all-start) | async-done | bytes 4718624 | tf_op jit(solution)/shard_map/all_to_all | solution.py:478
  130.5 8.9 %all-to-all-start.1 = ((bf16[32,40,512]{2,1,0:T(8,128)(2,1)}), bf16[32,40,512]{2,1,0:T(8,128)(2,1)}, u32[]{:S(2)}, u32[]{:S(2)}) async-start(bf16[32,40,512]{2,1,0:T(8,128)(2,1)} %bitcast.13), calls=%async_computation.1 | async-start | bytes 2621440 | tf_op jit(solution)/shard_map/all_to_all | solution.py:401
  142.8 4.4 %unload.1 = (bf16[1024,1024]{1,0:T(8,128)(2,1)S(1)}, bf16[2,640,1024]{2,1,0:T(8,128)(2,1)S(1)}) custom-call(bf16[32,72,1024]{2,1,0:T(8,128)(2,1)} %all-to-all-done.raw_ref), custom_call_target="tpu_custom_call" | custom-call | tf_op jit(solution)/shard_map/unload/pallas_call | solution.py:169
  148.7 5.3 %product.4 = bf16[1024,1280]{1,0:T(8,128)(2,1)S(1)} custom-call(bf16[1024,1024]{1,0:T(8,128)(2,1)S(1)} %get-tuple-element.17.a_ref, bf16[1280,1024]{1,0:T(8,128)(2,1)} %bitcast.50), custom_call_target="tpu_custom_call" | custom-call | tf_op jit(solution)/shard_map/product/pallas_call | solution.py:342
  155.3 17.4 %all-to-all-done.1 = bf16[32,40,512]{2,1,0:T(8,128)(2,1)} async-done(((bf16[32,40,512]{2,1,0:T(8,128)(2,1)}), bf16[32,40,512]{2,1,0:T(8,128)(2,1)}, u32[]{:S(2)}, u32[]{:S(2)}) %all-to-all-start.1) | async-done | bytes 1310752 | tf_op jit(solution)/shard_map/all_to_all | solution.py:401
  172.8 5.8 %all-to-all-start.2 = ((bf16[32,32,1024]{2,1,0:T(8,128)(2,1)}), bf16[32,32,1024]{2,1,0:T(8,128)(2,1)}, u32[]{:S(2)}, u32[]{:S(2)}) async-start(bf16[32,32,1024]{2,1,0:T(8,128)(2,1)} %bitcast.56), calls=%async_computation.2 | async-start | bytes 4194304 | tf_op jit(solution)/shard_map/all_to_all | solution.py:401
  179.7 3.4 collective-permute-done.other_ref
  187.1 4.2 %collective-permute-done.1.half_ref = bf16[128,640]{1,0:T(8,128)(2,1)S(1)} collective-permute-done((bf16[128,640]{1,0:T(8,128)(2,1)S(1)}, bf16[128,640]{1,0:T(8,128)(2,1)S(1)}, u32[]{:S(2)}, u32[]{:S(2)}) %collective-permute-start.1) | collective-permute-done | bytes 163872 | tf_op jit(solution)/shard_map/ppermute | solution.py:416
  193.6 6.9 %collective-permute-done.2.below_ref = bf16[128,1280]{1,0:T(8,128)(2,1)S(1)} collective-permute-done((bf16[128,1280]{1,0:T(8,128)(2,1)S(1)}, bf16[128,1280]{1,0:T(8,128)(2,1)S(1)}, u32[]{:S(2)}, u32[]{:S(2)}) %collective-permute-start.2) | collective-permute-done | bytes 327712 | tf_op jit(solution)/shard_map/ppermute | solution.py:416
  203.4 3.2 collective-permute-start.5
  206.6 3.3 collective-permute-done.6.above_ref
  210.0 3.3 collective-permute-start.7
  219.3 3.3 product.5
  223.7 3.7 %all-to-all-done.2 = bf16[32,32,1024]{2,1,0:T(8,128)(2,1)} async-done(((bf16[32,32,1024]{2,1,0:T(8,128)(2,1)}), bf16[32,32,1024]{2,1,0:T(8,128)(2,1)}, u32[]{:S(2)}, u32[]{:S(2)}) %all-to-all-start.2) | async-done | bytes 2097184 | tf_op jit(solution)/shard_map/all_to_all | solution.py:401
  227.4 6.1 %all-to-all-start.3 = ((bf16[32,32,1024]{2,1,0:T(8,128)(2,1)}), bf16[32,32,1024]{2,1,0:T(8,128)(2,1)}, u32[]{:S(2)}, u32[]{:S(2)}) async-start(bf16[32,32,1024]{2,1,0:T(8,128)(2,1)} %bitcast.17), calls=%async_computation.3 | async-start | bytes 4194304 | tf_op jit(solution)/shard_map/all_to_all | solution.py:401
  233.5 4.0 %product.6 = bf16[1024,640]{1,0:T(8,128)(2,1)S(1)} custom-call(bf16[1024,1024]{1,0:T(8,128)(2,1)} %bitcast.16.a_ref, bf16[640,1024]{1,0:T(8,128)(2,1)S(1)} %unpack_one.1.b_ref), custom_call_target="tpu_custom_call" | custom-call | tf_op jit(solution)/shard_map/product/pallas_call | solution.py:342
  245.3 3.6 %collective-permute-start.12 = (bf16[128,640]{1,0:T(8,128)(2,1)S(1)}, bf16[128,640]{1,0:T(8,128)(2,1)S(1)}, u32[]{:S(2)}, u32[]{:S(2)}) collective-permute-start(bf16[128,640]{1,0:T(8,128)(2,1)S(1)} %add_half.6), channel_id=1, source_target_pairs={{0,64},{64,128},{128,192},{192,0},{1,65},{65,129},{129,193},{193,1... | collective-permute-start | bytes 491528 | tf_op jit(solution)/shard_map/ppermute | solution.py:416
  251.9 3.7 %collective-permute-done.14.above_ref = bf16[128,640]{1,0:T(8,128)(2,1)S(1)} collective-permute-done((bf16[128,640]{1,0:T(8,128)(2,1)S(1)}, bf16[128,640]{1,0:T(8,128)(2,1)S(1)}, u32[]{:S(2)}, u32[]{:S(2)}) %collective-permute-start.14) | collective-permute-done | bytes 163872 | tf_op jit(solution)/shard_map/ppermute | solution.py:416
  255.9 3.2 collective-permute-start.15
  259.1 5.9 %collective-permute-done.16.above_ref = bf16[128,1280]{1,0:T(8,128)(2,1)S(1)} collective-permute-done((bf16[128,1280]{1,0:T(8,128)(2,1)S(1)}, bf16[128,1280]{1,0:T(8,128)(2,1)S(1)}, u32[]{:S(2)}, u32[]{:S(2)}) %collective-permute-start.16) | collective-permute-done | bytes 327712 | tf_op jit(solution)/shard_map/ppermute | solution.py:416
  265.2 3.3 collective-permute-start.17
  268.4 3.2 collective-permute-done.18.high_ref
  275.0 5.3 %product.7 = bf16[1024,1024]{1,0:T(8,128)(2,1)S(1)} custom-call(bf16[1024,1280]{1,0:T(8,128)(2,1)S(1)} %bitcast.52, bf16[1280,1024]{1,0:T(8,128)(2,1)} %bitcast.51), custom_call_target="tpu_custom_call" | custom-call | tf_op jit(solution)/shard_map/product/pallas_call | solution.py:342
  284.3 7.4 %all-to-all-start.4 = ((bf16[32,32,1024]{2,1,0:T(8,128)(2,1)}), bf16[32,32,1024]{2,1,0:T(8,128)(2,1)}, u32[]{:S(2)}, u32[]{:S(2)}) async-start(bf16[32,32,1024]{2,1,0:T(8,128)(2,1)} %bitcast.55), calls=%async_computation.4 | async-start | bytes 4194304 | tf_op jit(solution)/shard_map/all_to_all | solution.py:401
  291.7 4.4 %fusion.1 = bf16[1,640,1024]{2,1,0:T(8,128)(2,1)} fusion(bf16[1024,1024]{1,0:T(8,128)(2,1)} %copy-done.6, bf16[1024,1280]{1,0:T(8,128)(2,1)S(1)} %bitcast.53), kind=kOutput, calls=%fused_computation.4 | convolution fusion | flops 1342832640 | bytes 4718592 | tf_op jit(solution)/shard_map/dot_general | solution.py:502
  298.7 4.2 %fusion.2 = bf16[1,640,1024]{2,1,0:T(8,128)(2,1)} fusion(bf16[1024,640]{1,0:T(8,128)(2,1)S(1)} %bitcast.60, bf16[1024,1024]{1,0:T(8,128)(2,1)} %bitcast.16.a_ref), kind=kOutput, calls=%fused_computation.5 | convolution fusion | flops 1342832640 | bytes 4718592 | tf_op jit(solution)/shard_map/dot_general | solution.py:498
  302.9 4.1 %combine.2 = bf16[256,1024]{1,0:T(8,128)(2,1)} custom-call(s32[2,256]{1,0:T(2,128)S(1)} %bitcast.63, s32[2,256]{1,0:T(2,128)S(1)} %bitcast.66, bf16[1024,1024]{1,0:T(8,128)(2,1)} %bitcast.18.refs_2_), custom_call_target="tpu_custom_call" | custom-call | tf_op jit(solution)/shard_map/combine/pallas_call | solution.py:388
  307.0 34.9 %all-to-all-done.4 = bf16[32,32,1024]{2,1,0:T(8,128)(2,1)} async-done(((bf16[32,32,1024]{2,1,0:T(8,128)(2,1)}), bf16[32,32,1024]{2,1,0:T(8,128)(2,1)}, u32[]{:S(2)}, u32[]{:S(2)}) %all-to-all-start.4) | async-done | bytes 2097184 | tf_op jit(solution)/shard_map/all_to_all | solution.py:401
  341.9 3.4 combine.3
  (89 shorter events, 49.3 us)
Async XLA Ops:
  13.7 11.6 %copy-start.5 = (bf16[448,1024]{1,0:T(8,128)(2,1)S(1)}, bf16[448,1024]{1,0:T(8,128)(2,1)}, u32[]{:S(2)}) copy-start(bf16[448,1024]{1,0:T(8,128)(2,1)} %b_ref.3) | copy-start | bytes 2752516
  13.7 11.6 %copy-start.16 = (s32[448,1]{0,1:T(1,128)S(1)}, s32[448,1]{0,1:T(1,128)}, u32[]{:S(2)}) copy-start(s32[448,1]{0,1:T(1,128)} %param.12) | copy-start | bytes 5380
  13.7 116.8 %all-to-all-start = ((bf16[32,72,1024]{2,1,0:T(8,128)(2,1)}), bf16[32,72,1024]{2,1,0:T(8,128)(2,1)}, u32[]{:S(2)}, u32[]{:S(2)}) async-start(bf16[32,72,1024]{2,1,0:T(8,128)(2,1)} %load.1), calls=%async_computation | async-start | bytes 9437184 | tf_op jit(solution)/shard_map/all_to_all | solution.py:478
  29.4 110.1 %copy-start.11 = (bf16[256,1024]{1,0:T(8,128)(2,1)S(1)}, bf16[256,1024]{1,0:T(8,128)(2,1)}, u32[]{:S(2)}) copy-start(bf16[256,1024]{1,0:T(8,128)(2,1)} %refs_2_.1) | copy-start | bytes 1572868
  29.4 110.1 %copy-start.13 = (s32[256,2]{0,1:T(2,128)S(1)}, s32[256,2]{0,1:T(2,128)}, u32[]{:S(2)}) copy-start(s32[256,2]{0,1:T(2,128)} %param.10) | copy-start | bytes 6148
  29.4 110.1 %copy-start.14 = (s32[256,2]{0,1:T(2,128)S(1)}, s32[256,2]{0,1:T(2,128)}, u32[]{:S(2)}) copy-start(s32[256,2]{0,1:T(2,128)} %param.11) | copy-start | bytes 6148
  130.5 42.2 %all-to-all-start.1 = ((bf16[32,40,512]{2,1,0:T(8,128)(2,1)}), bf16[32,40,512]{2,1,0:T(8,128)(2,1)}, u32[]{:S(2)}, u32[]{:S(2)}) async-start(bf16[32,40,512]{2,1,0:T(8,128)(2,1)} %bitcast.13), calls=%async_computation.1 | async-start | bytes 2621440 | tf_op jit(solution)/shard_map/all_to_all | solution.py:401
  172.8 54.6 %all-to-all-start.2 = ((bf16[32,32,1024]{2,1,0:T(8,128)(2,1)}), bf16[32,32,1024]{2,1,0:T(8,128)(2,1)}, u32[]{:S(2)}, u32[]{:S(2)}) async-start(bf16[32,32,1024]{2,1,0:T(8,128)(2,1)} %bitcast.56), calls=%async_computation.2 | async-start | bytes 4194304 | tf_op jit(solution)/shard_map/all_to_all | solution.py:401
  179.7 3.4 collective-permute-start
  185.0 6.3 %collective-permute-start.1 = (bf16[128,640]{1,0:T(8,128)(2,1)S(1)}, bf16[128,640]{1,0:T(8,128)(2,1)S(1)}, u32[]{:S(2)}, u32[]{:S(2)}) collective-permute-start(bf16[128,640]{1,0:T(8,128)(2,1)S(1)} %get-tuple-element.38), channel_id=1, source_target_pairs={{0,64},{64,128},{128,192},{192,0},{1,65},{65,129},{129,193},{193,1... | collective-permute-start | bytes 491528 | tf_op jit(solution)/shard_map/ppermute | solution.py:416
  185.3 7.7 %collective-permute-start.3 = (bf16[128,640]{1,0:T(8,128)(2,1)S(1)}, bf16[128,640]{1,0:T(8,128)(2,1)S(1)}, u32[]{:S(2)}, u32[]{:S(2)}) collective-permute-start(bf16[128,640]{1,0:T(8,128)(2,1)S(1)} %get-tuple-element.37), channel_id=1, source_target_pairs={{0,192},{64,0},{128,64},{192,128},{1,193},{65,1},{129,65},{193,129... | collective-permute-start | bytes 491528 | tf_op jit(solution)/shard_map/ppermute | solution.py:416
  191.4 9.1 %collective-permute-start.2 = (bf16[128,1280]{1,0:T(8,128)(2,1)S(1)}, bf16[128,1280]{1,0:T(8,128)(2,1)S(1)}, u32[]{:S(2)}, u32[]{:S(2)}) collective-permute-start(bf16[128,1280]{1,0:T(8,128)(2,1)S(1)} %add_half.4), channel_id=1, source_target_pairs={{0,64},{64,128},{128,192},{192,0},{1,65},{65,129},{129,193},{193,1... | collective-permute-start | bytes 983048 | tf_op jit(solution)/shard_map/ppermute | solution.py:416
  193.0 10.1 %collective-permute-start.4 = (bf16[128,1280]{1,0:T(8,128)(2,1)S(1)}, bf16[128,1280]{1,0:T(8,128)(2,1)S(1)}, u32[]{:S(2)}, u32[]{:S(2)}) collective-permute-start(bf16[128,1280]{1,0:T(8,128)(2,1)S(1)} %add_half.5), channel_id=1, source_target_pairs={{0,192},{64,0},{128,64},{192,128},{1,193},{65,1},{129,65},{193,129... | collective-permute-start | bytes 983048 | tf_op jit(solution)/shard_map/ppermute | solution.py:416
  203.3 6.6 %collective-permute-start.6 = (bf16[128,640]{1,0:T(8,128)(2,1)S(1)}, bf16[128,640]{1,0:T(8,128)(2,1)S(1)}, u32[]{:S(2)}, u32[]{:S(2)}) collective-permute-start(bf16[128,640]{1,0:T(8,128)(2,1)S(1)} %get-tuple-element.19.own_ref), channel_id=1, source_target_pairs={{0,192},{64,0},{128,64},{192,128},{1,193},{65,1},{129,65},{193,129... | collective-permute-start | bytes 491528 | tf_op jit(solution)/shard_map/ppermute | solution.py:416
  203.4 6.6 %collective-permute-start.5 = (bf16[128,640]{1,0:T(8,128)(2,1)S(1)}, bf16[128,640]{1,0:T(8,128)(2,1)S(1)}, u32[]{:S(2)}, u32[]{:S(2)}) collective-permute-start(bf16[128,640]{1,0:T(8,128)(2,1)S(1)} %get-tuple-element.19.own_ref), channel_id=1, source_target_pairs={{0,64},{64,128},{128,192},{192,0},{1,65},{65,129},{129,193},{193,1... | collective-permute-start | bytes 491528 | tf_op jit(solution)/shard_map/ppermute | solution.py:416
  209.9 5.9 %collective-permute-start.8 = (bf16[128,384]{1,0:T(8,128)(2,1)S(1)}, bf16[128,384]{1,0:T(8,128)(2,1)S(1)}, u32[]{:S(2)}, u32[]{:S(2)}) collective-permute-start(bf16[128,384]{1,0:T(8,128)(2,1)S(1)} %slice.43), channel_id=1, source_target_pairs={{0,192},{64,0},{128,64},{192,128},{1,193},{65,1},{129,65},{193,129... | collective-permute-start | bytes 294920 | tf_op jit(solution)/shard_map/ppermute | solution.py:416
  210.0 5.2 %collective-permute-start.7 = (bf16[128,256]{1,0:T(8,128)(2,1)S(1)}, bf16[128,256]{1,0:T(8,128)(2,1)S(1)}, u32[]{:S(2)}, u32[]{:S(2)}) collective-permute-start(bf16[128,256]{1,0:T(8,128)(2,1)S(1)} %slice.42), channel_id=1, source_target_pairs={{0,64},{64,128},{128,192},{192,0},{1,65},{65,129},{129,193},{193,1... | collective-permute-start | bytes 196616 | tf_op jit(solution)/shard_map/ppermute | solution.py:416
  215.9 3.3 collective-permute-start.9
  227.4 56.9 %all-to-all-start.3 = ((bf16[32,32,1024]{2,1,0:T(8,128)(2,1)}), bf16[32,32,1024]{2,1,0:T(8,128)(2,1)}, u32[]{:S(2)}, u32[]{:S(2)}) async-start(bf16[32,32,1024]{2,1,0:T(8,128)(2,1)} %bitcast.17), calls=%async_computation.3 | async-start | bytes 4194304 | tf_op jit(solution)/shard_map/all_to_all | solution.py:401
  237.6 2.2 collective-permute-start.10
  240.1 8.9 %collective-permute-start.13 = (bf16[128,384]{1,0:T(8,128)(2,1)S(1)}, bf16[128,384]{1,0:T(8,128)(2,1)S(1)}, u32[]{:S(2)}, u32[]{:S(2)}) collective-permute-start(bf16[128,384]{1,0:T(8,128)(2,1)S(1)} %slice.45), channel_id=1, source_target_pairs={{0,192},{64,0},{128,64},{192,128},{1,193},{65,1},{129,65},{193,129... | collective-permute-start | bytes 294920 | tf_op jit(solution)/shard_map/ppermute | solution.py:416
  240.8 4.5 %collective-permute-start.11 = (bf16[128,256]{1,0:T(8,128)(2,1)S(1)}, bf16[128,256]{1,0:T(8,128)(2,1)S(1)}, u32[]{:S(2)}, u32[]{:S(2)}) collective-permute-start(bf16[128,256]{1,0:T(8,128)(2,1)S(1)} %slice.44), channel_id=1, source_target_pairs={{0,64},{64,128},{128,192},{192,0},{1,65},{65,129},{129,193},{193,1... | collective-permute-start | bytes 196616 | tf_op jit(solution)/shard_map/ppermute | solution.py:416
  245.3 6.6 %collective-permute-start.12 = (bf16[128,640]{1,0:T(8,128)(2,1)S(1)}, bf16[128,640]{1,0:T(8,128)(2,1)S(1)}, u32[]{:S(2)}, u32[]{:S(2)}) collective-permute-start(bf16[128,640]{1,0:T(8,128)(2,1)S(1)} %add_half.6), channel_id=1, source_target_pairs={{0,64},{64,128},{128,192},{192,0},{1,65},{65,129},{129,193},{193,1... | collective-permute-start | bytes 491528 | tf_op jit(solution)/shard_map/ppermute | solution.py:416
  249.0 6.6 %collective-permute-start.14 = (bf16[128,640]{1,0:T(8,128)(2,1)S(1)}, bf16[128,640]{1,0:T(8,128)(2,1)S(1)}, u32[]{:S(2)}, u32[]{:S(2)}) collective-permute-start(bf16[128,640]{1,0:T(8,128)(2,1)S(1)} %add_half.7), channel_id=1, source_target_pairs={{0,192},{64,0},{128,64},{192,128},{1,193},{65,1},{129,65},{193,129... | collective-permute-start | bytes 491528 | tf_op jit(solution)/shard_map/ppermute | solution.py:416
  255.8 9.2 %collective-permute-start.16 = (bf16[128,1280]{1,0:T(8,128)(2,1)S(1)}, bf16[128,1280]{1,0:T(8,128)(2,1)S(1)}, u32[]{:S(2)}, u32[]{:S(2)}) collective-permute-start(bf16[128,1280]{1,0:T(8,128)(2,1)S(1)} %backprop.1.own_ref), channel_id=1, source_target_pairs={{0,192},{64,0},{128,64},{192,128},{1,193},{65,1},{129,65},{193,129... | collective-permute-start | bytes 983048 | tf_op jit(solution)/shard_map/ppermute | solution.py:416
  255.9 9.2 %collective-permute-start.15 = (bf16[128,1280]{1,0:T(8,128)(2,1)S(1)}, bf16[128,1280]{1,0:T(8,128)(2,1)S(1)}, u32[]{:S(2)}, u32[]{:S(2)}) collective-permute-start(bf16[128,1280]{1,0:T(8,128)(2,1)S(1)} %backprop.1.own_ref), channel_id=1, source_target_pairs={{0,64},{64,128},{128,192},{192,0},{1,65},{65,129},{129,193},{193,1... | collective-permute-start | bytes 983048 | tf_op jit(solution)/shard_map/ppermute | solution.py:416
  265.0 6.6 %collective-permute-start.18 = (bf16[128,640]{1,0:T(8,128)(2,1)S(1)}, bf16[128,640]{1,0:T(8,128)(2,1)S(1)}, u32[]{:S(2)}, u32[]{:S(2)}) collective-permute-start(bf16[128,640]{1,0:T(8,128)(2,1)S(1)} %slice.47), channel_id=1, source_target_pairs={{0,192},{64,0},{128,64},{192,128},{1,193},{65,1},{129,65},{193,129... | collective-permute-start | bytes 491528 | tf_op jit(solution)/shard_map/ppermute | solution.py:416
  265.2 6.5 %collective-permute-start.17 = (bf16[128,640]{1,0:T(8,128)(2,1)S(1)}, bf16[128,640]{1,0:T(8,128)(2,1)S(1)}, u32[]{:S(2)}, u32[]{:S(2)}) collective-permute-start(bf16[128,640]{1,0:T(8,128)(2,1)S(1)} %slice.46), channel_id=1, source_target_pairs={{0,64},{64,128},{128,192},{192,0},{1,65},{65,129},{129,193},{193,1... | collective-permute-start | bytes 491528 | tf_op jit(solution)/shard_map/ppermute | solution.py:416
  271.7 3.1 collective-permute-start.19
  284.3 57.7 %all-to-all-start.4 = ((bf16[32,32,1024]{2,1,0:T(8,128)(2,1)}), bf16[32,32,1024]{2,1,0:T(8,128)(2,1)}, u32[]{:S(2)}, u32[]{:S(2)}) async-start(bf16[32,32,1024]{2,1,0:T(8,128)(2,1)} %bitcast.55), calls=%async_computation.4 | async-start | bytes 4194304 | tf_op jit(solution)/shard_map/all_to_all | solution.py:401
  291.7 4.4 %copy-start.7 = (bf16[1024,1024]{1,0:T(8,128)(2,1)S(1)}, bf16[1024,1024]{1,0:T(8,128)(2,1)}, u32[]{:S(2)}) copy-start(bf16[1024,1024]{1,0:T(8,128)(2,1)} %copy-done.6) | copy-start | bytes 6291460
  296.1 2.6 copy-start.4
  (10 other events, 11.4 us)

commit v4 on v3

--- a/solution.py
+++ b/solution.py
@@ -117,15 +117,25 @@
     )(ids, a, b)
 
 
-def load_body(experts, cap, pair_cap, route_ref, ids_ref, x_ref, a_ref, b_ref, out_ref):
+def load_body(
+    experts, cap, pair_cap, route_ref, ids_ref, x_ref, a_ref, b_ref, out_ref, token_at, row_at
+):
     per = out_ref.shape[0]
     first = pl.program_id(0) * per
-    places = token_places(route_ref, experts, cap)
+    pairs = 2 * pair_cap
+
+    @pl.when(pl.program_id(0) == 0)
+    def _():
+        for k, place in enumerate(token_places(route_ref, experts, cap)):
+            token_at[k : k + 1, :] = place
+        ids = ids_ref[...]
+        row_at[0:1, :] = ids * pairs + ranks([ids], experts)[0]
+
+    places = [token_at[k : k + 1, :] for k in (0, 1)]
     slot = iota((per * cap, x_ref.shape[0]), 0) + first * cap
     pick = jnp.where((slot == places[0]) | (slot == places[1]), 1.0, 0.0).astype(BF16)
     tokens = jnp.dot(pick, x_ref[...], preferred_element_type=F32)
-    ids, pairs = ids_ref[...], 2 * pair_cap
-    place = ids * pairs + ranks([ids], experts)[0]
+    place = row_at[0:1, :]
     slot = iota((per * pairs, a_ref.shape[0]), 0) + first * pairs
     pick_a = jnp.where(slot == place, 1.0, 0.0).astype(BF16)
     pick_b = jnp.where(slot == place + pair_cap, 1.0, 0.0).astype(BF16)
@@ -148,6 +158,10 @@
         in_specs=[pl.BlockSpec(v.shape, whole) for v in (route, ids, x, a, b)],
         out_specs=pl.BlockSpec((per, cap + 2 * pair_cap, width), lambda i: (i, 0, 0)),
         out_shape=jax.ShapeDtypeStruct((experts, cap + 2 * pair_cap, width), BF16),
+        scratch_shapes=[
+            pltpu.VMEM((8, x.shape[0]), jnp.int32),
+            pltpu.VMEM((8, a.shape[0]), jnp.int32),
+        ],
     )(route, ids, x, a, b)
 
 
@@ -360,39 +374,46 @@
 
 
 def combine_body(scaled, experts, cap, *refs):
-    route_ref, rows_ref, out_ref = refs[0], refs[-2], refs[-1]
+    terms = 2 if scaled else 1
+    route_ref, rows_ref, out_ref = refs[0], refs[terms], refs[terms + 1]
+    picks = refs[terms + 2 :]
     count, total = out_ref.shape[0], rows_ref.shape[0]
-    places = [column_of(place) for place in token_places(route_ref, experts, cap)]
-    slot = iota((count, total), 1)
-    hits = [slot == place for place in places]
+
+    @pl.when(pl.program_id(0) == 0)
+    def _():
+        places = [column_of(place) for place in token_places(route_ref, experts, cap)]
+        slot = iota((count, total), 1)
+        hits = [slot == place for place in places]
+        if scaled:
+            shares = [column_of(share) for share in token_shares(refs[1])]
+            weight = jnp.where(hits[0], shares[0], 0.0) + jnp.where(hits[1], shares[1], 0.0)
+            high = weight.astype(BF16)
+            picks[0][...] = high
+            picks[1][...] = (weight - high.astype(F32)).astype(BF16)
+        else:
+            picks[0][...] = jnp.where(hits[0] | hits[1], 1.0, 0.0).astype(BF16)
+
     rows = rows_ref[...]
-    if scaled:
-        shares = [column_of(share) for share in token_shares(refs[1])]
-        weight = jnp.where(hits[0], shares[0], 0.0) + jnp.where(hits[1], shares[1], 0.0)
-        high = weight.astype(BF16)
-        low = (weight - high.astype(F32)).astype(BF16)
-        total_rows = jnp.dot(high, rows, preferred_element_type=F32) + jnp.dot(
-            low, rows, preferred_element_type=F32
-        )
-    else:
-        pick = jnp.where(hits[0] | hits[1], 1.0, 0.0).astype(BF16)
-        total_rows = jnp.dot(pick, rows, preferred_element_type=F32)
-    out_ref[...] = total_rows.astype(BF16)
+    out_ref[...] = sum(
+        jnp.dot(pick[...], rows, preferred_element_type=F32) for pick in picks
+    ).astype(BF16)
 
 
 def combine(route, score, rows, experts, cap, scaled):
     count = route.shape[1]
     total, width = rows.shape
-    block = 512
+    block = 256
     whole = lambda i: (0, 0)
+    terms = 2 if scaled else 1
     return kernel_call(
         functools.partial(combine_body, scaled, experts, cap),
         "combine",
         grid=(width // block,),
-        in_specs=[pl.BlockSpec((2, count), whole)] * (2 if scaled else 1)
+        in_specs=[pl.BlockSpec((2, count), whole)] * terms
         + [pl.BlockSpec((total, block), lambda i: (0, i))],
         out_specs=pl.BlockSpec((count, block), lambda i: (0, i)),
         out_shape=jax.ShapeDtypeStruct((count, width), BF16),
+        scratch_shapes=[pltpu.VMEM((count, total), BF16)] * terms,
     )(*((route, score) if scaled else (route,)), rows)
 
 
@@ -424,7 +445,7 @@
     return lax.dynamic_update_slice(value, part[None, None], (y, core, 0, 0))
 
 
-def scatter_sum(value):
+def scatter_start(value):
     rows, n = value.shape
     ys, cores = lax.axis_size("y"), lax.axis_size("core")
     y, core = lax.axis_index("y"), lax.axis_index("core")
@@ -437,7 +458,11 @@
     high = shift(far[:, half:], "y", -1)
     to_above = add_half(pick(pair, (y + 1) % ys, 0), low, 0)
     to_below = add_half(pick(pair, (y + ys - 1) % ys, 0), high, half)
-    return pick(pair, y, 0), shift(to_above, "y", 1), shift(to_below, "y", -1)
+    return pick(pair, y, 0), to_above, to_below
+
+
+def scatter_end(own, to_above, to_below):
+    return own, shift(to_above, "y", 1), shift(to_below, "y", -1)
 
 
 def gather_blocks(part):
@@ -477,19 +502,20 @@
     sent = load(route, ids, tokens, w_gate, w_up, experts, tok_cap, pair_cap)
     raw = lax.all_to_all(sent, EXPERT, split_axis=0, concat_axis=0, tiled=True)
     packed_down = pack(ids, w_down, w_down, experts, pair_cap, width // 2, (0, 1))
-    raw_down = exchange(after(packed_down, raw), experts)
+    sent_grads = dispatch(route, score, cotangent, experts, tok_cap, True)
+    raw_down = exchange(after(packed_down, (raw, sent_grads)), experts)
     rows_x, gate_up_rows = unload(raw, tok_cap, pair_cap)
-    part = product(rows_x, gate_up_rows, True)
-    sent_grads = dispatch(route, score, cotangent, experts, tok_cap, True)
-    rows_dy = exchange(after(sent_grads, (raw_down, part)), experts)
-    hidden, sums = hidden_of(scatter_sum(part))
+    steps = scatter_start(product(rows_x, gate_up_rows, True))
+    rows_dy = exchange(after(sent_grads, (raw_down, steps)), experts)
+    terms = scatter_end(*steps)
+    hidden, sums = hidden_of(terms)
     hidden = gather_blocks(hidden)
     down_rows = unpack_one(raw_down, pair_cap)
     out_part = product(hidden, down_rows, False)
     out_part, rows_dy = lax.optimization_barrier((out_part, rows_dy))
     back_out = exchange(out_part, experts)
 
-    back = scatter_sum(product(rows_dy, down_rows, True))
+    back = scatter_end(*scatter_start(product(rows_dy, down_rows, True)))
     d_both = gather_blocks(backprop_of(back, sums))
     input_part = product(d_both, gate_up_rows, False)
     back_in = exchange(after(input_part, back_out), experts)

time: 349 us -> 344 us (0.986)
    unnamed x34 -> x42, local copies, waits for them, and re-layouts: 11.4 us -> 10.9 us
  transfers between devices with their start and end apart: 25 -> 25, of which waited for: 19 -> 19; matrix products, arithmetic and copies ran while one was open for 4% -> 3% of each run, Pallas kernels for 11% -> 11%
where the time goes in v4:
time: 344 us; the launch traced here: 343 us
  waiting for transfers between devices  204 us (59%)
  starting transfers between devices  66.3 us (19%)
  Pallas kernels  49.6 us (14%)
  local copies, waits for them, and re-layouts  12.3 us (4%)
  matrix products  9.62 us (3%)
    all_to_all x1, waiting for transfers between devices, body(): raw = lax.all_to_all(sent, EXPERT, split_axis=0, concat_axis=0, tiled=True)  98.1 us
    all_to_all x4, waiting for transfers between devices, exchange(): lax.all_to_all(rows.reshape(parts, total // parts, width), EXPERT, split_...  61.8 us
    ppermute x20, waiting for transfers between devices, shift(): lax.ppermute(value, axis, [(i, (i + step) % size) for i in range(size)])  44.4 us
    all_to_all x4, starting transfers between devices, exchange(): lax.all_to_all(rows.reshape(parts, total // parts, width), EXPERT, split_...  29.8 us
    ppermute x20, starting transfers between devices, shift(): lax.ppermute(value, axis, [(i, (i + step) % size) for i in range(size)])  25 us
    pallas_call x4, Pallas kernels, product(): kernel_call(functools.partial(product_body, dims), 'product', grid=(rows...  16.2 us
    all_to_all x1, starting transfers between devices, body(): raw = lax.all_to_all(sent, EXPERT, split_axis=0, concat_axis=0, tiled=True)  11.6 us
    unnamed x42, local copies, waits for them, and re-layouts  10.9 us
  transfers between devices with their start and end apart: 25, of which 19 were waited for; matrix products, arithmetic and copies ran while one was open for 3% of the time, Pallas kernels for 11%

profile of v4, /device:TPU:24, one launch (start us, length us, event | category | flops | bytes accessed | tf_op | source)
XLA Modules:
  0.0 343.3 jit_solution(11287204698351439011)
XLA Ops:
  5.4 6.5 %load.1 = bf16[32,72,1024]{2,1,0:T(8,128)(2,1)} custom-call(s32[2,256]{1,0:T(2,128)S(1)} %bitcast.63, s32[1,448]{1,0:T(1,128)S(1)} %bitcast.69, bf16[256,1024]{1,0:T(8,128)(2,1)S(1)} %copy-done.14, bf16[448,1024]{1,0:T(8,128)(2,1)S(1)} %copy-done.10, bf16[448,1024]{1,0:T(8,128)(2,1)S(1)} %copy-done.11), custom_call_target="tpu_custom_call" | custom-call | tf_op jit(solution)/shard_map/load/pallas_call | solution.py:154
  11.9 11.6 %all-to-all-start = ((bf16[32,72,1024]{2,1,0:T(8,128)(2,1)}), bf16[32,72,1024]{2,1,0:T(8,128)(2,1)}, u32[]{:S(2)}, u32[]{:S(2)}) async-start(bf16[32,72,1024]{2,1,0:T(8,128)(2,1)} %load.1), calls=%async_computation | async-start | bytes 9437184 | tf_op jit(solution)/shard_map/all_to_all | solution.py:503
  23.6 4.0 %pack.1 = bf16[1280,512]{1,0:T(8,128)(2,1)} custom-call(s32[1,448]{1,0:T(1,128)S(1)} %bitcast.70, bf16[448,1024]{1,0:T(8,128)(2,1)S(1)} %copy-done.7, bf16[448,1024]{1,0:T(8,128)(2,1)S(1)} %copy-done.7), custom_call_target="tpu_custom_call" | custom-call | tf_op jit(solution)/shard_map/pack/pallas_call | solution.py:106
  27.6 3.1 dispatch.1
  30.7 98.1 %all-to-all-done.raw_ref = bf16[32,72,1024]{2,1,0:T(8,128)(2,1)} async-done(((bf16[32,72,1024]{2,1,0:T(8,128)(2,1)}), bf16[32,72,1024]{2,1,0:T(8,128)(2,1)}, u32[]{:S(2)}, u32[]{:S(2)}) %all-to-all-start) | async-done | bytes 4718624 | tf_op jit(solution)/shard_map/all_to_all | solution.py:503
  128.7 8.9 %all-to-all-start.1 = ((bf16[32,40,512]{2,1,0:T(8,128)(2,1)}), bf16[32,40,512]{2,1,0:T(8,128)(2,1)}, u32[]{:S(2)}, u32[]{:S(2)}) async-start(bf16[32,40,512]{2,1,0:T(8,128)(2,1)} %bitcast.13), calls=%async_computation.1 | async-start | bytes 2621440 | tf_op jit(solution)/shard_map/all_to_all | solution.py:422
  137.7 4.4 %unload.1 = (bf16[1024,1024]{1,0:T(8,128)(2,1)S(1)}, bf16[2,640,1024]{2,1,0:T(8,128)(2,1)S(1)}) custom-call(bf16[32,72,1024]{2,1,0:T(8,128)(2,1)} %all-to-all-done.raw_ref), custom_call_target="tpu_custom_call" | custom-call | tf_op jit(solution)/shard_map/unload/pallas_call | solution.py:183
  143.6 6.0 %product.4 = bf16[1024,1280]{1,0:T(8,128)(2,1)S(1)} custom-call(bf16[1024,1024]{1,0:T(8,128)(2,1)S(1)} %get-tuple-element.17.a_ref, bf16[1280,1024]{1,0:T(8,128)(2,1)} %bitcast.50), custom_call_target="tpu_custom_call" | custom-call | tf_op jit(solution)/shard_map/product/pallas_call | solution.py:356
  150.8 3.4 collective-permute-done.other_ref
  159.3 4.2 %collective-permute-done.3.half_ref = bf16[128,640]{1,0:T(8,128)(2,1)S(1)} collective-permute-done((bf16[128,640]{1,0:T(8,128)(2,1)S(1)}, bf16[128,640]{1,0:T(8,128)(2,1)S(1)}, u32[]{:S(2)}, u32[]{:S(2)}) %collective-permute-start.3) | collective-permute-done | bytes 163872 | tf_op jit(solution)/shard_map/ppermute | solution.py:437
  163.7 7.3 %all-to-all-done.1 = bf16[32,40,512]{2,1,0:T(8,128)(2,1)} async-done(((bf16[32,40,512]{2,1,0:T(8,128)(2,1)}), bf16[32,40,512]{2,1,0:T(8,128)(2,1)}, u32[]{:S(2)}, u32[]{:S(2)}) %all-to-all-start.1) | async-done | bytes 1310752 | tf_op jit(solution)/shard_map/all_to_all | solution.py:422
  171.0 5.7 %all-to-all-start.2 = ((bf16[32,32,1024]{2,1,0:T(8,128)(2,1)}), bf16[32,32,1024]{2,1,0:T(8,128)(2,1)S(1)}, u32[]{:S(2)}, u32[]{:S(2)}) async-start(bf16[32,32,1024]{2,1,0:T(8,128)(2,1)} %bitcast.15), calls=%async_computation.2 | async-start | bytes 4194304 | tf_op jit(solution)/shard_map/all_to_all | solution.py:422
  180.0 5.8 %collective-permute-done.4.above_ref = bf16[128,1280]{1,0:T(8,128)(2,1)S(1)} collective-permute-done((bf16[128,1280]{1,0:T(8,128)(2,1)S(1)}, bf16[128,1280]{1,0:T(8,128)(2,1)S(1)}, u32[]{:S(2)}, u32[]{:S(2)}) %collective-permute-start.4) | collective-permute-done | bytes 327712 | tf_op jit(solution)/shard_map/ppermute | solution.py:437
  186.8 3.2 collective-permute-start.5
  190.1 3.3 collective-permute-done.6.above_ref
  193.5 3.3 collective-permute-start.7
  199.6 3.0 unpack_one.1.b_ref
  207.5 18.0 %all-to-all-done.2 = bf16[32,32,1024]{2,1,0:T(8,128)(2,1)S(1)} async-done(((bf16[32,32,1024]{2,1,0:T(8,128)(2,1)}), bf16[32,32,1024]{2,1,0:T(8,128)(2,1)S(1)}, u32[]{:S(2)}, u32[]{:S(2)}) %all-to-all-start.2) | async-done | bytes 2097184 | tf_op jit(solution)/shard_map/all_to_all | solution.py:422
  225.5 6.1 %all-to-all-start.3 = ((bf16[32,32,1024]{2,1,0:T(8,128)(2,1)}), bf16[32,32,1024]{2,1,0:T(8,128)(2,1)}, u32[]{:S(2)}, u32[]{:S(2)}) async-start(bf16[32,32,1024]{2,1,0:T(8,128)(2,1)} %bitcast.58), calls=%async_computation.3 | async-start | bytes 4194304 | tf_op jit(solution)/shard_map/all_to_all | solution.py:422
  241.9 3.6 %collective-permute-start.12 = (bf16[128,640]{1,0:T(8,128)(2,1)S(1)}, bf16[128,640]{1,0:T(8,128)(2,1)S(1)}, u32[]{:S(2)}, u32[]{:S(2)}) collective-permute-start(bf16[128,640]{1,0:T(8,128)(2,1)S(1)} %add_half.6), channel_id=1, source_target_pairs={{0,64},{64,128},{128,192},{192,0},{1,65},{65,129},{129,193},{193,1... | collective-permute-start | bytes 491528 | tf_op jit(solution)/shard_map/ppermute | solution.py:437
  245.7 2.7 collective-permute-done.12.below_ref
  248.4 3.8 %collective-permute-done.14.above_ref = bf16[128,640]{1,0:T(8,128)(2,1)S(1)} collective-permute-done((bf16[128,640]{1,0:T(8,128)(2,1)S(1)}, bf16[128,640]{1,0:T(8,128)(2,1)S(1)}, u32[]{:S(2)}, u32[]{:S(2)}) %collective-permute-start.14) | collective-permute-done | bytes 163872 | tf_op jit(solution)/shard_map/ppermute | solution.py:437
  254.5 5.7 %collective-permute-done.15.below_ref = bf16[128,1280]{1,0:T(8,128)(2,1)S(1)} collective-permute-done((bf16[128,1280]{1,0:T(8,128)(2,1)S(1)}, bf16[128,1280]{1,0:T(8,128)(2,1)S(1)}, u32[]{:S(2)}, u32[]{:S(2)}) %collective-permute-start.15) | collective-permute-done | bytes 327712 | tf_op jit(solution)/shard_map/ppermute | solution.py:437
  262.4 3.2 collective-permute-done.17.low_ref
  265.6 2.8 collective-permute-done.18.high_ref
  268.6 3.0 collective-permute-done.19.other_ref
  271.8 5.3 %product.7 = bf16[1024,1024]{1,0:T(8,128)(2,1)S(1)} custom-call(bf16[1024,1280]{1,0:T(8,128)(2,1)S(1)} %bitcast.52, bf16[1280,1024]{1,0:T(8,128)(2,1)} %bitcast.51), custom_call_target="tpu_custom_call" | custom-call | tf_op jit(solution)/shard_map/product/pallas_call | solution.py:356
  279.4 9.1 %all-to-all-start.4 = ((bf16[32,32,1024]{2,1,0:T(8,128)(2,1)}), bf16[32,32,1024]{2,1,0:T(8,128)(2,1)}, u32[]{:S(2)}, u32[]{:S(2)}) async-start(bf16[32,32,1024]{2,1,0:T(8,128)(2,1)} %bitcast.55), calls=%async_computation.4 | async-start | bytes 4194304 | tf_op jit(solution)/shard_map/all_to_all | solution.py:422
  288.5 4.4 %fusion.1 = bf16[1,640,1024]{2,1,0:T(8,128)(2,1)} fusion(bf16[1024,1024]{1,0:T(8,128)(2,1)} %copy-done.8, bf16[1024,1280]{1,0:T(8,128)(2,1)S(1)} %bitcast.53), kind=kOutput, calls=%fused_computation.4 | convolution fusion | flops 1342832640 | bytes 4718592 | tf_op jit(solution)/shard_map/dot_general | solution.py:528
  298.1 5.0 %combine.2 = bf16[256,1024]{1,0:T(8,128)(2,1)} custom-call(s32[2,256]{1,0:T(2,128)S(1)} %bitcast.65, s32[2,256]{1,0:T(2,128)S(1)} %bitcast.68, bf16[1024,1024]{1,0:T(8,128)(2,1)} %bitcast.18.refs_2_), custom_call_target="tpu_custom_call" | custom-call | tf_op jit(solution)/shard_map/combine/pallas_call | solution.py:408
  303.2 35.6 %all-to-all-done.4 = bf16[32,32,1024]{2,1,0:T(8,128)(2,1)} async-done(((bf16[32,32,1024]{2,1,0:T(8,128)(2,1)}), bf16[32,32,1024]{2,1,0:T(8,128)(2,1)}, u32[]{:S(2)}, u32[]{:S(2)}) %all-to-all-start.4) | async-done | bytes 2097184 | tf_op jit(solution)/shard_map/all_to_all | solution.py:422
  338.7 4.5 %combine.3 = bf16[256,1024]{1,0:T(8,128)(2,1)} custom-call(s32[2,256]{1,0:T(2,128)S(1)} %bitcast.66, bf16[1024,1024]{1,0:T(8,128)(2,1)} %bitcast.27.refs_1_), custom_call_target="tpu_custom_call" | custom-call | tf_op jit(solution)/shard_map/combine/pallas_call | solution.py:408
  (97 shorter events, 47.6 us)
Async XLA Ops:
  11.9 11.6 %copy-start.7 = (bf16[448,1024]{1,0:T(8,128)(2,1)S(1)}, bf16[448,1024]{1,0:T(8,128)(2,1)}, u32[]{:S(2)}) copy-start(bf16[448,1024]{1,0:T(8,128)(2,1)} %b_ref.3) | copy-start | bytes 2752516
  11.9 11.6 %copy-start.20 = (s32[448,1]{0,1:T(1,128)S(1)}, s32[448,1]{0,1:T(1,128)}, u32[]{:S(2)}) copy-start(s32[448,1]{0,1:T(1,128)} %param.12) | copy-start | bytes 5380
  11.9 116.8 %all-to-all-start = ((bf16[32,72,1024]{2,1,0:T(8,128)(2,1)}), bf16[32,72,1024]{2,1,0:T(8,128)(2,1)}, u32[]{:S(2)}, u32[]{:S(2)}) async-start(bf16[32,72,1024]{2,1,0:T(8,128)(2,1)} %load.1), calls=%async_computation | async-start | bytes 9437184 | tf_op jit(solution)/shard_map/all_to_all | solution.py:503
  23.5 4.1 %copy-start.15 = (bf16[256,1024]{1,0:T(8,128)(2,1)S(1)}, bf16[256,1024]{1,0:T(8,128)(2,1)}, u32[]{:S(2)}) copy-start(bf16[256,1024]{1,0:T(8,128)(2,1)} %refs_2_.1) | copy-start | bytes 1572868
  128.7 42.2 %all-to-all-start.1 = ((bf16[32,40,512]{2,1,0:T(8,128)(2,1)}), bf16[32,40,512]{2,1,0:T(8,128)(2,1)}, u32[]{:S(2)}, u32[]{:S(2)}) async-start(bf16[32,40,512]{2,1,0:T(8,128)(2,1)} %bitcast.13), calls=%async_computation.1 | async-start | bytes 2621440 | tf_op jit(solution)/shard_map/all_to_all | solution.py:422
  143.6 6.0 %copy-start.8 = (bf16[1024,1024]{1,0:T(8,128)(2,1)}, bf16[1024,1024]{1,0:T(8,128)(2,1)S(1)}, u32[]{:S(2)}) copy-start(bf16[1024,1024]{1,0:T(8,128)(2,1)S(1)} %get-tuple-element.17.a_ref) | copy-start | bytes 6291460
  150.8 3.4 collective-permute-start
  156.0 7.5 %collective-permute-start.3 = (bf16[128,640]{1,0:T(8,128)(2,1)S(1)}, bf16[128,640]{1,0:T(8,128)(2,1)S(1)}, u32[]{:S(2)}, u32[]{:S(2)}) collective-permute-start(bf16[128,640]{1,0:T(8,128)(2,1)S(1)} %get-tuple-element.37), channel_id=1, source_target_pairs={{0,192},{64,0},{128,64},{192,128},{1,193},{65,1},{129,65},{193,129... | collective-permute-start | bytes 491528 | tf_op jit(solution)/shard_map/ppermute | solution.py:437
  156.9 6.8 %collective-permute-start.1 = (bf16[128,640]{1,0:T(8,128)(2,1)S(1)}, bf16[128,640]{1,0:T(8,128)(2,1)S(1)}, u32[]{:S(2)}, u32[]{:S(2)}) collective-permute-start(bf16[128,640]{1,0:T(8,128)(2,1)S(1)} %get-tuple-element.38), channel_id=1, source_target_pairs={{0,64},{64,128},{128,192},{192,0},{1,65},{65,129},{129,193},{193,1... | collective-permute-start | bytes 491528 | tf_op jit(solution)/shard_map/ppermute | solution.py:437
  171.0 54.5 %all-to-all-start.2 = ((bf16[32,32,1024]{2,1,0:T(8,128)(2,1)}), bf16[32,32,1024]{2,1,0:T(8,128)(2,1)S(1)}, u32[]{:S(2)}, u32[]{:S(2)}) async-start(bf16[32,32,1024]{2,1,0:T(8,128)(2,1)} %bitcast.15), calls=%async_computation.2 | async-start | bytes 4194304 | tf_op jit(solution)/shard_map/all_to_all | solution.py:422
  176.7 9.2 %collective-permute-start.4 = (bf16[128,1280]{1,0:T(8,128)(2,1)S(1)}, bf16[128,1280]{1,0:T(8,128)(2,1)S(1)}, u32[]{:S(2)}, u32[]{:S(2)}) collective-permute-start(bf16[128,1280]{1,0:T(8,128)(2,1)S(1)} %add_half.5), channel_id=1, source_target_pairs={{0,192},{64,0},{128,64},{192,128},{1,193},{65,1},{129,65},{193,129... | collective-permute-start | bytes 983048 | tf_op jit(solution)/shard_map/ppermute | solution.py:437
  177.5 8.3 %collective-permute-start.2 = (bf16[128,1280]{1,0:T(8,128)(2,1)S(1)}, bf16[128,1280]{1,0:T(8,128)(2,1)S(1)}, u32[]{:S(2)}, u32[]{:S(2)}) collective-permute-start(bf16[128,1280]{1,0:T(8,128)(2,1)S(1)} %add_half.4), channel_id=1, source_target_pairs={{0,64},{64,128},{128,192},{192,0},{1,65},{65,129},{129,193},{193,1... | collective-permute-start | bytes 983048 | tf_op jit(solution)/shard_map/ppermute | solution.py:437
  186.8 6.5 %collective-permute-start.6 = (bf16[128,640]{1,0:T(8,128)(2,1)S(1)}, bf16[128,640]{1,0:T(8,128)(2,1)S(1)}, u32[]{:S(2)}, u32[]{:S(2)}) collective-permute-start(bf16[128,640]{1,0:T(8,128)(2,1)S(1)} %get-tuple-element.19.own_ref), channel_id=1, source_target_pairs={{0,192},{64,0},{128,64},{192,128},{1,193},{65,1},{129,65},{193,129... | collective-permute-start | bytes 491528 | tf_op jit(solution)/shard_map/ppermute | solution.py:437
  186.8 6.6 %collective-permute-start.5 = (bf16[128,640]{1,0:T(8,128)(2,1)S(1)}, bf16[128,640]{1,0:T(8,128)(2,1)S(1)}, u32[]{:S(2)}, u32[]{:S(2)}) collective-permute-start(bf16[128,640]{1,0:T(8,128)(2,1)S(1)} %get-tuple-element.19.own_ref), channel_id=1, source_target_pairs={{0,64},{64,128},{128,192},{192,0},{1,65},{65,129},{129,193},{193,1... | collective-permute-start | bytes 491528 | tf_op jit(solution)/shard_map/ppermute | solution.py:437
  193.4 5.9 %collective-permute-start.8 = (bf16[128,384]{1,0:T(8,128)(2,1)S(1)}, bf16[128,384]{1,0:T(8,128)(2,1)S(1)}, u32[]{:S(2)}, u32[]{:S(2)}) collective-permute-start(bf16[128,384]{1,0:T(8,128)(2,1)S(1)} %slice.43), channel_id=1, source_target_pairs={{0,192},{64,0},{128,64},{192,128},{1,193},{65,1},{129,65},{193,129... | collective-permute-start | bytes 294920 | tf_op jit(solution)/shard_map/ppermute | solution.py:437
  193.5 5.2 %collective-permute-start.7 = (bf16[128,256]{1,0:T(8,128)(2,1)S(1)}, bf16[128,256]{1,0:T(8,128)(2,1)S(1)}, u32[]{:S(2)}, u32[]{:S(2)}) collective-permute-start(bf16[128,256]{1,0:T(8,128)(2,1)S(1)} %slice.42), channel_id=1, source_target_pairs={{0,64},{64,128},{128,192},{192,0},{1,65},{65,129},{129,193},{193,1... | collective-permute-start | bytes 196616 | tf_op jit(solution)/shard_map/ppermute | solution.py:437
  199.3 3.3 collective-permute-start.9
  225.5 6.1 %copy-start.2 = (bf16[32,32,1024]{2,1,0:T(8,128)(2,1)}, bf16[32,32,1024]{2,1,0:T(8,128)(2,1)S(1)}, u32[]{:S(2)}) copy-start(bf16[32,32,1024]{2,1,0:T(8,128)(2,1)S(1)} %all-to-all-done.2) | copy-start | bytes 6291460
  225.5 53.9 %all-to-all-start.3 = ((bf16[32,32,1024]{2,1,0:T(8,128)(2,1)}), bf16[32,32,1024]{2,1,0:T(8,128)(2,1)}, u32[]{:S(2)}, u32[]{:S(2)}) async-start(bf16[32,32,1024]{2,1,0:T(8,128)(2,1)} %bitcast.58), calls=%async_computation.3 | async-start | bytes 4194304 | tf_op jit(solution)/shard_map/all_to_all | solution.py:422
  234.2 18.0 %copy-start.13 = (f32[128,1280]{1,0:T(8,128)S(1)}, f32[128,1280]{1,0:T(8,128)}, u32[]{:S(2)}) copy-start(f32[128,1280]{1,0:T(8,128)} %copy-done.12) | copy-start | bytes 1966084
  234.2 2.2 collective-permute-start.10
  236.6 8.9 %collective-permute-start.13 = (bf16[128,384]{1,0:T(8,128)(2,1)S(1)}, bf16[128,384]{1,0:T(8,128)(2,1)S(1)}, u32[]{:S(2)}, u32[]{:S(2)}) collective-permute-start(bf16[128,384]{1,0:T(8,128)(2,1)S(1)} %slice.45), channel_id=1, source_target_pairs={{0,192},{64,0},{128,64},{192,128},{1,193},{65,1},{129,65},{193,129... | collective-permute-start | bytes 294920 | tf_op jit(solution)/shard_map/ppermute | solution.py:437
  237.5 4.4 %collective-permute-start.11 = (bf16[128,256]{1,0:T(8,128)(2,1)S(1)}, bf16[128,256]{1,0:T(8,128)(2,1)S(1)}, u32[]{:S(2)}, u32[]{:S(2)}) collective-permute-start(bf16[128,256]{1,0:T(8,128)(2,1)S(1)} %slice.44), channel_id=1, source_target_pairs={{0,64},{64,128},{128,192},{192,0},{1,65},{65,129},{129,193},{193,1... | collective-permute-start | bytes 196616 | tf_op jit(solution)/shard_map/ppermute | solution.py:437
  241.9 6.5 %collective-permute-start.12 = (bf16[128,640]{1,0:T(8,128)(2,1)S(1)}, bf16[128,640]{1,0:T(8,128)(2,1)S(1)}, u32[]{:S(2)}, u32[]{:S(2)}) collective-permute-start(bf16[128,640]{1,0:T(8,128)(2,1)S(1)} %add_half.6), channel_id=1, source_target_pairs={{0,64},{64,128},{128,192},{192,0},{1,65},{65,129},{129,193},{193,1... | collective-permute-start | bytes 491528 | tf_op jit(solution)/shard_map/ppermute | solution.py:437
  245.6 6.6 %collective-permute-start.14 = (bf16[128,640]{1,0:T(8,128)(2,1)S(1)}, bf16[128,640]{1,0:T(8,128)(2,1)S(1)}, u32[]{:S(2)}, u32[]{:S(2)}) collective-permute-start(bf16[128,640]{1,0:T(8,128)(2,1)S(1)} %add_half.7), channel_id=1, source_target_pairs={{0,192},{64,0},{128,64},{192,128},{1,193},{65,1},{129,65},{193,129... | collective-permute-start | bytes 491528 | tf_op jit(solution)/shard_map/ppermute | solution.py:437
  252.4 7.8 %collective-permute-start.15 = (bf16[128,1280]{1,0:T(8,128)(2,1)S(1)}, bf16[128,1280]{1,0:T(8,128)(2,1)S(1)}, u32[]{:S(2)}, u32[]{:S(2)}) collective-permute-start(bf16[128,1280]{1,0:T(8,128)(2,1)S(1)} %backprop.1.own_ref), channel_id=1, source_target_pairs={{0,64},{64,128},{128,192},{192,0},{1,65},{65,129},{129,193},{193,1... | collective-permute-start | bytes 983048 | tf_op jit(solution)/shard_map/ppermute | solution.py:437
  252.5 9.3 %collective-permute-start.16 = (bf16[128,1280]{1,0:T(8,128)(2,1)S(1)}, bf16[128,1280]{1,0:T(8,128)(2,1)S(1)}, u32[]{:S(2)}, u32[]{:S(2)}) collective-permute-start(bf16[128,1280]{1,0:T(8,128)(2,1)S(1)} %backprop.1.own_ref), channel_id=1, source_target_pairs={{0,192},{64,0},{128,64},{192,128},{1,193},{65,1},{129,65},{193,129... | collective-permute-start | bytes 983048 | tf_op jit(solution)/shard_map/ppermute | solution.py:437
  260.2 5.4 %collective-permute-start.17 = (bf16[128,640]{1,0:T(8,128)(2,1)S(1)}, bf16[128,640]{1,0:T(8,128)(2,1)S(1)}, u32[]{:S(2)}, u32[]{:S(2)}) collective-permute-start(bf16[128,640]{1,0:T(8,128)(2,1)S(1)} %slice.46), channel_id=1, source_target_pairs={{0,64},{64,128},{128,192},{192,0},{1,65},{65,129},{129,193},{193,1... | collective-permute-start | bytes 491528 | tf_op jit(solution)/shard_map/ppermute | solution.py:437
  261.8 6.6 %collective-permute-start.18 = (bf16[128,640]{1,0:T(8,128)(2,1)S(1)}, bf16[128,640]{1,0:T(8,128)(2,1)S(1)}, u32[]{:S(2)}, u32[]{:S(2)}) collective-permute-start(bf16[128,640]{1,0:T(8,128)(2,1)S(1)} %slice.47), channel_id=1, source_target_pairs={{0,192},{64,0},{128,64},{192,128},{1,193},{65,1},{129,65},{193,129... | collective-permute-start | bytes 491528 | tf_op jit(solution)/shard_map/ppermute | solution.py:437
  268.5 3.1 collective-permute-start.19
  279.4 59.3 %all-to-all-start.4 = ((bf16[32,32,1024]{2,1,0:T(8,128)(2,1)}), bf16[32,32,1024]{2,1,0:T(8,128)(2,1)}, u32[]{:S(2)}, u32[]{:S(2)}) async-start(bf16[32,32,1024]{2,1,0:T(8,128)(2,1)} %bitcast.55), calls=%async_computation.4 | async-start | bytes 4194304 | tf_op jit(solution)/shard_map/all_to_all | solution.py:422
  288.5 4.4 %copy-start.9 = (bf16[1024,1024]{1,0:T(8,128)(2,1)S(1)}, bf16[1024,1024]{1,0:T(8,128)(2,1)}, u32[]{:S(2)}) copy-start(bf16[1024,1024]{1,0:T(8,128)(2,1)} %copy-done.8) | copy-start | bytes 6291460
  (14 other events, 24.3 us)

commit v5 on v4

--- a/solution.py
+++ b/solution.py
@@ -14,6 +14,7 @@
 BF16 = jnp.bfloat16
 F32 = jnp.float32
 LIMIT = 48 * 1024 * 1024
+MOST = 63 * 1024 * 1024
 FREE = pl.CostEstimate(flops=0, bytes_accessed=0, transcendentals=0)
 
 
@@ -21,11 +22,11 @@
     return lax.broadcasted_iota(jnp.int32, shape, axis)
 
 
-def kernel_call(body, name, **kwargs):
+def kernel_call(body, name, limit=LIMIT, **kwargs):
     return pl.pallas_call(
         body,
         name=name,
-        compiler_params=pltpu.CompilerParams(vmem_limit_bytes=LIMIT),
+        compiler_params=pltpu.CompilerParams(vmem_limit_bytes=limit),
         **kwargs,
     )
 
@@ -117,20 +118,29 @@
     )(ids, a, b)
 
 
-def load_body(
-    experts, cap, pair_cap, route_ref, ids_ref, x_ref, a_ref, b_ref, out_ref, token_at, row_at
-):
+def load_body(experts, cap, pair_cap, route_ref, ids_ref, *refs):
+    held_in, out_ref, token_at, row_at = refs[:3], refs[3], refs[4], refs[5]
+    held, sems = refs[6:9], refs[9]
     per = out_ref.shape[0]
     first = pl.program_id(0) * per
     pairs = 2 * pair_cap
 
     @pl.when(pl.program_id(0) == 0)
     def _():
+        copies = [
+            pltpu.make_async_copy(source, target, sems.at[k])
+            for k, (source, target) in enumerate(zip(held_in, held))
+        ]
+        for copy in copies:
+            copy.start()
         for k, place in enumerate(token_places(route_ref, experts, cap)):
             token_at[k : k + 1, :] = place
         ids = ids_ref[...]
         row_at[0:1, :] = ids * pairs + ranks([ids], experts)[0]
-
+        for copy in copies:
+            copy.wait()
+
+    x_ref, a_ref, b_ref = held
     places = [token_at[k : k + 1, :] for k in (0, 1)]
     slot = iota((per * cap, x_ref.shape[0]), 0) + first * cap
     pick = jnp.where((slot == places[0]) | (slot == places[1]), 1.0, 0.0).astype(BF16)
@@ -154,14 +164,18 @@
     return kernel_call(
         functools.partial(load_body, experts, cap, pair_cap),
         "load",
+        MOST,
         grid=(experts // per,),
-        in_specs=[pl.BlockSpec(v.shape, whole) for v in (route, ids, x, a, b)],
+        in_specs=[pl.BlockSpec(v.shape, whole) for v in (route, ids)]
+        + [pl.BlockSpec(memory_space=pltpu.HBM)] * 3,
         out_specs=pl.BlockSpec((per, cap + 2 * pair_cap, width), lambda i: (i, 0, 0)),
         out_shape=jax.ShapeDtypeStruct((experts, cap + 2 * pair_cap, width), BF16),
         scratch_shapes=[
             pltpu.VMEM((8, x.shape[0]), jnp.int32),
             pltpu.VMEM((8, a.shape[0]), jnp.int32),
-        ],
+        ]
+        + [pltpu.VMEM(v.shape, v.dtype) for v in (x, a, b)]
+        + [pltpu.SemaphoreType.DMA((3,))],
     )(route, ids, x, a, b)
 
 
@@ -373,48 +387,73 @@
     return jnp.sum(jnp.where(same, row, jnp.zeros_like(row)), axis=1, keepdims=True)
 
 
-def combine_body(scaled, experts, cap, *refs):
-    terms = 2 if scaled else 1
-    route_ref, rows_ref, out_ref = refs[0], refs[terms], refs[terms + 1]
-    picks = refs[terms + 2 :]
+def combine_body(experts, cap, route_ref, score_ref, rows_ref, out_ref):
     count, total = out_ref.shape[0], rows_ref.shape[0]
-
-    @pl.when(pl.program_id(0) == 0)
-    def _():
-        places = [column_of(place) for place in token_places(route_ref, experts, cap)]
-        slot = iota((count, total), 1)
-        hits = [slot == place for place in places]
-        if scaled:
-            shares = [column_of(share) for share in token_shares(refs[1])]
-            weight = jnp.where(hits[0], shares[0], 0.0) + jnp.where(hits[1], shares[1], 0.0)
-            high = weight.astype(BF16)
-            picks[0][...] = high
-            picks[1][...] = (weight - high.astype(F32)).astype(BF16)
-        else:
-            picks[0][...] = jnp.where(hits[0] | hits[1], 1.0, 0.0).astype(BF16)
-
+    places = [column_of(place) for place in token_places(route_ref, experts, cap)]
+    slot = iota((count, total), 1)
+    hits = [slot == place for place in places]
     rows = rows_ref[...]
-    out_ref[...] = sum(
-        jnp.dot(pick[...], rows, preferred_element_type=F32) for pick in picks
+    shares = [column_of(share) for share in token_shares(score_ref)]
+    weight = jnp.where(hits[0], shares[0], 0.0) + jnp.where(hits[1], shares[1], 0.0)
+    high = weight.astype(BF16)
+    low = (weight - high.astype(F32)).astype(BF16)
+    out_ref[...] = (
+        jnp.dot(high, rows, preferred_element_type=F32)
+        + jnp.dot(low, rows, preferred_element_type=F32)
     ).astype(BF16)
 
 
-def combine(route, score, rows, experts, cap, scaled):
+def combine(route, score, rows, experts, cap):
     count = route.shape[1]
     total, width = rows.shape
-    block = 256
+    block = 512
     whole = lambda i: (0, 0)
-    terms = 2 if scaled else 1
-    return kernel_call(
-        functools.partial(combine_body, scaled, experts, cap),
+    return kernel_call(
+        functools.partial(combine_body, experts, cap),
         "combine",
         grid=(width // block,),
-        in_specs=[pl.BlockSpec((2, count), whole)] * terms
+        in_specs=[pl.BlockSpec((2, count), whole)] * 2
         + [pl.BlockSpec((total, block), lambda i: (0, i))],
         out_specs=pl.BlockSpec((count, block), lambda i: (0, i)),
         out_shape=jax.ShapeDtypeStruct((count, width), BF16),
-        scratch_shapes=[pltpu.VMEM((count, total), BF16)] * terms,
-    )(*((route, score) if scaled else (route,)), rows)
+    )(route, score, rows)
+
+
+def pairs_body(experts, cap, route_ref, out_ref):
+    places = [column_of(place) for place in token_places(route_ref, experts, cap)]
+    slot = iota(out_ref.shape, 1)
+    out_ref[...] = jnp.where((slot == places[0]) | (slot == places[1]), 1.0, 0.0).astype(BF16)
+
+
+def token_pairs(route, experts, cap):
+    return kernel_call(
+        functools.partial(pairs_body, experts, cap),
+        "token_pairs",
+        out_shape=jax.ShapeDtypeStruct((route.shape[1], experts * cap), BF16),
+    )(route)
+
+
+def pair_rows_body(picks_ref, rows_ref, out_ref):
+    out_ref[...] = jnp.dot(
+        picks_ref[...], rows_ref[...], preferred_element_type=F32
+    ).astype(BF16)
+
+
+def pair_rows(picks, rows):
+    count, total = picks.shape
+    width = rows.shape[1]
+    block = 256
+    return kernel_call(
+        pair_rows_body,
+        "pair_rows",
+        grid=(width // block,),
+        in_specs=[
+            pl.BlockSpec((count, total), lambda i: (0, 0)),
+            pl.BlockSpec((total, block), lambda i: (0, i)),
+        ],
+        out_specs=pl.BlockSpec((count, block), lambda i: (0, i)),
+        out_shape=jax.ShapeDtypeStruct((count, width), BF16),
+    )(picks, rows)
 
 
 def exchange(rows, parts):
@@ -512,7 +551,8 @@
     hidden = gather_blocks(hidden)
     down_rows = unpack_one(raw_down, pair_cap)
     out_part = product(hidden, down_rows, False)
-    out_part, rows_dy = lax.optimization_barrier((out_part, rows_dy))
+    picks = token_pairs(route, experts, tok_cap)
+    out_part, rows_dy, picks = lax.optimization_barrier((out_part, rows_dy, picks))
     back_out = exchange(out_part, experts)
 
     back = scatter_end(*scatter_start(product(rows_dy, down_rows, True)))
@@ -526,8 +566,8 @@
         d_both[:, :SLOTS], rows_x, over_rows, preferred_element_type=F32
     )
     grad_up = lax.dot_general(d_both[:, SLOTS:], rows_x, over_rows, preferred_element_type=F32)
-    mixed = combine(route, score, back_out, experts, tok_cap, True)
-    input_grad = combine(route, score, back_in, experts, tok_cap, False)
+    mixed = combine(route, score, back_out, experts, tok_cap)
+    input_grad = pair_rows(picks, back_in)
     return (
         mixed,
         input_grad,

time: 344 us -> 341 us (level)
  local copies, waits for them, and re-layouts: 12.3 us -> 8.41 us
    unnamed x42 -> x36, local copies, waits for them, and re-layouts: 10.9 us -> 6.92 us
    pallas_call x2 -> x3, Pallas kernels: 9.55 us -> 8.69 us  [the longest x1 4.17 us: combine(): kernel_call(functools.partial(combine_body, experts, cap), 'combine', gri...]
where the time goes in v5:
time: 341 us; the launch traced here: 340 us
  waiting for transfers between devices  204 us (60%)
  starting transfers between devices  66.4 us (19%)
  Pallas kernels  50.9 us (15%)
  matrix products  9.61 us (3%)
  local copies, waits for them, and re-layouts  8.41 us (2%)
    all_to_all x1, waiting for transfers between devices, body(): raw = lax.all_to_all(sent, EXPERT, split_axis=0, concat_axis=0, tiled=True)  98.1 us
    all_to_all x4, waiting for transfers between devices, exchange(): lax.all_to_all(rows.reshape(parts, total // parts, width), EXPERT, split_...  61.3 us
    ppermute x20, waiting for transfers between devices, shift(): lax.ppermute(value, axis, [(i, (i + step) % size) for i in range(size)])  44.4 us
    all_to_all x4, starting transfers between devices, exchange(): lax.all_to_all(rows.reshape(parts, total // parts, width), EXPERT, split_...  29.8 us
    ppermute x20, starting transfers between devices, shift(): lax.ppermute(value, axis, [(i, (i + step) % size) for i in range(size)])  25 us
    pallas_call x4, Pallas kernels, product(): kernel_call(functools.partial(product_body, dims), 'product', grid=(rows...  16.2 us
    all_to_all x1, starting transfers between devices, body(): raw = lax.all_to_all(sent, EXPERT, split_axis=0, concat_axis=0, tiled=True)  11.6 us
    pallas_call x1, Pallas kernels, load(): kernel_call(functools.partial(load_body, experts, cap, pair_cap), 'load',...  8.68 us
  transfers between devices with their start and end apart: 25, of which 19 were waited for; matrix products, arithmetic and copies ran while one was open for 3% of the time, Pallas kernels for 11%

profile of v5, /device:TPU:24, one launch (start us, length us, event | category | flops | bytes accessed | tf_op | source)
XLA Modules:
  0.0 340.2 jit_solution(282323045305619804)
XLA Ops:
  0.6 8.7 %load.1 = bf16[32,72,1024]{2,1,0:T(8,128)(2,1)} custom-call(s32[2,256]{1,0:T(2,128)} %bitcast.63, s32[1,448]{1,0:T(1,128)} %bitcast.69, bf16[256,1024]{1,0:T(8,128)(2,1)} %refs_0_.1, bf16[448,1024]{1,0:T(8,128)(2,1)} %refs_1_.1, bf16[448,1024]{1,0:T(8,128)(2,1)} %refs_2_.2), custom_call_target="tpu_custom_call" | custom-call | tf_op jit(solution)/shard_map/load/pallas_call | solution.py:164
  9.3 11.6 %all-to-all-start = ((bf16[32,72,1024]{2,1,0:T(8,128)(2,1)}), bf16[32,72,1024]{2,1,0:T(8,128)(2,1)}, u32[]{:S(2)}, u32[]{:S(2)}) async-start(bf16[32,72,1024]{2,1,0:T(8,128)(2,1)} %load.1), calls=%async_computation | async-start | bytes 9437184 | tf_op jit(solution)/shard_map/all_to_all | solution.py:542
  21.0 4.0 %pack.1 = bf16[1280,512]{1,0:T(8,128)(2,1)} custom-call(s32[1,448]{1,0:T(1,128)S(1)} %bitcast.70, bf16[448,1024]{1,0:T(8,128)(2,1)S(1)} %copy-done.7, bf16[448,1024]{1,0:T(8,128)(2,1)S(1)} %copy-done.7), custom_call_target="tpu_custom_call" | custom-call | tf_op jit(solution)/shard_map/pack/pallas_call | solution.py:107
  25.0 3.1 dispatch.1
  28.1 98.1 %all-to-all-done.raw_ref = bf16[32,72,1024]{2,1,0:T(8,128)(2,1)} async-done(((bf16[32,72,1024]{2,1,0:T(8,128)(2,1)}), bf16[32,72,1024]{2,1,0:T(8,128)(2,1)}, u32[]{:S(2)}, u32[]{:S(2)}) %all-to-all-start) | async-done | bytes 4718624 | tf_op jit(solution)/shard_map/all_to_all | solution.py:542
  126.2 8.9 %all-to-all-start.1 = ((bf16[32,40,512]{2,1,0:T(8,128)(2,1)}), bf16[32,40,512]{2,1,0:T(8,128)(2,1)}, u32[]{:S(2)}, u32[]{:S(2)}) async-start(bf16[32,40,512]{2,1,0:T(8,128)(2,1)} %bitcast.13), calls=%async_computation.1 | async-start | bytes 2621440 | tf_op jit(solution)/shard_map/all_to_all | solution.py:461
  135.1 4.4 %unload.1 = (bf16[1024,1024]{1,0:T(8,128)(2,1)S(1)}, bf16[2,640,1024]{2,1,0:T(8,128)(2,1)S(1)}) custom-call(bf16[32,72,1024]{2,1,0:T(8,128)(2,1)} %all-to-all-done.raw_ref), custom_call_target="tpu_custom_call" | custom-call | tf_op jit(solution)/shard_map/unload/pallas_call | solution.py:197
  141.0 6.0 %product.4 = bf16[1024,1280]{1,0:T(8,128)(2,1)S(1)} custom-call(bf16[1024,1024]{1,0:T(8,128)(2,1)S(1)} %get-tuple-element.18.a_ref, bf16[1280,1024]{1,0:T(8,128)(2,1)} %bitcast.50), custom_call_target="tpu_custom_call" | custom-call | tf_op jit(solution)/shard_map/product/pallas_call | solution.py:370
  148.2 3.4 collective-permute-done.other_ref
  156.8 4.2 %collective-permute-done.3.half_ref = bf16[128,640]{1,0:T(8,128)(2,1)S(1)} collective-permute-done((bf16[128,640]{1,0:T(8,128)(2,1)S(1)}, bf16[128,640]{1,0:T(8,128)(2,1)S(1)}, u32[]{:S(2)}, u32[]{:S(2)}) %collective-permute-start.3) | collective-permute-done | bytes 163872 | tf_op jit(solution)/shard_map/ppermute | solution.py:476
  161.1 7.2 %all-to-all-done.1 = bf16[32,40,512]{2,1,0:T(8,128)(2,1)} async-done(((bf16[32,40,512]{2,1,0:T(8,128)(2,1)}), bf16[32,40,512]{2,1,0:T(8,128)(2,1)}, u32[]{:S(2)}, u32[]{:S(2)}) %all-to-all-start.1) | async-done | bytes 1310752 | tf_op jit(solution)/shard_map/all_to_all | solution.py:461
  168.4 5.7 %all-to-all-start.2 = ((bf16[32,32,1024]{2,1,0:T(8,128)(2,1)}), bf16[32,32,1024]{2,1,0:T(8,128)(2,1)S(1)}, u32[]{:S(2)}, u32[]{:S(2)}) async-start(bf16[32,32,1024]{2,1,0:T(8,128)(2,1)} %bitcast.15), calls=%async_computation.2 | async-start | bytes 4194304 | tf_op jit(solution)/shard_map/all_to_all | solution.py:461
  177.4 5.8 %collective-permute-done.4.above_ref = bf16[128,1280]{1,0:T(8,128)(2,1)S(1)} collective-permute-done((bf16[128,1280]{1,0:T(8,128)(2,1)S(1)}, bf16[128,1280]{1,0:T(8,128)(2,1)S(1)}, u32[]{:S(2)}, u32[]{:S(2)}) %collective-permute-start.4) | collective-permute-done | bytes 327712 | tf_op jit(solution)/shard_map/ppermute | solution.py:476
  184.3 3.2 collective-permute-start.5
  187.5 3.3 collective-permute-done.6.above_ref
  190.9 3.3 collective-permute-start.7
  198.3 3.0 unpack_one.1.b_ref
  206.2 16.7 %all-to-all-done.2 = bf16[32,32,1024]{2,1,0:T(8,128)(2,1)S(1)} async-done(((bf16[32,32,1024]{2,1,0:T(8,128)(2,1)}), bf16[32,32,1024]{2,1,0:T(8,128)(2,1)S(1)}, u32[]{:S(2)}, u32[]{:S(2)}) %all-to-all-start.2) | async-done | bytes 2097184 | tf_op jit(solution)/shard_map/all_to_all | solution.py:461
  222.9 6.1 %all-to-all-start.3 = ((bf16[32,32,1024]{2,1,0:T(8,128)(2,1)}), bf16[32,32,1024]{2,1,0:T(8,128)(2,1)}, u32[]{:S(2)}, u32[]{:S(2)}) async-start(bf16[32,32,1024]{2,1,0:T(8,128)(2,1)} %bitcast.58), calls=%async_computation.3 | async-start | bytes 4194304 | tf_op jit(solution)/shard_map/all_to_all | solution.py:461
  239.3 3.6 %collective-permute-start.12 = (bf16[128,640]{1,0:T(8,128)(2,1)S(1)}, bf16[128,640]{1,0:T(8,128)(2,1)S(1)}, u32[]{:S(2)}, u32[]{:S(2)}) collective-permute-start(bf16[128,640]{1,0:T(8,128)(2,1)S(1)} %add_half.6), channel_id=1, source_target_pairs={{0,64},{64,128},{128,192},{192,0},{1,65},{65,129},{129,193},{193,1... | collective-permute-start | bytes 491528 | tf_op jit(solution)/shard_map/ppermute | solution.py:476
  243.1 2.7 collective-permute-done.12.below_ref
  245.8 3.8 %collective-permute-done.14.above_ref = bf16[128,640]{1,0:T(8,128)(2,1)S(1)} collective-permute-done((bf16[128,640]{1,0:T(8,128)(2,1)S(1)}, bf16[128,640]{1,0:T(8,128)(2,1)S(1)}, u32[]{:S(2)}, u32[]{:S(2)}) %collective-permute-start.14) | collective-permute-done | bytes 163872 | tf_op jit(solution)/shard_map/ppermute | solution.py:476
  251.9 5.7 %collective-permute-done.15.below_ref = bf16[128,1280]{1,0:T(8,128)(2,1)S(1)} collective-permute-done((bf16[128,1280]{1,0:T(8,128)(2,1)S(1)}, bf16[128,1280]{1,0:T(8,128)(2,1)S(1)}, u32[]{:S(2)}, u32[]{:S(2)}) %collective-permute-start.15) | collective-permute-done | bytes 327712 | tf_op jit(solution)/shard_map/ppermute | solution.py:476
  259.8 3.2 collective-permute-done.17.low_ref
  263.0 2.8 collective-permute-done.18.high_ref
  266.0 3.0 collective-permute-done.19.other_ref
  269.2 5.3 %product.7 = bf16[1024,1024]{1,0:T(8,128)(2,1)S(1)} custom-call(bf16[1024,1280]{1,0:T(8,128)(2,1)S(1)} %bitcast.52, bf16[1280,1024]{1,0:T(8,128)(2,1)} %bitcast.51), custom_call_target="tpu_custom_call" | custom-call | tf_op jit(solution)/shard_map/product/pallas_call | solution.py:370
  276.8 9.1 %all-to-all-start.4 = ((bf16[32,32,1024]{2,1,0:T(8,128)(2,1)}), bf16[32,32,1024]{2,1,0:T(8,128)(2,1)}, u32[]{:S(2)}, u32[]{:S(2)}) async-start(bf16[32,32,1024]{2,1,0:T(8,128)(2,1)} %bitcast.55), calls=%async_computation.4 | async-start | bytes 4194304 | tf_op jit(solution)/shard_map/all_to_all | solution.py:461
  286.0 4.4 %fusion.1 = bf16[1,640,1024]{2,1,0:T(8,128)(2,1)} fusion(bf16[1024,1024]{1,0:T(8,128)(2,1)} %copy-done.8, bf16[1024,1280]{1,0:T(8,128)(2,1)S(1)} %bitcast.53), kind=kOutput, calls=%fused_computation.4 | convolution fusion | flops 1342832640 | bytes 4718592 | tf_op jit(solution)/shard_map/dot_general | solution.py:568
  295.6 4.2 %combine.1 = bf16[256,1024]{1,0:T(8,128)(2,1)} custom-call(s32[2,256]{1,0:T(2,128)S(1)} %bitcast.66, s32[2,256]{1,0:T(2,128)S(1)} %bitcast.68, bf16[1024,1024]{1,0:T(8,128)(2,1)} %bitcast.18.rows_ref), custom_call_target="tpu_custom_call" | custom-call | tf_op jit(solution)/shard_map/combine/pallas_call | solution.py:411
  299.8 36.4 %all-to-all-done.4 = bf16[32,32,1024]{2,1,0:T(8,128)(2,1)} async-done(((bf16[32,32,1024]{2,1,0:T(8,128)(2,1)}), bf16[32,32,1024]{2,1,0:T(8,128)(2,1)}, u32[]{:S(2)}, u32[]{:S(2)}) %all-to-all-start.4) | async-done | bytes 2097184 | tf_op jit(solution)/shard_map/all_to_all | solution.py:461
  336.2 4.0 %pair_rows.1 = bf16[256,1024]{1,0:T(8,128)(2,1)} custom-call(bf16[256,1024]{1,0:T(8,128)(2,1)S(1)} %copy-done.11, bf16[1024,1024]{1,0:T(8,128)(2,1)} %bitcast.27.rows_ref), custom_call_target="tpu_custom_call" | custom-call | tf_op jit(solution)/shard_map/pair_rows/pallas_call | solution.py:446
  (92 shorter events, 44.1 us)
Async XLA Ops:
  9.3 11.6 %copy-start.7 = (bf16[448,1024]{1,0:T(8,128)(2,1)S(1)}, bf16[448,1024]{1,0:T(8,128)(2,1)}, u32[]{:S(2)}) copy-start(bf16[448,1024]{1,0:T(8,128)(2,1)} %b_ref.1) | copy-start | bytes 2752516
  9.3 11.6 %copy-start.17 = (s32[448,1]{0,1:T(1,128)S(1)}, s32[448,1]{0,1:T(1,128)}, u32[]{:S(2)}) copy-start(s32[448,1]{0,1:T(1,128)} %param.12) | copy-start | bytes 5380
  9.3 116.8 %all-to-all-start = ((bf16[32,72,1024]{2,1,0:T(8,128)(2,1)}), bf16[32,72,1024]{2,1,0:T(8,128)(2,1)}, u32[]{:S(2)}, u32[]{:S(2)}) async-start(bf16[32,72,1024]{2,1,0:T(8,128)(2,1)} %load.1), calls=%async_computation | async-start | bytes 9437184 | tf_op jit(solution)/shard_map/all_to_all | solution.py:542
  126.2 42.2 %all-to-all-start.1 = ((bf16[32,40,512]{2,1,0:T(8,128)(2,1)}), bf16[32,40,512]{2,1,0:T(8,128)(2,1)}, u32[]{:S(2)}, u32[]{:S(2)}) async-start(bf16[32,40,512]{2,1,0:T(8,128)(2,1)} %bitcast.13), calls=%async_computation.1 | async-start | bytes 2621440 | tf_op jit(solution)/shard_map/all_to_all | solution.py:461
  141.0 6.1 %copy-start.8 = (bf16[1024,1024]{1,0:T(8,128)(2,1)}, bf16[1024,1024]{1,0:T(8,128)(2,1)S(1)}, u32[]{:S(2)}) copy-start(bf16[1024,1024]{1,0:T(8,128)(2,1)S(1)} %get-tuple-element.18.a_ref) | copy-start | bytes 6291460
  148.2 3.4 collective-permute-start
  153.5 7.5 %collective-permute-start.3 = (bf16[128,640]{1,0:T(8,128)(2,1)S(1)}, bf16[128,640]{1,0:T(8,128)(2,1)S(1)}, u32[]{:S(2)}, u32[]{:S(2)}) collective-permute-start(bf16[128,640]{1,0:T(8,128)(2,1)S(1)} %get-tuple-element.39), channel_id=1, source_target_pairs={{0,192},{64,0},{128,64},{192,128},{1,193},{65,1},{129,65},{193,129... | collective-permute-start | bytes 491528 | tf_op jit(solution)/shard_map/ppermute | solution.py:476
  154.3 6.8 %collective-permute-start.1 = (bf16[128,640]{1,0:T(8,128)(2,1)S(1)}, bf16[128,640]{1,0:T(8,128)(2,1)S(1)}, u32[]{:S(2)}, u32[]{:S(2)}) collective-permute-start(bf16[128,640]{1,0:T(8,128)(2,1)S(1)} %get-tuple-element.40), channel_id=1, source_target_pairs={{0,64},{64,128},{128,192},{192,0},{1,65},{65,129},{129,193},{193,1... | collective-permute-start | bytes 491528 | tf_op jit(solution)/shard_map/ppermute | solution.py:476
  168.4 54.5 %all-to-all-start.2 = ((bf16[32,32,1024]{2,1,0:T(8,128)(2,1)}), bf16[32,32,1024]{2,1,0:T(8,128)(2,1)S(1)}, u32[]{:S(2)}, u32[]{:S(2)}) async-start(bf16[32,32,1024]{2,1,0:T(8,128)(2,1)} %bitcast.15), calls=%async_computation.2 | async-start | bytes 4194304 | tf_op jit(solution)/shard_map/all_to_all | solution.py:461
  174.1 9.2 %collective-permute-start.4 = (bf16[128,1280]{1,0:T(8,128)(2,1)S(1)}, bf16[128,1280]{1,0:T(8,128)(2,1)S(1)}, u32[]{:S(2)}, u32[]{:S(2)}) collective-permute-start(bf16[128,1280]{1,0:T(8,128)(2,1)S(1)} %add_half.5), channel_id=1, source_target_pairs={{0,192},{64,0},{128,64},{192,128},{1,193},{65,1},{129,65},{193,129... | collective-permute-start | bytes 983048 | tf_op jit(solution)/shard_map/ppermute | solution.py:476
  174.9 8.3 %collective-permute-start.2 = (bf16[128,1280]{1,0:T(8,128)(2,1)S(1)}, bf16[128,1280]{1,0:T(8,128)(2,1)S(1)}, u32[]{:S(2)}, u32[]{:S(2)}) collective-permute-start(bf16[128,1280]{1,0:T(8,128)(2,1)S(1)} %add_half.4), channel_id=1, source_target_pairs={{0,64},{64,128},{128,192},{192,0},{1,65},{65,129},{129,193},{193,1... | collective-permute-start | bytes 983048 | tf_op jit(solution)/shard_map/ppermute | solution.py:476
  184.2 6.5 %collective-permute-start.6 = (bf16[128,640]{1,0:T(8,128)(2,1)S(1)}, bf16[128,640]{1,0:T(8,128)(2,1)S(1)}, u32[]{:S(2)}, u32[]{:S(2)}) collective-permute-start(bf16[128,640]{1,0:T(8,128)(2,1)S(1)} %get-tuple-element.20.own_ref), channel_id=1, source_target_pairs={{0,192},{64,0},{128,64},{192,128},{1,193},{65,1},{129,65},{193,129... | collective-permute-start | bytes 491528 | tf_op jit(solution)/shard_map/ppermute | solution.py:476
  184.3 6.6 %collective-permute-start.5 = (bf16[128,640]{1,0:T(8,128)(2,1)S(1)}, bf16[128,640]{1,0:T(8,128)(2,1)S(1)}, u32[]{:S(2)}, u32[]{:S(2)}) collective-permute-start(bf16[128,640]{1,0:T(8,128)(2,1)S(1)} %get-tuple-element.20.own_ref), channel_id=1, source_target_pairs={{0,64},{64,128},{128,192},{192,0},{1,65},{65,129},{129,193},{193,1... | collective-permute-start | bytes 491528 | tf_op jit(solution)/shard_map/ppermute | solution.py:476
  190.8 5.9 %collective-permute-start.8 = (bf16[128,384]{1,0:T(8,128)(2,1)S(1)}, bf16[128,384]{1,0:T(8,128)(2,1)S(1)}, u32[]{:S(2)}, u32[]{:S(2)}) collective-permute-start(bf16[128,384]{1,0:T(8,128)(2,1)S(1)} %slice.43), channel_id=1, source_target_pairs={{0,192},{64,0},{128,64},{192,128},{1,193},{65,1},{129,65},{193,129... | collective-permute-start | bytes 294920 | tf_op jit(solution)/shard_map/ppermute | solution.py:476
  190.9 5.2 %collective-permute-start.7 = (bf16[128,256]{1,0:T(8,128)(2,1)S(1)}, bf16[128,256]{1,0:T(8,128)(2,1)S(1)}, u32[]{:S(2)}, u32[]{:S(2)}) collective-permute-start(bf16[128,256]{1,0:T(8,128)(2,1)S(1)} %slice.42), channel_id=1, source_target_pairs={{0,64},{64,128},{128,192},{192,0},{1,65},{65,129},{129,193},{193,1... | collective-permute-start | bytes 196616 | tf_op jit(solution)/shard_map/ppermute | solution.py:476
  196.8 4.6 %collective-permute-start.9 = (bf16[4,128,640]{2,1,0:T(8,128)(2,1)S(1)}, bf16[4,128,640]{2,1,0:T(8,128)(2,1)S(1)}, u32[]{:S(2)}, u32[]{:S(2)}) collective-permute-start(bf16[4,128,640]{2,1,0:T(8,128)(2,1)S(1)} %column.2.own_ref), channel_id=1, source_target_pairs={{0,32},{32,0},{1,33},{33,1},{2,34},{34,2},{3,35},{35,3},{4,36},{36... | collective-permute-start | bytes 1966088 | tf_op jit(solution)/shard_map/ppermute | solution.py:476
  222.9 6.1 %copy-start.2 = (bf16[32,32,1024]{2,1,0:T(8,128)(2,1)}, bf16[32,32,1024]{2,1,0:T(8,128)(2,1)S(1)}, u32[]{:S(2)}) copy-start(bf16[32,32,1024]{2,1,0:T(8,128)(2,1)S(1)} %all-to-all-done.2) | copy-start | bytes 6291460
  222.9 53.9 %all-to-all-start.3 = ((bf16[32,32,1024]{2,1,0:T(8,128)(2,1)}), bf16[32,32,1024]{2,1,0:T(8,128)(2,1)}, u32[]{:S(2)}, u32[]{:S(2)}) async-start(bf16[32,32,1024]{2,1,0:T(8,128)(2,1)} %bitcast.58), calls=%async_computation.3 | async-start | bytes 4194304 | tf_op jit(solution)/shard_map/all_to_all | solution.py:461
  231.6 18.0 %copy-start.13 = (f32[128,1280]{1,0:T(8,128)S(1)}, f32[128,1280]{1,0:T(8,128)}, u32[]{:S(2)}) copy-start(f32[128,1280]{1,0:T(8,128)} %copy-done.12) | copy-start | bytes 1966084
  231.6 2.2 collective-permute-start.10
  234.1 8.9 %collective-permute-start.13 = (bf16[128,384]{1,0:T(8,128)(2,1)S(1)}, bf16[128,384]{1,0:T(8,128)(2,1)S(1)}, u32[]{:S(2)}, u32[]{:S(2)}) collective-permute-start(bf16[128,384]{1,0:T(8,128)(2,1)S(1)} %slice.45), channel_id=1, source_target_pairs={{0,192},{64,0},{128,64},{192,128},{1,193},{65,1},{129,65},{193,129... | collective-permute-start | bytes 294920 | tf_op jit(solution)/shard_map/ppermute | solution.py:476
  234.9 4.4 %collective-permute-start.11 = (bf16[128,256]{1,0:T(8,128)(2,1)S(1)}, bf16[128,256]{1,0:T(8,128)(2,1)S(1)}, u32[]{:S(2)}, u32[]{:S(2)}) collective-permute-start(bf16[128,256]{1,0:T(8,128)(2,1)S(1)} %slice.44), channel_id=1, source_target_pairs={{0,64},{64,128},{128,192},{192,0},{1,65},{65,129},{129,193},{193,1... | collective-permute-start | bytes 196616 | tf_op jit(solution)/shard_map/ppermute | solution.py:476
  239.3 6.5 %collective-permute-start.12 = (bf16[128,640]{1,0:T(8,128)(2,1)S(1)}, bf16[128,640]{1,0:T(8,128)(2,1)S(1)}, u32[]{:S(2)}, u32[]{:S(2)}) collective-permute-start(bf16[128,640]{1,0:T(8,128)(2,1)S(1)} %add_half.6), channel_id=1, source_target_pairs={{0,64},{64,128},{128,192},{192,0},{1,65},{65,129},{129,193},{193,1... | collective-permute-start | bytes 491528 | tf_op jit(solution)/shard_map/ppermute | solution.py:476
  243.0 6.6 %collective-permute-start.14 = (bf16[128,640]{1,0:T(8,128)(2,1)S(1)}, bf16[128,640]{1,0:T(8,128)(2,1)S(1)}, u32[]{:S(2)}, u32[]{:S(2)}) collective-permute-start(bf16[128,640]{1,0:T(8,128)(2,1)S(1)} %add_half.7), channel_id=1, source_target_pairs={{0,192},{64,0},{128,64},{192,128},{1,193},{65,1},{129,65},{193,129... | collective-permute-start | bytes 491528 | tf_op jit(solution)/shard_map/ppermute | solution.py:476
  249.8 7.8 %collective-permute-start.15 = (bf16[128,1280]{1,0:T(8,128)(2,1)S(1)}, bf16[128,1280]{1,0:T(8,128)(2,1)S(1)}, u32[]{:S(2)}, u32[]{:S(2)}) collective-permute-start(bf16[128,1280]{1,0:T(8,128)(2,1)S(1)} %backprop.1.own_ref), channel_id=1, source_target_pairs={{0,64},{64,128},{128,192},{192,0},{1,65},{65,129},{129,193},{193,1... | collective-permute-start | bytes 983048 | tf_op jit(solution)/shard_map/ppermute | solution.py:476
  249.9 9.3 %collective-permute-start.16 = (bf16[128,1280]{1,0:T(8,128)(2,1)S(1)}, bf16[128,1280]{1,0:T(8,128)(2,1)S(1)}, u32[]{:S(2)}, u32[]{:S(2)}) collective-permute-start(bf16[128,1280]{1,0:T(8,128)(2,1)S(1)} %backprop.1.own_ref), channel_id=1, source_target_pairs={{0,192},{64,0},{128,64},{192,128},{1,193},{65,1},{129,65},{193,129... | collective-permute-start | bytes 983048 | tf_op jit(solution)/shard_map/ppermute | solution.py:476
  257.6 5.4 %collective-permute-start.17 = (bf16[128,640]{1,0:T(8,128)(2,1)S(1)}, bf16[128,640]{1,0:T(8,128)(2,1)S(1)}, u32[]{:S(2)}, u32[]{:S(2)}) collective-permute-start(bf16[128,640]{1,0:T(8,128)(2,1)S(1)} %slice.46), channel_id=1, source_target_pairs={{0,64},{64,128},{128,192},{192,0},{1,65},{65,129},{129,193},{193,1... | collective-permute-start | bytes 491528 | tf_op jit(solution)/shard_map/ppermute | solution.py:476
  259.2 6.6 %collective-permute-start.18 = (bf16[128,640]{1,0:T(8,128)(2,1)S(1)}, bf16[128,640]{1,0:T(8,128)(2,1)S(1)}, u32[]{:S(2)}, u32[]{:S(2)}) collective-permute-start(bf16[128,640]{1,0:T(8,128)(2,1)S(1)} %slice.47), channel_id=1, source_target_pairs={{0,192},{64,0},{128,64},{192,128},{1,193},{65,1},{129,65},{193,129... | collective-permute-start | bytes 491528 | tf_op jit(solution)/shard_map/ppermute | solution.py:476
  265.9 3.1 collective-permute-start.19
  276.8 59.3 %all-to-all-start.4 = ((bf16[32,32,1024]{2,1,0:T(8,128)(2,1)}), bf16[32,32,1024]{2,1,0:T(8,128)(2,1)}, u32[]{:S(2)}, u32[]{:S(2)}) async-start(bf16[32,32,1024]{2,1,0:T(8,128)(2,1)} %bitcast.55), calls=%async_computation.4 | async-start | bytes 4194304 | tf_op jit(solution)/shard_map/all_to_all | solution.py:461
  285.9 4.4 %copy-start.9 = (bf16[1024,1024]{1,0:T(8,128)(2,1)S(1)}, bf16[1024,1024]{1,0:T(8,128)(2,1)}, u32[]{:S(2)}) copy-start(bf16[1024,1024]{1,0:T(8,128)(2,1)} %copy-done.8) | copy-start | bytes 6291460
  295.6 40.6 %copy-start.11 = (bf16[256,1024]{1,0:T(8,128)(2,1)S(1)}, bf16[256,1024]{1,0:T(8,128)(2,1)}, u32[]{:S(2)}) copy-start(bf16[256,1024]{1,0:T(8,128)(2,1)} %copy-done.10) | copy-start | bytes 1572868
  (11 other events, 24.4 us)

commit v6 on v5

--- a/solution.py
+++ b/solution.py
@@ -159,7 +159,7 @@
 
 def load(route, ids, x, a, b, experts, cap, pair_cap):
     width = x.shape[1]
-    per = 4
+    per = 8
     whole = lambda i: (0, 0)
     return kernel_call(
         functools.partial(load_body, experts, cap, pair_cap),
@@ -365,7 +365,7 @@
 def product(a, b, transposed):
     rows, depth = a.shape
     n = b.shape[0 if transposed else 1]
-    block = 256
+    block = 512
     dims = (((1,), (1 if transposed else 0,)), ((), ()))
     return kernel_call(
         functools.partial(product_body, dims),
@@ -433,26 +433,39 @@
     )(route)
 
 
-def pair_rows_body(picks_ref, rows_ref, out_ref):
-    out_ref[...] = jnp.dot(
-        picks_ref[...], rows_ref[...], preferred_element_type=F32
-    ).astype(BF16)
+def pair_rows_body(parts, picks_in, rows_in, out_ref, picks, rows, sems):
+    block = rows.shape[0] // parts
+    copies = [pltpu.make_async_copy(picks_in, picks, sems.at[parts])]
+    for k in range(parts):
+        some = pl.ds(k * block, block)
+        copies.append(pltpu.make_async_copy(rows_in.at[some], rows.at[some], sems.at[k]))
+    for copy in copies:
+        copy.start()
+    copies[0].wait()
+    total = None
+    for k in range(parts):
+        copies[k + 1].wait()
+        some = slice(k * block, (k + 1) * block)
+        term = jnp.dot(picks[:, some], rows[some, :], preferred_element_type=F32)
+        total = term if total is None else total + term
+    out_ref[...] = total.astype(BF16)
 
 
 def pair_rows(picks, rows):
-    count, total = picks.shape
-    width = rows.shape[1]
-    block = 256
-    return kernel_call(
-        pair_rows_body,
+    parts = 4
+    held = pl.BlockSpec(memory_space=pltpu.HBM)
+    return kernel_call(
+        functools.partial(pair_rows_body, parts),
         "pair_rows",
-        grid=(width // block,),
-        in_specs=[
-            pl.BlockSpec((count, total), lambda i: (0, 0)),
-            pl.BlockSpec((total, block), lambda i: (0, i)),
+        MOST,
+        in_specs=[held, held],
+        out_specs=pl.BlockSpec(memory_space=pltpu.VMEM),
+        out_shape=jax.ShapeDtypeStruct((picks.shape[0], rows.shape[1]), BF16),
+        scratch_shapes=[
+            pltpu.VMEM(picks.shape, BF16),
+            pltpu.VMEM(rows.shape, BF16),
+            pltpu.SemaphoreType.DMA((parts + 1,)),
         ],
-        out_specs=pl.BlockSpec((count, block), lambda i: (0, i)),
-        out_shape=jax.ShapeDtypeStruct((count, width), BF16),
     )(picks, rows)
 
 

time: 341 us -> 338 us (level)
  Pallas kernels: 50.9 us -> 46.9 us
    unnamed x36 -> x34, local copies, waits for them, and re-layouts: 6.92 us -> 6.9 us
where the time goes in v6:
time: 338 us; the launch traced here: 337 us
  waiting for transfers between devices  206 us (61%)
  starting transfers between devices  65.2 us (19%)
  Pallas kernels  46.9 us (14%)
  matrix products  9.61 us (3%)
  local copies, waits for them, and re-layouts  8.38 us (2%)
    all_to_all x1, waiting for transfers between devices, body(): raw = lax.all_to_all(sent, EXPERT, split_axis=0, concat_axis=0, tiled=True)  98.1 us
    all_to_all x4, waiting for transfers between devices, exchange(): lax.all_to_all(rows.reshape(parts, total // parts, width), EXPERT, split_...  63.4 us
    ppermute x20, waiting for transfers between devices, shift(): lax.ppermute(value, axis, [(i, (i + step) % size) for i in range(size)])  44.2 us
    all_to_all x4, starting transfers between devices, exchange(): lax.all_to_all(rows.reshape(parts, total // parts, width), EXPERT, split_...  28.6 us
    ppermute x20, starting transfers between devices, shift(): lax.ppermute(value, axis, [(i, (i + step) % size) for i in range(size)])  25 us
    pallas_call x4, Pallas kernels, product(): kernel_call(functools.partial(product_body, dims), 'product', grid=(rows...  14.6 us
    all_to_all x1, starting transfers between devices, body(): raw = lax.all_to_all(sent, EXPERT, split_axis=0, concat_axis=0, tiled=True)  11.6 us
    pallas_call x1, Pallas kernels, load(): kernel_call(functools.partial(load_body, experts, cap, pair_cap), 'load',...  7.4 us
  transfers between devices with their start and end apart: 25, of which 19 were waited for; matrix products, arithmetic and copies ran while one was open for 3% of the time, Pallas kernels for 11%

profile of v6, /device:TPU:24, one launch (start us, length us, event | category | flops | bytes accessed | tf_op | source)
XLA Modules:
  0.0 337.2 jit_solution(10090234285814629171)
XLA Ops:
  0.6 7.4 %load.1 = bf16[32,72,1024]{2,1,0:T(8,128)(2,1)} custom-call(s32[2,256]{1,0:T(2,128)} %bitcast.63, s32[1,448]{1,0:T(1,128)} %bitcast.69, bf16[256,1024]{1,0:T(8,128)(2,1)} %refs_0_.1, bf16[448,1024]{1,0:T(8,128)(2,1)} %refs_1_.1, bf16[448,1024]{1,0:T(8,128)(2,1)} %refs_2_.2), custom_call_target="tpu_custom_call" | custom-call | tf_op jit(solution)/shard_map/load/pallas_call | solution.py:164
  8.1 11.6 %all-to-all-start = ((bf16[32,72,1024]{2,1,0:T(8,128)(2,1)}), bf16[32,72,1024]{2,1,0:T(8,128)(2,1)}, u32[]{:S(2)}, u32[]{:S(2)}) async-start(bf16[32,72,1024]{2,1,0:T(8,128)(2,1)} %load.1), calls=%async_computation | async-start | bytes 9437184 | tf_op jit(solution)/shard_map/all_to_all | solution.py:555
  19.7 4.1 %pack.1 = bf16[1280,512]{1,0:T(8,128)(2,1)} custom-call(s32[1,448]{1,0:T(1,128)S(1)} %bitcast.70, bf16[448,1024]{1,0:T(8,128)(2,1)S(1)} %copy-done.7, bf16[448,1024]{1,0:T(8,128)(2,1)S(1)} %copy-done.7), custom_call_target="tpu_custom_call" | custom-call | tf_op jit(solution)/shard_map/pack/pallas_call | solution.py:107
  23.8 3.1 dispatch.1
  26.8 98.1 %all-to-all-done.raw_ref = bf16[32,72,1024]{2,1,0:T(8,128)(2,1)} async-done(((bf16[32,72,1024]{2,1,0:T(8,128)(2,1)}), bf16[32,72,1024]{2,1,0:T(8,128)(2,1)}, u32[]{:S(2)}, u32[]{:S(2)}) %all-to-all-start) | async-done | bytes 4718624 | tf_op jit(solution)/shard_map/all_to_all | solution.py:555
  124.9 8.9 %all-to-all-start.1 = ((bf16[32,40,512]{2,1,0:T(8,128)(2,1)}), bf16[32,40,512]{2,1,0:T(8,128)(2,1)}, u32[]{:S(2)}, u32[]{:S(2)}) async-start(bf16[32,40,512]{2,1,0:T(8,128)(2,1)} %bitcast.13), calls=%async_computation.1 | async-start | bytes 2621440 | tf_op jit(solution)/shard_map/all_to_all | solution.py:474
  133.8 4.4 %unload.1 = (bf16[1024,1024]{1,0:T(8,128)(2,1)S(1)}, bf16[2,640,1024]{2,1,0:T(8,128)(2,1)S(1)}) custom-call(bf16[32,72,1024]{2,1,0:T(8,128)(2,1)} %all-to-all-done.raw_ref), custom_call_target="tpu_custom_call" | custom-call | tf_op jit(solution)/shard_map/unload/pallas_call | solution.py:197
  139.7 5.6 %product.4 = bf16[1024,1280]{1,0:T(8,128)(2,1)S(1)} custom-call(bf16[1024,1024]{1,0:T(8,128)(2,1)S(1)} %get-tuple-element.18.a_ref, bf16[1280,1024]{1,0:T(8,128)(2,1)} %bitcast.50), custom_call_target="tpu_custom_call" | custom-call | tf_op jit(solution)/shard_map/product/pallas_call | solution.py:370
  146.5 3.4 %collective-permute-done.other_ref = bf16[4,128,1280]{2,1,0:T(8,128)(2,1)} collective-permute-done((bf16[4,128,1280]{2,1,0:T(8,128)(2,1)}, bf16[4,128,1280]{2,1,0:T(8,128)(2,1)}, u32[]{:S(2)}, u32[]{:S(2)}) %collective-permute-start) | collective-permute-done | bytes 1310752 | tf_op jit(solution)/shard_map/ppermute | solution.py:489
  155.1 4.2 %collective-permute-done.3.half_ref = bf16[128,640]{1,0:T(8,128)(2,1)S(1)} collective-permute-done((bf16[128,640]{1,0:T(8,128)(2,1)S(1)}, bf16[128,640]{1,0:T(8,128)(2,1)S(1)}, u32[]{:S(2)}, u32[]{:S(2)}) %collective-permute-start.3) | collective-permute-done | bytes 163872 | tf_op jit(solution)/shard_map/ppermute | solution.py:489
  159.5 7.7 %all-to-all-done.1 = bf16[32,40,512]{2,1,0:T(8,128)(2,1)} async-done(((bf16[32,40,512]{2,1,0:T(8,128)(2,1)}), bf16[32,40,512]{2,1,0:T(8,128)(2,1)}, u32[]{:S(2)}, u32[]{:S(2)}) %all-to-all-start.1) | async-done | bytes 1310752 | tf_op jit(solution)/shard_map/all_to_all | solution.py:474
  167.1 5.7 %all-to-all-start.2 = ((bf16[32,32,1024]{2,1,0:T(8,128)(2,1)}), bf16[32,32,1024]{2,1,0:T(8,128)(2,1)S(1)}, u32[]{:S(2)}, u32[]{:S(2)}) async-start(bf16[32,32,1024]{2,1,0:T(8,128)(2,1)} %bitcast.15), calls=%async_computation.2 | async-start | bytes 4194304 | tf_op jit(solution)/shard_map/all_to_all | solution.py:474
  176.1 5.8 %collective-permute-done.4.above_ref = bf16[128,1280]{1,0:T(8,128)(2,1)S(1)} collective-permute-done((bf16[128,1280]{1,0:T(8,128)(2,1)S(1)}, bf16[128,1280]{1,0:T(8,128)(2,1)S(1)}, u32[]{:S(2)}, u32[]{:S(2)}) %collective-permute-start.4) | collective-permute-done | bytes 327712 | tf_op jit(solution)/shard_map/ppermute | solution.py:489
  183.0 3.2 collective-permute-start.5
  186.2 3.3 collective-permute-done.6.above_ref
  189.6 3.5 %collective-permute-start.7 = (bf16[128,256]{1,0:T(8,128)(2,1)S(1)}, bf16[128,256]{1,0:T(8,128)(2,1)S(1)}, u32[]{:S(2)}, u32[]{:S(2)}) collective-permute-start(bf16[128,256]{1,0:T(8,128)(2,1)S(1)} %slice.42), channel_id=1, source_target_pairs={{0,64},{64,128},{128,192},{192,0},{1,65},{65,129},{129,193},{193,1... | collective-permute-start | bytes 196616 | tf_op jit(solution)/shard_map/ppermute | solution.py:489
  196.9 3.0 unpack_one.1.b_ref
  204.4 17.2 %all-to-all-done.2 = bf16[32,32,1024]{2,1,0:T(8,128)(2,1)S(1)} async-done(((bf16[32,32,1024]{2,1,0:T(8,128)(2,1)}), bf16[32,32,1024]{2,1,0:T(8,128)(2,1)S(1)}, u32[]{:S(2)}, u32[]{:S(2)}) %all-to-all-start.2) | async-done | bytes 2097184 | tf_op jit(solution)/shard_map/all_to_all | solution.py:474
  221.7 6.1 %all-to-all-start.3 = ((bf16[32,32,1024]{2,1,0:T(8,128)(2,1)}), bf16[32,32,1024]{2,1,0:T(8,128)(2,1)}, u32[]{:S(2)}, u32[]{:S(2)}) async-start(bf16[32,32,1024]{2,1,0:T(8,128)(2,1)} %bitcast.58), calls=%async_computation.3 | async-start | bytes 4194304 | tf_op jit(solution)/shard_map/all_to_all | solution.py:474
  237.6 3.6 %collective-permute-start.12 = (bf16[128,640]{1,0:T(8,128)(2,1)S(1)}, bf16[128,640]{1,0:T(8,128)(2,1)S(1)}, u32[]{:S(2)}, u32[]{:S(2)}) collective-permute-start(bf16[128,640]{1,0:T(8,128)(2,1)S(1)} %add_half.6), channel_id=1, source_target_pairs={{0,64},{64,128},{128,192},{192,0},{1,65},{65,129},{129,193},{193,1... | collective-permute-start | bytes 491528 | tf_op jit(solution)/shard_map/ppermute | solution.py:489
  241.4 2.7 collective-permute-done.12.below_ref
  244.1 3.8 %collective-permute-done.14.above_ref = bf16[128,640]{1,0:T(8,128)(2,1)S(1)} collective-permute-done((bf16[128,640]{1,0:T(8,128)(2,1)S(1)}, bf16[128,640]{1,0:T(8,128)(2,1)S(1)}, u32[]{:S(2)}, u32[]{:S(2)}) %collective-permute-start.14) | collective-permute-done | bytes 163872 | tf_op jit(solution)/shard_map/ppermute | solution.py:489
  250.2 5.7 %collective-permute-done.15.below_ref = bf16[128,1280]{1,0:T(8,128)(2,1)S(1)} collective-permute-done((bf16[128,1280]{1,0:T(8,128)(2,1)S(1)}, bf16[128,1280]{1,0:T(8,128)(2,1)S(1)}, u32[]{:S(2)}, u32[]{:S(2)}) %collective-permute-start.15) | collective-permute-done | bytes 327712 | tf_op jit(solution)/shard_map/ppermute | solution.py:489
  258.1 3.2 collective-permute-done.17.low_ref
  261.3 2.8 collective-permute-done.18.high_ref
  264.3 3.0 collective-permute-done.19.other_ref
  267.5 4.9 %product.7 = bf16[1024,1024]{1,0:T(8,128)(2,1)S(1)} custom-call(bf16[1024,1280]{1,0:T(8,128)(2,1)S(1)} %bitcast.52, bf16[1280,1024]{1,0:T(8,128)(2,1)} %bitcast.51), custom_call_target="tpu_custom_call" | custom-call | tf_op jit(solution)/shard_map/product/pallas_call | solution.py:370
  275.6 8.0 %all-to-all-start.4 = ((bf16[32,32,1024]{2,1,0:T(8,128)(2,1)}), bf16[32,32,1024]{2,1,0:T(8,128)(2,1)}, u32[]{:S(2)}, u32[]{:S(2)}) async-start(bf16[32,32,1024]{2,1,0:T(8,128)(2,1)} %bitcast.55), calls=%async_computation.4 | async-start | bytes 4194304 | tf_op jit(solution)/shard_map/all_to_all | solution.py:474
  283.5 4.4 %fusion.1 = bf16[1,640,1024]{2,1,0:T(8,128)(2,1)} fusion(bf16[1024,1024]{1,0:T(8,128)(2,1)} %copy-done.8, bf16[1024,1280]{1,0:T(8,128)(2,1)S(1)} %bitcast.53), kind=kOutput, calls=%fused_computation.4 | convolution fusion | flops 1342832640 | bytes 4718592 | tf_op jit(solution)/shard_map/dot_general | solution.py:581
  293.2 4.1 %combine.1 = bf16[256,1024]{1,0:T(8,128)(2,1)} custom-call(s32[2,256]{1,0:T(2,128)S(1)} %bitcast.66, s32[2,256]{1,0:T(2,128)S(1)} %bitcast.68, bf16[1024,1024]{1,0:T(8,128)(2,1)} %bitcast.18.rows_ref), custom_call_target="tpu_custom_call" | custom-call | tf_op jit(solution)/shard_map/combine/pallas_call | solution.py:411
  297.3 36.7 %all-to-all-done.4 = bf16[32,32,1024]{2,1,0:T(8,128)(2,1)} async-done(((bf16[32,32,1024]{2,1,0:T(8,128)(2,1)}), bf16[32,32,1024]{2,1,0:T(8,128)(2,1)}, u32[]{:S(2)}, u32[]{:S(2)}) %all-to-all-start.4) | async-done | bytes 2097184 | tf_op jit(solution)/shard_map/all_to_all | solution.py:474
  334.0 3.0 pair_rows.1
  (90 shorter events, 43.9 us)
Async XLA Ops:
  8.0 11.6 %copy-start.7 = (bf16[448,1024]{1,0:T(8,128)(2,1)S(1)}, bf16[448,1024]{1,0:T(8,128)(2,1)}, u32[]{:S(2)}) copy-start(bf16[448,1024]{1,0:T(8,128)(2,1)} %b_ref.1) | copy-start | bytes 2752516
  8.1 11.6 %copy-start.16 = (s32[448,1]{0,1:T(1,128)S(1)}, s32[448,1]{0,1:T(1,128)}, u32[]{:S(2)}) copy-start(s32[448,1]{0,1:T(1,128)} %param.12) | copy-start | bytes 5380
  8.1 116.8 %all-to-all-start = ((bf16[32,72,1024]{2,1,0:T(8,128)(2,1)}), bf16[32,72,1024]{2,1,0:T(8,128)(2,1)}, u32[]{:S(2)}, u32[]{:S(2)}) async-start(bf16[32,72,1024]{2,1,0:T(8,128)(2,1)} %load.1), calls=%async_computation | async-start | bytes 9437184 | tf_op jit(solution)/shard_map/all_to_all | solution.py:555
  19.7 4.1 %copy-start.13 = (bf16[256,1024]{1,0:T(8,128)(2,1)S(1)}, bf16[256,1024]{1,0:T(8,128)(2,1)}, u32[]{:S(2)}) copy-start(bf16[256,1024]{1,0:T(8,128)(2,1)} %refs_2_.3) | copy-start | bytes 1572868
  124.9 42.2 %all-to-all-start.1 = ((bf16[32,40,512]{2,1,0:T(8,128)(2,1)}), bf16[32,40,512]{2,1,0:T(8,128)(2,1)}, u32[]{:S(2)}, u32[]{:S(2)}) async-start(bf16[32,40,512]{2,1,0:T(8,128)(2,1)} %bitcast.13), calls=%async_computation.1 | async-start | bytes 2621440 | tf_op jit(solution)/shard_map/all_to_all | solution.py:474
  139.7 5.7 %copy-start.8 = (bf16[1024,1024]{1,0:T(8,128)(2,1)}, bf16[1024,1024]{1,0:T(8,128)(2,1)S(1)}, u32[]{:S(2)}) copy-start(bf16[1024,1024]{1,0:T(8,128)(2,1)S(1)} %get-tuple-element.18.a_ref) | copy-start | bytes 6291460
  146.5 3.4 %collective-permute-start = (bf16[4,128,1280]{2,1,0:T(8,128)(2,1)}, bf16[4,128,1280]{2,1,0:T(8,128)(2,1)}, u32[]{:S(2)}, u32[]{:S(2)}) collective-permute-start(bf16[4,128,1280]{2,1,0:T(8,128)(2,1)} %dynamic-slice_bitcast_fusion), channel_id=1, source_target_pairs={{0,32},{32,0},{1,33},{33,1},{2,34},{34,2},{3,35},{35,3},{4,36},{36... | collective-permute-start | bytes 3932168 | tf_op jit(solution)/shard_map/ppermute | solution.py:489
  151.8 7.5 %collective-permute-start.3 = (bf16[128,640]{1,0:T(8,128)(2,1)S(1)}, bf16[128,640]{1,0:T(8,128)(2,1)S(1)}, u32[]{:S(2)}, u32[]{:S(2)}) collective-permute-start(bf16[128,640]{1,0:T(8,128)(2,1)S(1)} %get-tuple-element.39), channel_id=1, source_target_pairs={{0,192},{64,0},{128,64},{192,128},{1,193},{65,1},{129,65},{193,129... | collective-permute-start | bytes 491528 | tf_op jit(solution)/shard_map/ppermute | solution.py:489
  152.6 6.8 %collective-permute-start.1 = (bf16[128,640]{1,0:T(8,128)(2,1)S(1)}, bf16[128,640]{1,0:T(8,128)(2,1)S(1)}, u32[]{:S(2)}, u32[]{:S(2)}) collective-permute-start(bf16[128,640]{1,0:T(8,128)(2,1)S(1)} %get-tuple-element.40), channel_id=1, source_target_pairs={{0,64},{64,128},{128,192},{192,0},{1,65},{65,129},{129,193},{193,1... | collective-permute-start | bytes 491528 | tf_op jit(solution)/shard_map/ppermute | solution.py:489
  167.1 54.5 %all-to-all-start.2 = ((bf16[32,32,1024]{2,1,0:T(8,128)(2,1)}), bf16[32,32,1024]{2,1,0:T(8,128)(2,1)S(1)}, u32[]{:S(2)}, u32[]{:S(2)}) async-start(bf16[32,32,1024]{2,1,0:T(8,128)(2,1)} %bitcast.15), calls=%async_computation.2 | async-start | bytes 4194304 | tf_op jit(solution)/shard_map/all_to_all | solution.py:474
  172.8 9.2 %collective-permute-start.4 = (bf16[128,1280]{1,0:T(8,128)(2,1)S(1)}, bf16[128,1280]{1,0:T(8,128)(2,1)S(1)}, u32[]{:S(2)}, u32[]{:S(2)}) collective-permute-start(bf16[128,1280]{1,0:T(8,128)(2,1)S(1)} %add_half.5), channel_id=1, source_target_pairs={{0,192},{64,0},{128,64},{192,128},{1,193},{65,1},{129,65},{193,129... | collective-permute-start | bytes 983048 | tf_op jit(solution)/shard_map/ppermute | solution.py:489
  173.6 8.3 %collective-permute-start.2 = (bf16[128,1280]{1,0:T(8,128)(2,1)S(1)}, bf16[128,1280]{1,0:T(8,128)(2,1)S(1)}, u32[]{:S(2)}, u32[]{:S(2)}) collective-permute-start(bf16[128,1280]{1,0:T(8,128)(2,1)S(1)} %add_half.4), channel_id=1, source_target_pairs={{0,64},{64,128},{128,192},{192,0},{1,65},{65,129},{129,193},{193,1... | collective-permute-start | bytes 983048 | tf_op jit(solution)/shard_map/ppermute | solution.py:489
  183.0 6.5 %collective-permute-start.6 = (bf16[128,640]{1,0:T(8,128)(2,1)S(1)}, bf16[128,640]{1,0:T(8,128)(2,1)S(1)}, u32[]{:S(2)}, u32[]{:S(2)}) collective-permute-start(bf16[128,640]{1,0:T(8,128)(2,1)S(1)} %get-tuple-element.20.own_ref), channel_id=1, source_target_pairs={{0,192},{64,0},{128,64},{192,128},{1,193},{65,1},{129,65},{193,129... | collective-permute-start | bytes 491528 | tf_op jit(solution)/shard_map/ppermute | solution.py:489
  183.0 6.6 %collective-permute-start.5 = (bf16[128,640]{1,0:T(8,128)(2,1)S(1)}, bf16[128,640]{1,0:T(8,128)(2,1)S(1)}, u32[]{:S(2)}, u32[]{:S(2)}) collective-permute-start(bf16[128,640]{1,0:T(8,128)(2,1)S(1)} %get-tuple-element.20.own_ref), channel_id=1, source_target_pairs={{0,64},{64,128},{128,192},{192,0},{1,65},{65,129},{129,193},{193,1... | collective-permute-start | bytes 491528 | tf_op jit(solution)/shard_map/ppermute | solution.py:489
  189.5 5.9 %collective-permute-start.8 = (bf16[128,384]{1,0:T(8,128)(2,1)S(1)}, bf16[128,384]{1,0:T(8,128)(2,1)S(1)}, u32[]{:S(2)}, u32[]{:S(2)}) collective-permute-start(bf16[128,384]{1,0:T(8,128)(2,1)S(1)} %slice.43), channel_id=1, source_target_pairs={{0,192},{64,0},{128,64},{192,128},{1,193},{65,1},{129,65},{193,129... | collective-permute-start | bytes 294920 | tf_op jit(solution)/shard_map/ppermute | solution.py:489
  189.6 5.4 %collective-permute-start.7 = (bf16[128,256]{1,0:T(8,128)(2,1)S(1)}, bf16[128,256]{1,0:T(8,128)(2,1)S(1)}, u32[]{:S(2)}, u32[]{:S(2)}) collective-permute-start(bf16[128,256]{1,0:T(8,128)(2,1)S(1)} %slice.42), channel_id=1, source_target_pairs={{0,64},{64,128},{128,192},{192,0},{1,65},{65,129},{129,193},{193,1... | collective-permute-start | bytes 196616 | tf_op jit(solution)/shard_map/ppermute | solution.py:489
  195.5 4.4 %collective-permute-start.9 = (bf16[4,128,640]{2,1,0:T(8,128)(2,1)S(1)}, bf16[4,128,640]{2,1,0:T(8,128)(2,1)S(1)}, u32[]{:S(2)}, u32[]{:S(2)}) collective-permute-start(bf16[4,128,640]{2,1,0:T(8,128)(2,1)S(1)} %column.2.own_ref), channel_id=1, source_target_pairs={{0,32},{32,0},{1,33},{33,1},{2,34},{34,2},{3,35},{35,3},{4,36},{36... | collective-permute-start | bytes 1966088 | tf_op jit(solution)/shard_map/ppermute | solution.py:489
  221.7 6.1 %copy-start.2 = (bf16[32,32,1024]{2,1,0:T(8,128)(2,1)}, bf16[32,32,1024]{2,1,0:T(8,128)(2,1)S(1)}, u32[]{:S(2)}) copy-start(bf16[32,32,1024]{2,1,0:T(8,128)(2,1)S(1)} %all-to-all-done.2) | copy-start | bytes 6291460
  221.7 53.9 %all-to-all-start.3 = ((bf16[32,32,1024]{2,1,0:T(8,128)(2,1)}), bf16[32,32,1024]{2,1,0:T(8,128)(2,1)}, u32[]{:S(2)}, u32[]{:S(2)}) async-start(bf16[32,32,1024]{2,1,0:T(8,128)(2,1)} %bitcast.58), calls=%async_computation.3 | async-start | bytes 4194304 | tf_op jit(solution)/shard_map/all_to_all | solution.py:474
  229.9 18.0 %copy-start.12 = (f32[128,1280]{1,0:T(8,128)S(1)}, f32[128,1280]{1,0:T(8,128)}, u32[]{:S(2)}) copy-start(f32[128,1280]{1,0:T(8,128)} %copy-done.11) | copy-start | bytes 1966084
  229.9 2.2 collective-permute-start.10
  232.4 8.9 %collective-permute-start.13 = (bf16[128,384]{1,0:T(8,128)(2,1)S(1)}, bf16[128,384]{1,0:T(8,128)(2,1)S(1)}, u32[]{:S(2)}, u32[]{:S(2)}) collective-permute-start(bf16[128,384]{1,0:T(8,128)(2,1)S(1)} %slice.45), channel_id=1, source_target_pairs={{0,192},{64,0},{128,64},{192,128},{1,193},{65,1},{129,65},{193,129... | collective-permute-start | bytes 294920 | tf_op jit(solution)/shard_map/ppermute | solution.py:489
  233.2 4.4 %collective-permute-start.11 = (bf16[128,256]{1,0:T(8,128)(2,1)S(1)}, bf16[128,256]{1,0:T(8,128)(2,1)S(1)}, u32[]{:S(2)}, u32[]{:S(2)}) collective-permute-start(bf16[128,256]{1,0:T(8,128)(2,1)S(1)} %slice.44), channel_id=1, source_target_pairs={{0,64},{64,128},{128,192},{192,0},{1,65},{65,129},{129,193},{193,1... | collective-permute-start | bytes 196616 | tf_op jit(solution)/shard_map/ppermute | solution.py:489
  237.6 6.5 %collective-permute-start.12 = (bf16[128,640]{1,0:T(8,128)(2,1)S(1)}, bf16[128,640]{1,0:T(8,128)(2,1)S(1)}, u32[]{:S(2)}, u32[]{:S(2)}) collective-permute-start(bf16[128,640]{1,0:T(8,128)(2,1)S(1)} %add_half.6), channel_id=1, source_target_pairs={{0,64},{64,128},{128,192},{192,0},{1,65},{65,129},{129,193},{193,1... | collective-permute-start | bytes 491528 | tf_op jit(solution)/shard_map/ppermute | solution.py:489
  241.3 6.6 %collective-permute-start.14 = (bf16[128,640]{1,0:T(8,128)(2,1)S(1)}, bf16[128,640]{1,0:T(8,128)(2,1)S(1)}, u32[]{:S(2)}, u32[]{:S(2)}) collective-permute-start(bf16[128,640]{1,0:T(8,128)(2,1)S(1)} %add_half.7), channel_id=1, source_target_pairs={{0,192},{64,0},{128,64},{192,128},{1,193},{65,1},{129,65},{193,129... | collective-permute-start | bytes 491528 | tf_op jit(solution)/shard_map/ppermute | solution.py:489
  248.1 7.8 %collective-permute-start.15 = (bf16[128,1280]{1,0:T(8,128)(2,1)S(1)}, bf16[128,1280]{1,0:T(8,128)(2,1)S(1)}, u32[]{:S(2)}, u32[]{:S(2)}) collective-permute-start(bf16[128,1280]{1,0:T(8,128)(2,1)S(1)} %backprop.1.own_ref), channel_id=1, source_target_pairs={{0,64},{64,128},{128,192},{192,0},{1,65},{65,129},{129,193},{193,1... | collective-permute-start | bytes 983048 | tf_op jit(solution)/shard_map/ppermute | solution.py:489
  248.2 9.3 %collective-permute-start.16 = (bf16[128,1280]{1,0:T(8,128)(2,1)S(1)}, bf16[128,1280]{1,0:T(8,128)(2,1)S(1)}, u32[]{:S(2)}, u32[]{:S(2)}) collective-permute-start(bf16[128,1280]{1,0:T(8,128)(2,1)S(1)} %backprop.1.own_ref), channel_id=1, source_target_pairs={{0,192},{64,0},{128,64},{192,128},{1,193},{65,1},{129,65},{193,129... | collective-permute-start | bytes 983048 | tf_op jit(solution)/shard_map/ppermute | solution.py:489
  255.9 5.4 %collective-permute-start.17 = (bf16[128,640]{1,0:T(8,128)(2,1)S(1)}, bf16[128,640]{1,0:T(8,128)(2,1)S(1)}, u32[]{:S(2)}, u32[]{:S(2)}) collective-permute-start(bf16[128,640]{1,0:T(8,128)(2,1)S(1)} %slice.46), channel_id=1, source_target_pairs={{0,64},{64,128},{128,192},{192,0},{1,65},{65,129},{129,193},{193,1... | collective-permute-start | bytes 491528 | tf_op jit(solution)/shard_map/ppermute | solution.py:489
  257.5 6.6 %collective-permute-start.18 = (bf16[128,640]{1,0:T(8,128)(2,1)S(1)}, bf16[128,640]{1,0:T(8,128)(2,1)S(1)}, u32[]{:S(2)}, u32[]{:S(2)}) collective-permute-start(bf16[128,640]{1,0:T(8,128)(2,1)S(1)} %slice.47), channel_id=1, source_target_pairs={{0,192},{64,0},{128,64},{192,128},{1,193},{65,1},{129,65},{193,129... | collective-permute-start | bytes 491528 | tf_op jit(solution)/shard_map/ppermute | solution.py:489
  264.2 3.1 collective-permute-start.19
  275.6 58.4 %all-to-all-start.4 = ((bf16[32,32,1024]{2,1,0:T(8,128)(2,1)}), bf16[32,32,1024]{2,1,0:T(8,128)(2,1)}, u32[]{:S(2)}, u32[]{:S(2)}) async-start(bf16[32,32,1024]{2,1,0:T(8,128)(2,1)} %bitcast.55), calls=%async_computation.4 | async-start | bytes 4194304 | tf_op jit(solution)/shard_map/all_to_all | solution.py:474
  283.5 4.4 %copy-start.9 = (bf16[1024,1024]{1,0:T(8,128)(2,1)S(1)}, bf16[1024,1024]{1,0:T(8,128)(2,1)}, u32[]{:S(2)}) copy-start(bf16[1024,1024]{1,0:T(8,128)(2,1)} %copy-done.8) | copy-start | bytes 6291460
  (10 other events, 20.3 us)

commit v7 on v6

--- a/solution.py
+++ b/solution.py
@@ -365,7 +365,7 @@
 def product(a, b, transposed):
     rows, depth = a.shape
     n = b.shape[0 if transposed else 1]
-    block = 512
+    block = 1024
     dims = (((1,), (1 if transposed else 0,)), ((), ()))
     return kernel_call(
         functools.partial(product_body, dims),

time: 338 us -> 338 us (level)
  no operation moved by 1% of the time
where the time goes in v7:
time: 338 us; the launch traced here: 337 us
  waiting for transfers between devices  206 us (61%)
  starting transfers between devices  65.2 us (19%)
  Pallas kernels  46 us (14%)
  matrix products  9.61 us (3%)
  local copies, waits for them, and re-layouts  8.38 us (2%)
    all_to_all x1, waiting for transfers between devices, body(): raw = lax.all_to_all(sent, EXPERT, split_axis=0, concat_axis=0, tiled=True)  98.1 us
    all_to_all x4, waiting for transfers between devices, exchange(): lax.all_to_all(rows.reshape(parts, total // parts, width), EXPERT, split_...  64 us
    ppermute x20, waiting for transfers between devices, shift(): lax.ppermute(value, axis, [(i, (i + step) % size) for i in range(size)])  44.4 us
    all_to_all x4, starting transfers between devices, exchange(): lax.all_to_all(rows.reshape(parts, total // parts, width), EXPERT, split_...  28.4 us
    ppermute x20, starting transfers between devices, shift(): lax.ppermute(value, axis, [(i, (i + step) % size) for i in range(size)])  25.2 us
    pallas_call x4, Pallas kernels, product(): kernel_call(functools.partial(product_body, dims), 'product', grid=(rows...  13.6 us
    all_to_all x1, starting transfers between devices, body(): raw = lax.all_to_all(sent, EXPERT, split_axis=0, concat_axis=0, tiled=True)  11.6 us
    pallas_call x1, Pallas kernels, load(): kernel_call(functools.partial(load_body, experts, cap, pair_cap), 'load',...  7.4 us
  transfers between devices with their start and end apart: 25, of which 19 were waited for; matrix products, arithmetic and copies ran while one was open for 3% of the time, Pallas kernels for 11%

profile of v7, /device:TPU:24, one launch (start us, length us, event | category | flops | bytes accessed | tf_op | source)
XLA Modules:
  0.0 336.9 jit_solution(2199307216375874844)
XLA Ops:
  0.6 7.4 %load.1 = bf16[32,72,1024]{2,1,0:T(8,128)(2,1)} custom-call(s32[2,256]{1,0:T(2,128)} %bitcast.63, s32[1,448]{1,0:T(1,128)} %bitcast.69, bf16[256,1024]{1,0:T(8,128)(2,1)} %refs_0_.1, bf16[448,1024]{1,0:T(8,128)(2,1)} %refs_1_.1, bf16[448,1024]{1,0:T(8,128)(2,1)} %refs_2_.2), custom_call_target="tpu_custom_call" | custom-call | tf_op jit(solution)/shard_map/load/pallas_call | solution.py:164
  8.1 11.6 %all-to-all-start = ((bf16[32,72,1024]{2,1,0:T(8,128)(2,1)}), bf16[32,72,1024]{2,1,0:T(8,128)(2,1)}, u32[]{:S(2)}, u32[]{:S(2)}) async-start(bf16[32,72,1024]{2,1,0:T(8,128)(2,1)} %load.1), calls=%async_computation | async-start | bytes 9437184 | tf_op jit(solution)/shard_map/all_to_all | solution.py:555
  19.7 4.1 %pack.1 = bf16[1280,512]{1,0:T(8,128)(2,1)} custom-call(s32[1,448]{1,0:T(1,128)S(1)} %bitcast.70, bf16[448,1024]{1,0:T(8,128)(2,1)S(1)} %copy-done.7, bf16[448,1024]{1,0:T(8,128)(2,1)S(1)} %copy-done.7), custom_call_target="tpu_custom_call" | custom-call | tf_op jit(solution)/shard_map/pack/pallas_call | solution.py:107
  23.8 3.1 dispatch.1
  26.8 98.1 %all-to-all-done.raw_ref = bf16[32,72,1024]{2,1,0:T(8,128)(2,1)} async-done(((bf16[32,72,1024]{2,1,0:T(8,128)(2,1)}), bf16[32,72,1024]{2,1,0:T(8,128)(2,1)}, u32[]{:S(2)}, u32[]{:S(2)}) %all-to-all-start) | async-done | bytes 4718624 | tf_op jit(solution)/shard_map/all_to_all | solution.py:555
  124.9 8.9 %all-to-all-start.1 = ((bf16[32,40,512]{2,1,0:T(8,128)(2,1)}), bf16[32,40,512]{2,1,0:T(8,128)(2,1)}, u32[]{:S(2)}, u32[]{:S(2)}) async-start(bf16[32,40,512]{2,1,0:T(8,128)(2,1)} %bitcast.13), calls=%async_computation.1 | async-start | bytes 2621440 | tf_op jit(solution)/shard_map/all_to_all | solution.py:474
  133.8 4.4 %unload.1 = (bf16[1024,1024]{1,0:T(8,128)(2,1)S(1)}, bf16[2,640,1024]{2,1,0:T(8,128)(2,1)S(1)}) custom-call(bf16[32,72,1024]{2,1,0:T(8,128)(2,1)} %all-to-all-done.raw_ref), custom_call_target="tpu_custom_call" | custom-call | tf_op jit(solution)/shard_map/unload/pallas_call | solution.py:197
  139.7 5.4 %product.4 = bf16[1024,1280]{1,0:T(8,128)(2,1)S(1)} custom-call(bf16[1024,1024]{1,0:T(8,128)(2,1)S(1)} %get-tuple-element.18.a_ref, bf16[1280,1024]{1,0:T(8,128)(2,1)} %bitcast.50), custom_call_target="tpu_custom_call" | custom-call | tf_op jit(solution)/shard_map/product/pallas_call | solution.py:370
  146.3 3.4 %collective-permute-done.other_ref = bf16[4,128,1280]{2,1,0:T(8,128)(2,1)} collective-permute-done((bf16[4,128,1280]{2,1,0:T(8,128)(2,1)}, bf16[4,128,1280]{2,1,0:T(8,128)(2,1)}, u32[]{:S(2)}, u32[]{:S(2)}) %collective-permute-start) | collective-permute-done | bytes 1310752 | tf_op jit(solution)/shard_map/ppermute | solution.py:489
  154.9 4.2 %collective-permute-done.3.half_ref = bf16[128,640]{1,0:T(8,128)(2,1)S(1)} collective-permute-done((bf16[128,640]{1,0:T(8,128)(2,1)S(1)}, bf16[128,640]{1,0:T(8,128)(2,1)S(1)}, u32[]{:S(2)}, u32[]{:S(2)}) %collective-permute-start.3) | collective-permute-done | bytes 163872 | tf_op jit(solution)/shard_map/ppermute | solution.py:489
  159.2 7.9 %all-to-all-done.1 = bf16[32,40,512]{2,1,0:T(8,128)(2,1)} async-done(((bf16[32,40,512]{2,1,0:T(8,128)(2,1)}), bf16[32,40,512]{2,1,0:T(8,128)(2,1)}, u32[]{:S(2)}, u32[]{:S(2)}) %all-to-all-start.1) | async-done | bytes 1310752 | tf_op jit(solution)/shard_map/all_to_all | solution.py:474
  167.1 5.7 %all-to-all-start.2 = ((bf16[32,32,1024]{2,1,0:T(8,128)(2,1)}), bf16[32,32,1024]{2,1,0:T(8,128)(2,1)S(1)}, u32[]{:S(2)}, u32[]{:S(2)}) async-start(bf16[32,32,1024]{2,1,0:T(8,128)(2,1)} %bitcast.15), calls=%async_computation.2 | async-start | bytes 4194304 | tf_op jit(solution)/shard_map/all_to_all | solution.py:474
  176.1 5.8 %collective-permute-done.4.above_ref = bf16[128,1280]{1,0:T(8,128)(2,1)S(1)} collective-permute-done((bf16[128,1280]{1,0:T(8,128)(2,1)S(1)}, bf16[128,1280]{1,0:T(8,128)(2,1)S(1)}, u32[]{:S(2)}, u32[]{:S(2)}) %collective-permute-start.4) | collective-permute-done | bytes 327712 | tf_op jit(solution)/shard_map/ppermute | solution.py:489
  183.0 3.2 collective-permute-start.5
  186.2 3.3 collective-permute-done.6.above_ref
  189.8 3.3 collective-permute-start.7
  197.0 3.0 unpack_one.1.b_ref
  204.4 17.2 %all-to-all-done.2 = bf16[32,32,1024]{2,1,0:T(8,128)(2,1)S(1)} async-done(((bf16[32,32,1024]{2,1,0:T(8,128)(2,1)}), bf16[32,32,1024]{2,1,0:T(8,128)(2,1)S(1)}, u32[]{:S(2)}, u32[]{:S(2)}) %all-to-all-start.2) | async-done | bytes 2097184 | tf_op jit(solution)/shard_map/all_to_all | solution.py:474
  221.7 6.1 %all-to-all-start.3 = ((bf16[32,32,1024]{2,1,0:T(8,128)(2,1)}), bf16[32,32,1024]{2,1,0:T(8,128)(2,1)}, u32[]{:S(2)}, u32[]{:S(2)}) async-start(bf16[32,32,1024]{2,1,0:T(8,128)(2,1)} %bitcast.58), calls=%async_computation.3 | async-start | bytes 4194304 | tf_op jit(solution)/shard_map/all_to_all | solution.py:474
  237.4 3.6 %collective-permute-start.12 = (bf16[128,640]{1,0:T(8,128)(2,1)S(1)}, bf16[128,640]{1,0:T(8,128)(2,1)S(1)}, u32[]{:S(2)}, u32[]{:S(2)}) collective-permute-start(bf16[128,640]{1,0:T(8,128)(2,1)S(1)} %add_half.6), channel_id=1, source_target_pairs={{0,64},{64,128},{128,192},{192,0},{1,65},{65,129},{129,193},{193,1... | collective-permute-start | bytes 491528 | tf_op jit(solution)/shard_map/ppermute | solution.py:489
  241.2 2.7 collective-permute-done.12.below_ref
  243.9 3.8 %collective-permute-done.14.above_ref = bf16[128,640]{1,0:T(8,128)(2,1)S(1)} collective-permute-done((bf16[128,640]{1,0:T(8,128)(2,1)S(1)}, bf16[128,640]{1,0:T(8,128)(2,1)S(1)}, u32[]{:S(2)}, u32[]{:S(2)}) %collective-permute-start.14) | collective-permute-done | bytes 163872 | tf_op jit(solution)/shard_map/ppermute | solution.py:489
  250.0 5.7 %collective-permute-done.15.below_ref = bf16[128,1280]{1,0:T(8,128)(2,1)S(1)} collective-permute-done((bf16[128,1280]{1,0:T(8,128)(2,1)S(1)}, bf16[128,1280]{1,0:T(8,128)(2,1)S(1)}, u32[]{:S(2)}, u32[]{:S(2)}) %collective-permute-start.15) | collective-permute-done | bytes 327712 | tf_op jit(solution)/shard_map/ppermute | solution.py:489
  257.9 3.2 collective-permute-done.17.low_ref
  261.1 2.8 collective-permute-done.18.high_ref
  264.3 3.0 collective-permute-done.19.other_ref
  267.5 4.6 %product.7 = bf16[1024,1024]{1,0:T(8,128)(2,1)S(1)} custom-call(bf16[1024,1280]{1,0:T(8,128)(2,1)S(1)} %bitcast.52, bf16[1280,1024]{1,0:T(8,128)(2,1)} %bitcast.51), custom_call_target="tpu_custom_call" | custom-call | tf_op jit(solution)/shard_map/product/pallas_call | solution.py:370
  275.6 7.7 %all-to-all-start.4 = ((bf16[32,32,1024]{2,1,0:T(8,128)(2,1)}), bf16[32,32,1024]{2,1,0:T(8,128)(2,1)}, u32[]{:S(2)}, u32[]{:S(2)}) async-start(bf16[32,32,1024]{2,1,0:T(8,128)(2,1)} %bitcast.55), calls=%async_computation.4 | async-start | bytes 4194304 | tf_op jit(solution)/shard_map/all_to_all | solution.py:474
  283.3 4.4 %fusion.1 = bf16[1,640,1024]{2,1,0:T(8,128)(2,1)} fusion(bf16[1024,1024]{1,0:T(8,128)(2,1)} %copy-done.8, bf16[1024,1280]{1,0:T(8,128)(2,1)S(1)} %bitcast.53), kind=kOutput, calls=%fused_computation.4 | convolution fusion | flops 1342832640 | bytes 4718592 | tf_op jit(solution)/shard_map/dot_general | solution.py:581
  292.9 4.1 %combine.1 = bf16[256,1024]{1,0:T(8,128)(2,1)} custom-call(s32[2,256]{1,0:T(2,128)S(1)} %bitcast.66, s32[2,256]{1,0:T(2,128)S(1)} %bitcast.68, bf16[1024,1024]{1,0:T(8,128)(2,1)} %bitcast.18.rows_ref), custom_call_target="tpu_custom_call" | custom-call | tf_op jit(solution)/shard_map/combine/pallas_call | solution.py:411
  297.0 36.7 %all-to-all-done.4 = bf16[32,32,1024]{2,1,0:T(8,128)(2,1)} async-done(((bf16[32,32,1024]{2,1,0:T(8,128)(2,1)}), bf16[32,32,1024]{2,1,0:T(8,128)(2,1)}, u32[]{:S(2)}, u32[]{:S(2)}) %all-to-all-start.4) | async-done | bytes 2097184 | tf_op jit(solution)/shard_map/all_to_all | solution.py:474
  333.7 3.0 pair_rows.1
  (90 shorter events, 44.3 us)
Async XLA Ops:
  8.0 11.6 %copy-start.7 = (bf16[448,1024]{1,0:T(8,128)(2,1)S(1)}, bf16[448,1024]{1,0:T(8,128)(2,1)}, u32[]{:S(2)}) copy-start(bf16[448,1024]{1,0:T(8,128)(2,1)} %b_ref.1) | copy-start | bytes 2752516
  8.1 11.6 %copy-start.16 = (s32[448,1]{0,1:T(1,128)S(1)}, s32[448,1]{0,1:T(1,128)}, u32[]{:S(2)}) copy-start(s32[448,1]{0,1:T(1,128)} %param.12) | copy-start | bytes 5380
  8.1 116.8 %all-to-all-start = ((bf16[32,72,1024]{2,1,0:T(8,128)(2,1)}), bf16[32,72,1024]{2,1,0:T(8,128)(2,1)}, u32[]{:S(2)}, u32[]{:S(2)}) async-start(bf16[32,72,1024]{2,1,0:T(8,128)(2,1)} %load.1), calls=%async_computation | async-start | bytes 9437184 | tf_op jit(solution)/shard_map/all_to_all | solution.py:555
  19.7 4.1 %copy-start.13 = (bf16[256,1024]{1,0:T(8,128)(2,1)S(1)}, bf16[256,1024]{1,0:T(8,128)(2,1)}, u32[]{:S(2)}) copy-start(bf16[256,1024]{1,0:T(8,128)(2,1)} %refs_2_.3) | copy-start | bytes 1572868
  124.9 42.2 %all-to-all-start.1 = ((bf16[32,40,512]{2,1,0:T(8,128)(2,1)}), bf16[32,40,512]{2,1,0:T(8,128)(2,1)}, u32[]{:S(2)}, u32[]{:S(2)}) async-start(bf16[32,40,512]{2,1,0:T(8,128)(2,1)} %bitcast.13), calls=%async_computation.1 | async-start | bytes 2621440 | tf_op jit(solution)/shard_map/all_to_all | solution.py:474
  139.7 5.4 %copy-start.8 = (bf16[1024,1024]{1,0:T(8,128)(2,1)}, bf16[1024,1024]{1,0:T(8,128)(2,1)S(1)}, u32[]{:S(2)}) copy-start(bf16[1024,1024]{1,0:T(8,128)(2,1)S(1)} %get-tuple-element.18.a_ref) | copy-start | bytes 6291460
  146.3 3.4 %collective-permute-start = (bf16[4,128,1280]{2,1,0:T(8,128)(2,1)}, bf16[4,128,1280]{2,1,0:T(8,128)(2,1)}, u32[]{:S(2)}, u32[]{:S(2)}) collective-permute-start(bf16[4,128,1280]{2,1,0:T(8,128)(2,1)} %dynamic-slice_bitcast_fusion), channel_id=1, source_target_pairs={{0,32},{32,0},{1,33},{33,1},{2,34},{34,2},{3,35},{35,3},{4,36},{36... | collective-permute-start | bytes 3932168 | tf_op jit(solution)/shard_map/ppermute | solution.py:489
  151.5 7.5 %collective-permute-start.3 = (bf16[128,640]{1,0:T(8,128)(2,1)S(1)}, bf16[128,640]{1,0:T(8,128)(2,1)S(1)}, u32[]{:S(2)}, u32[]{:S(2)}) collective-permute-start(bf16[128,640]{1,0:T(8,128)(2,1)S(1)} %get-tuple-element.39), channel_id=1, source_target_pairs={{0,192},{64,0},{128,64},{192,128},{1,193},{65,1},{129,65},{193,129... | collective-permute-start | bytes 491528 | tf_op jit(solution)/shard_map/ppermute | solution.py:489
  152.4 6.8 %collective-permute-start.1 = (bf16[128,640]{1,0:T(8,128)(2,1)S(1)}, bf16[128,640]{1,0:T(8,128)(2,1)S(1)}, u32[]{:S(2)}, u32[]{:S(2)}) collective-permute-start(bf16[128,640]{1,0:T(8,128)(2,1)S(1)} %get-tuple-element.40), channel_id=1, source_target_pairs={{0,64},{64,128},{128,192},{192,0},{1,65},{65,129},{129,193},{193,1... | collective-permute-start | bytes 491528 | tf_op jit(solution)/shard_map/ppermute | solution.py:489
  167.1 54.5 %all-to-all-start.2 = ((bf16[32,32,1024]{2,1,0:T(8,128)(2,1)}), bf16[32,32,1024]{2,1,0:T(8,128)(2,1)S(1)}, u32[]{:S(2)}, u32[]{:S(2)}) async-start(bf16[32,32,1024]{2,1,0:T(8,128)(2,1)} %bitcast.15), calls=%async_computation.2 | async-start | bytes 4194304 | tf_op jit(solution)/shard_map/all_to_all | solution.py:474
  172.8 9.2 %collective-permute-start.4 = (bf16[128,1280]{1,0:T(8,128)(2,1)S(1)}, bf16[128,1280]{1,0:T(8,128)(2,1)S(1)}, u32[]{:S(2)}, u32[]{:S(2)}) collective-permute-start(bf16[128,1280]{1,0:T(8,128)(2,1)S(1)} %add_half.5), channel_id=1, source_target_pairs={{0,192},{64,0},{128,64},{192,128},{1,193},{65,1},{129,65},{193,129... | collective-permute-start | bytes 983048 | tf_op jit(solution)/shard_map/ppermute | solution.py:489
  173.6 8.3 %collective-permute-start.2 = (bf16[128,1280]{1,0:T(8,128)(2,1)S(1)}, bf16[128,1280]{1,0:T(8,128)(2,1)S(1)}, u32[]{:S(2)}, u32[]{:S(2)}) collective-permute-start(bf16[128,1280]{1,0:T(8,128)(2,1)S(1)} %add_half.4), channel_id=1, source_target_pairs={{0,64},{64,128},{128,192},{192,0},{1,65},{65,129},{129,193},{193,1... | collective-permute-start | bytes 983048 | tf_op jit(solution)/shard_map/ppermute | solution.py:489
  183.0 6.5 %collective-permute-start.6 = (bf16[128,640]{1,0:T(8,128)(2,1)S(1)}, bf16[128,640]{1,0:T(8,128)(2,1)S(1)}, u32[]{:S(2)}, u32[]{:S(2)}) collective-permute-start(bf16[128,640]{1,0:T(8,128)(2,1)S(1)} %get-tuple-element.20.own_ref), channel_id=1, source_target_pairs={{0,192},{64,0},{128,64},{192,128},{1,193},{65,1},{129,65},{193,129... | collective-permute-start | bytes 491528 | tf_op jit(solution)/shard_map/ppermute | solution.py:489
  183.0 6.8 %collective-permute-start.5 = (bf16[128,640]{1,0:T(8,128)(2,1)S(1)}, bf16[128,640]{1,0:T(8,128)(2,1)S(1)}, u32[]{:S(2)}, u32[]{:S(2)}) collective-permute-start(bf16[128,640]{1,0:T(8,128)(2,1)S(1)} %get-tuple-element.20.own_ref), channel_id=1, source_target_pairs={{0,64},{64,128},{128,192},{192,0},{1,65},{65,129},{129,193},{193,1... | collective-permute-start | bytes 491528 | tf_op jit(solution)/shard_map/ppermute | solution.py:489
  189.5 6.1 %collective-permute-start.8 = (bf16[128,384]{1,0:T(8,128)(2,1)S(1)}, bf16[128,384]{1,0:T(8,128)(2,1)S(1)}, u32[]{:S(2)}, u32[]{:S(2)}) collective-permute-start(bf16[128,384]{1,0:T(8,128)(2,1)S(1)} %slice.43), channel_id=1, source_target_pairs={{0,192},{64,0},{128,64},{192,128},{1,193},{65,1},{129,65},{193,129... | collective-permute-start | bytes 294920 | tf_op jit(solution)/shard_map/ppermute | solution.py:489
  189.8 5.2 %collective-permute-start.7 = (bf16[128,256]{1,0:T(8,128)(2,1)S(1)}, bf16[128,256]{1,0:T(8,128)(2,1)S(1)}, u32[]{:S(2)}, u32[]{:S(2)}) collective-permute-start(bf16[128,256]{1,0:T(8,128)(2,1)S(1)} %slice.42), channel_id=1, source_target_pairs={{0,64},{64,128},{128,192},{192,0},{1,65},{65,129},{129,193},{193,1... | collective-permute-start | bytes 196616 | tf_op jit(solution)/shard_map/ppermute | solution.py:489
  195.7 4.4 %collective-permute-start.9 = (bf16[4,128,640]{2,1,0:T(8,128)(2,1)S(1)}, bf16[4,128,640]{2,1,0:T(8,128)(2,1)S(1)}, u32[]{:S(2)}, u32[]{:S(2)}) collective-permute-start(bf16[4,128,640]{2,1,0:T(8,128)(2,1)S(1)} %column.2.own_ref), channel_id=1, source_target_pairs={{0,32},{32,0},{1,33},{33,1},{2,34},{34,2},{3,35},{35,3},{4,36},{36... | collective-permute-start | bytes 1966088 | tf_op jit(solution)/shard_map/ppermute | solution.py:489
  221.7 6.1 %copy-start.2 = (bf16[32,32,1024]{2,1,0:T(8,128)(2,1)}, bf16[32,32,1024]{2,1,0:T(8,128)(2,1)S(1)}, u32[]{:S(2)}) copy-start(bf16[32,32,1024]{2,1,0:T(8,128)(2,1)S(1)} %all-to-all-done.2) | copy-start | bytes 6291460
  221.7 53.9 %all-to-all-start.3 = ((bf16[32,32,1024]{2,1,0:T(8,128)(2,1)}), bf16[32,32,1024]{2,1,0:T(8,128)(2,1)}, u32[]{:S(2)}, u32[]{:S(2)}) async-start(bf16[32,32,1024]{2,1,0:T(8,128)(2,1)} %bitcast.58), calls=%async_computation.3 | async-start | bytes 4194304 | tf_op jit(solution)/shard_map/all_to_all | solution.py:474
  229.7 18.0 %copy-start.12 = (f32[128,1280]{1,0:T(8,128)S(1)}, f32[128,1280]{1,0:T(8,128)}, u32[]{:S(2)}) copy-start(f32[128,1280]{1,0:T(8,128)} %copy-done.11) | copy-start | bytes 1966084
  229.7 2.2 collective-permute-start.10
  232.1 8.9 %collective-permute-start.13 = (bf16[128,384]{1,0:T(8,128)(2,1)S(1)}, bf16[128,384]{1,0:T(8,128)(2,1)S(1)}, u32[]{:S(2)}, u32[]{:S(2)}) collective-permute-start(bf16[128,384]{1,0:T(8,128)(2,1)S(1)} %slice.45), channel_id=1, source_target_pairs={{0,192},{64,0},{128,64},{192,128},{1,193},{65,1},{129,65},{193,129... | collective-permute-start | bytes 294920 | tf_op jit(solution)/shard_map/ppermute | solution.py:489
  232.9 4.4 %collective-permute-start.11 = (bf16[128,256]{1,0:T(8,128)(2,1)S(1)}, bf16[128,256]{1,0:T(8,128)(2,1)S(1)}, u32[]{:S(2)}, u32[]{:S(2)}) collective-permute-start(bf16[128,256]{1,0:T(8,128)(2,1)S(1)} %slice.44), channel_id=1, source_target_pairs={{0,64},{64,128},{128,192},{192,0},{1,65},{65,129},{129,193},{193,1... | collective-permute-start | bytes 196616 | tf_op jit(solution)/shard_map/ppermute | solution.py:489
  237.4 6.5 %collective-permute-start.12 = (bf16[128,640]{1,0:T(8,128)(2,1)S(1)}, bf16[128,640]{1,0:T(8,128)(2,1)S(1)}, u32[]{:S(2)}, u32[]{:S(2)}) collective-permute-start(bf16[128,640]{1,0:T(8,128)(2,1)S(1)} %add_half.6), channel_id=1, source_target_pairs={{0,64},{64,128},{128,192},{192,0},{1,65},{65,129},{129,193},{193,1... | collective-permute-start | bytes 491528 | tf_op jit(solution)/shard_map/ppermute | solution.py:489
  241.1 6.6 %collective-permute-start.14 = (bf16[128,640]{1,0:T(8,128)(2,1)S(1)}, bf16[128,640]{1,0:T(8,128)(2,1)S(1)}, u32[]{:S(2)}, u32[]{:S(2)}) collective-permute-start(bf16[128,640]{1,0:T(8,128)(2,1)S(1)} %add_half.7), channel_id=1, source_target_pairs={{0,192},{64,0},{128,64},{192,128},{1,193},{65,1},{129,65},{193,129... | collective-permute-start | bytes 491528 | tf_op jit(solution)/shard_map/ppermute | solution.py:489
  247.9 7.8 %collective-permute-start.15 = (bf16[128,1280]{1,0:T(8,128)(2,1)S(1)}, bf16[128,1280]{1,0:T(8,128)(2,1)S(1)}, u32[]{:S(2)}, u32[]{:S(2)}) collective-permute-start(bf16[128,1280]{1,0:T(8,128)(2,1)S(1)} %backprop.1.own_ref), channel_id=1, source_target_pairs={{0,64},{64,128},{128,192},{192,0},{1,65},{65,129},{129,193},{193,1... | collective-permute-start | bytes 983048 | tf_op jit(solution)/shard_map/ppermute | solution.py:489
  248.0 9.3 %collective-permute-start.16 = (bf16[128,1280]{1,0:T(8,128)(2,1)S(1)}, bf16[128,1280]{1,0:T(8,128)(2,1)S(1)}, u32[]{:S(2)}, u32[]{:S(2)}) collective-permute-start(bf16[128,1280]{1,0:T(8,128)(2,1)S(1)} %backprop.1.own_ref), channel_id=1, source_target_pairs={{0,192},{64,0},{128,64},{192,128},{1,193},{65,1},{129,65},{193,129... | collective-permute-start | bytes 983048 | tf_op jit(solution)/shard_map/ppermute | solution.py:489
  255.7 5.4 %collective-permute-start.17 = (bf16[128,640]{1,0:T(8,128)(2,1)S(1)}, bf16[128,640]{1,0:T(8,128)(2,1)S(1)}, u32[]{:S(2)}, u32[]{:S(2)}) collective-permute-start(bf16[128,640]{1,0:T(8,128)(2,1)S(1)} %slice.46), channel_id=1, source_target_pairs={{0,64},{64,128},{128,192},{192,0},{1,65},{65,129},{129,193},{193,1... | collective-permute-start | bytes 491528 | tf_op jit(solution)/shard_map/ppermute | solution.py:489
  257.3 6.6 %collective-permute-start.18 = (bf16[128,640]{1,0:T(8,128)(2,1)S(1)}, bf16[128,640]{1,0:T(8,128)(2,1)S(1)}, u32[]{:S(2)}, u32[]{:S(2)}) collective-permute-start(bf16[128,640]{1,0:T(8,128)(2,1)S(1)} %slice.47), channel_id=1, source_target_pairs={{0,192},{64,0},{128,64},{192,128},{1,193},{65,1},{129,65},{193,129... | collective-permute-start | bytes 491528 | tf_op jit(solution)/shard_map/ppermute | solution.py:489
  264.0 3.3 collective-permute-start.19
  275.6 58.2 %all-to-all-start.4 = ((bf16[32,32,1024]{2,1,0:T(8,128)(2,1)}), bf16[32,32,1024]{2,1,0:T(8,128)(2,1)}, u32[]{:S(2)}, u32[]{:S(2)}) async-start(bf16[32,32,1024]{2,1,0:T(8,128)(2,1)} %bitcast.55), calls=%async_computation.4 | async-start | bytes 4194304 | tf_op jit(solution)/shard_map/all_to_all | solution.py:474
  283.3 4.4 %copy-start.9 = (bf16[1024,1024]{1,0:T(8,128)(2,1)S(1)}, bf16[1024,1024]{1,0:T(8,128)(2,1)}, u32[]{:S(2)}) copy-start(bf16[1024,1024]{1,0:T(8,128)(2,1)} %copy-done.8) | copy-start | bytes 6291460
  (10 other events, 20.3 us)
